TPU v7x, 32 devices: a whole 2x2x4 slice. The times are simulated.
32 devices in a mesh: seq: 8 (over y, x, core), kv: 4 (over z).
Axes of the slice: x: 2, y: 2, z: 4, core: 2. Of those that a mesh axis runs over, the one named last changes fastest.
Arguments:
- tokens: bfloat16 [2, 4096, 1024], P(None, ('seq', 'kv')), may hold values from -6 to 6
- cotangent: bfloat16 [2, 4096, 1024], P(None, ('seq', 'kv'))
- norm_first: float32 [1024], replicated, may hold values from 0.1 to 1.9
- w_query: bfloat16 [1024, 1024], P(None, 'kv'), may hold values from -0.1875 to 0.1875
- w_key: bfloat16 [1024, 512], P(None, 'kv'), may hold values from -0.1875 to 0.1875
- w_value: bfloat16 [1024, 512], P(None, 'kv'), may hold values from -0.1875 to 0.1875
- w_out: bfloat16 [1024, 1024], P('kv'), may hold values from -3 to 3
- norm_second: float32 [1024], replicated, may hold values from 0.1 to 1.9
- w_gate: bfloat16 [4, 1024, 512], replicated, may hold values from -0.1875 to 0.1875
- w_up: bfloat16 [4, 1024, 512], replicated, may hold values from -0.1875 to 0.1875
- w_down: bfloat16 [4, 512, 1024], replicated, may hold values from -0.25 to 0.25
- routes: int32 [2, 4096, 2], P(None, ('seq', 'kv')), may hold values from 0 to 3, all different within a row; in each aligned block of 128 rows (0 to 127, 128 to 255, ..., all dimensions but the last counted through in order) at most 96 rows name the same one
- gate_weights: float32 [2, 4096, 2], P(None, ('seq', 'kv')), may hold values from 0.2 to 1
- segment_ids: int32 [2, 4096], replicated, may hold values from 0 to 3, as said below
- positions: int32 [2, 4096], P(None, 'seq'), may hold values from 0 to 3071, as said below
Outputs:
- block_out: bfloat16 [2, 4096, 1024], P(None, ('seq', 'kv'))
- d_tokens: bfloat16 [2, 4096, 1024], P(None, ('seq', 'kv'))
- grad_norm_first: float32 [1024], replicated
- grad_w_query: float32 [1024, 1024], P(None, 'kv')
- grad_w_key: float32 [1024, 512], P(None, 'kv')
- grad_w_value: float32 [1024, 512], P(None, 'kv')
- grad_w_out: float32 [1024, 1024], P('kv')
- grad_norm_second: float32 [1024], replicated
- grad_w_gate: float32 [4, 1024, 512], replicated
- grad_w_up: float32 [4, 1024, 512], replicated
- grad_w_down: float32 [4, 512, 1024], replicated
- expert_load: int32 [4], replicated
Inputs may be any that keep to these rules, and one draw needn't show every extreme that they name: `routes`: the 2 experts of a token differ. Within one row, the 128 positions that start at a multiple of 128 name each expert at most 96 times, and some such block names one expert exactly 96 times. `segment_ids`: in each row the ids start at 0, never fall and rise by one where a new document starts; each of the 4 documents has 1 to 3072 positions, and one document of each row has exactly 3072. `positions`: each position's offset from the first position of its document.
All inputs are finite; a program needn't handle non-finite values.
Results may differ from a plain program's by a relative error of at most 0.02.
Values may be sent and summed in bfloat16 or wider, within the bound.
No kernel may reach another device: no remote copies, remote signals or barrier semaphores. Data moves between devices by JAX's collectives and lax.ppermute only.
A program may use at most 192 MiB of HBM per device.

v0:
```python
import math

import jax
import jax.numpy as jnp
from jax import lax
from jax.sharding import PartitionSpec as P

DH = 64


epsilon = 1e-05
neg_big = -1e30
theta_base = 10000.0
highest = lax.Precision.HIGHEST


def shifted(value, axis, steps):
    count = lax.axis_size(axis)
    pairs = [(source, (source + steps) % count) for source in range(count)]
    return lax.ppermute(value, axis, pairs)


def rope_tables(positions, head_size):
    half_size = head_size // 2
    freqs = theta_base ** (-(jnp.arange(half_size, dtype=jnp.float32) * 2.0) / head_size)
    angles = positions.astype(jnp.float32)[..., None] * freqs
    return (jnp.cos(angles), jnp.sin(angles))


def rotate(values, cosine, sine):
    half_size = values.shape[-1] // 2
    first_half = values[..., :half_size]
    second_half = values[..., half_size:]
    cos_rows = cosine[:, :, None, :]
    sin_rows = sine[:, :, None, :]
    return jnp.concatenate(
        [
            first_half * cos_rows - second_half * sin_rows,
            second_half * cos_rows + first_half * sin_rows,
        ],
        axis=-1,
    )


def unrotate(grads, cosine, sine):
    half_size = grads.shape[-1] // 2
    first_half = grads[..., :half_size]
    second_half = grads[..., half_size:]
    cos_rows = cosine[:, :, None, :]
    sin_rows = sine[:, :, None, :]
    return jnp.concatenate(
        [
            first_half * cos_rows + second_half * sin_rows,
            second_half * cos_rows - first_half * sin_rows,
        ],
        axis=-1,
    )


def per_device(
    tokens,
    cotangent,
    norm_first,
    w_query,
    w_key,
    w_value,
    w_out,
    norm_second,
    w_gate,
    w_up,
    w_down,
    routes,
    gate_weights,
    segment_ids,
    positions,
):
    row_count = tokens.shape[0]
    block_len = tokens.shape[1]
    width = tokens.shape[2]
    kv_devices = lax.axis_size("kv")
    seq_devices = lax.axis_size("seq")
    seq_len = block_len * kv_devices
    seq_index = lax.axis_index("seq")
    head_size = DH
    query_cols = w_query.shape[1]
    key_cols = w_key.shape[1]
    query_heads = query_cols // head_size
    key_heads = key_cols // head_size
    group_size = query_heads // key_heads
    expert_count = w_gate.shape[0]
    top_count = routes.shape[2]
    capacity = 3 * block_len // 4
    slot_count = expert_count * capacity
    score_scale = head_size ** (-0.5)
    query_start = seq_index * seq_len
    query_place = query_start + jnp.arange(seq_len, dtype=jnp.int32)
    query_segs = lax.dynamic_slice_in_dim(segment_ids, query_start, seq_len, 1)
    lse_shape = (row_count, key_heads, group_size, seq_len)
    x_float = tokens.astype(jnp.float32)
    recip_first = lax.rsqrt(jnp.mean(x_float * x_float, axis=-1, keepdims=True) + epsilon)
    x_hat = x_float * recip_first
    normed = (x_hat * norm_first).astype(jnp.bfloat16)
    gathered_norm = lax.all_gather(normed, "kv", axis=1, tiled=True)
    w_inner = jnp.concatenate([w_query, w_key, w_value], axis=1)
    projected = jnp.einsum(
        "rsd,de->rse", gathered_norm, w_inner, preferred_element_type=jnp.float32
    )
    cosine, sine = rope_tables(positions, head_size)
    q_raw = projected[..., :query_cols].reshape(row_count, seq_len, query_heads, head_size)
    k_raw = projected[..., query_cols : query_cols + key_cols].reshape(
        row_count, seq_len, key_heads, head_size
    )
    queries = rotate(q_raw, cosine, sine).astype(jnp.bfloat16)
    keys_low = rotate(k_raw, cosine, sine).astype(jnp.bfloat16)
    values_low = (
        projected[..., query_cols + key_cols :]
        .reshape(row_count, seq_len, key_heads, head_size)
        .astype(jnp.bfloat16)
    )
    grouped_q = queries.reshape(row_count, seq_len, key_heads, group_size, head_size).transpose(
        0, 2, 3, 1, 4
    )
    key_pack = jnp.stack([keys_low, values_low], axis=2).reshape(row_count, seq_len, 2 * key_cols)

    def block_scores(key_block, key_start):
        span = key_block.shape[1]
        split_kv = key_block.reshape(row_count, span, 2, key_heads, head_size)
        block_keys = split_kv[:, :, 0]
        block_values = split_kv[:, :, 1]
        scores = (
            jnp.einsum(
                "rhgsd,rkhd->rhgsk", grouped_q, block_keys, preferred_element_type=jnp.float32
            )
            * score_scale
        )
        key_place = key_start + jnp.arange(span, dtype=jnp.int32)
        key_segs = lax.dynamic_slice_in_dim(segment_ids, key_start, span, 1)
        allowed = (key_place[None, None, :] <= query_place[None, :, None]) & (
            key_segs[:, None, :] == query_segs[:, :, None]
        )
        return (scores, allowed[:, None, None], block_keys, block_values)

    def forward_block(carry, key_block, key_start):
        run_max, run_total, accum = carry
        scores, allowed, block_keys, block_values = block_scores(key_block, key_start)
        masked = jnp.where(allowed, scores, neg_big)
        new_max = jnp.maximum(run_max, jnp.max(masked, axis=-1))
        weights = jnp.where(allowed, jnp.exp(masked - new_max[..., None]), 0.0)
        factor = jnp.exp(run_max - new_max)
        run_total = run_total * factor + jnp.sum(weights, axis=-1)
        accum = accum * factor[..., None] + jnp.einsum(
            "rhgsk,rkhd->rhgsd",
            weights.astype(jnp.bfloat16),
            block_values,
            preferred_element_type=jnp.float32,
        )
        return (new_max, run_total, accum)

    def forward_guarded(carry, key_block, key_start):
        return forward_block(carry, key_block, key_start)

    carry_init = (
        jnp.full(lse_shape, neg_big, jnp.float32),
        jnp.zeros(lse_shape, jnp.float32),
        jnp.zeros(lse_shape + (head_size,), jnp.float32),
    )
    piece = lax.all_gather(key_pack, "seq", axis=1, tiled=True)
    span = piece.shape[1]
    step_len = math.gcd(span, seq_len)
    piece_count = span // step_len
    stacked = piece.reshape(row_count, piece_count, step_len, piece.shape[2]).transpose(1, 0, 2, 3)

    def scan_step(state, block_input):
        return (forward_guarded(state, block_input[1], block_input[0] * step_len), None)

    run_max, run_total, accum = lax.scan(
        scan_step, carry_init, (jnp.arange(piece_count, dtype=jnp.int32), stacked)
    )[0]
    head_out = accum / run_total[..., None]
    heads_low = (
        head_out.transpose(0, 3, 1, 2, 4)
        .reshape(row_count, seq_len, query_cols)
        .astype(jnp.bfloat16)
    )
    partial_branch = jnp.einsum("rse,ed->rsd", heads_low, w_out, preferred_element_type=jnp.float32)
    branch = lax.psum_scatter(
        partial_branch.astype(jnp.bfloat16), "kv", scatter_dimension=1, tiled=True
    ).astype(jnp.float32)
    log_total = run_max + jnp.log(run_total)
    hidden_state = x_float + branch
    recip_second = lax.rsqrt(
        jnp.mean(hidden_state * hidden_state, axis=-1, keepdims=True) + epsilon
    )
    h_hat = hidden_state * recip_second
    h_norm = (h_hat * norm_second).astype(jnp.bfloat16)
    expert_ids = jnp.arange(expert_count, dtype=jnp.int32)
    choice_hot = (
        (routes[..., None] == expert_ids)
        .astype(jnp.int32)
        .reshape(row_count, block_len * top_count, expert_count)
    )
    earlier = jnp.cumsum(choice_hot, axis=1) - choice_hot
    slot_of = jnp.sum(choice_hot * (earlier + expert_ids * capacity), axis=-1)
    slot_hot = (
        (slot_of[..., None] == jnp.arange(slot_count, dtype=jnp.int32))
        .astype(jnp.float32)
        .reshape(row_count, block_len, top_count, slot_count)
    )
    dispatch = jnp.sum(slot_hot, axis=2)
    combine = jnp.sum(slot_hot * gate_weights[..., None], axis=2)
    local_load = jnp.sum(choice_hot, axis=(0, 1)).astype(jnp.float32)
    slot_rows = (
        jnp.einsum(
            "rte,rtd->red",
            dispatch.astype(jnp.bfloat16),
            h_norm,
            preferred_element_type=jnp.float32,
        )
        .astype(jnp.bfloat16)
        .reshape(row_count, expert_count, capacity, width)
    )
    gate_pre = jnp.einsum("recd,edf->recf", slot_rows, w_gate, preferred_element_type=jnp.float32)
    up_pre = jnp.einsum("recd,edf->recf", slot_rows, w_up, preferred_element_type=jnp.float32)
    gate_sig = jax.nn.sigmoid(gate_pre)
    gate_act = gate_pre * gate_sig
    hid_low = (gate_act * up_pre).astype(jnp.bfloat16)
    expert_out = jnp.einsum(
        "recf,efd->recd", hid_low, w_down, preferred_element_type=jnp.float32
    ).reshape(row_count, slot_count, width)
    branch_moe = jnp.einsum("rte,red->rtd", combine, expert_out, precision=highest)
    block_out = (hidden_state + branch_moe).astype(jnp.bfloat16)
    d_top = cotangent.astype(jnp.float32)
    d_expert = (
        jnp.einsum("rte,rtd->red", combine, d_top, precision=highest)
        .astype(jnp.bfloat16)
        .reshape(row_count, expert_count, capacity, width)
    )
    d_hid = jnp.einsum("recd,efd->recf", d_expert, w_down, preferred_element_type=jnp.float32)
    d_gate = (d_hid * up_pre * gate_sig * (1.0 + gate_pre * (1.0 - gate_sig))).astype(jnp.bfloat16)
    d_up = (d_hid * gate_act).astype(jnp.bfloat16)
    grad_down = jnp.einsum("recf,recd->efd", hid_low, d_expert, preferred_element_type=jnp.float32)
    grad_gate = jnp.einsum("recd,recf->edf", slot_rows, d_gate, preferred_element_type=jnp.float32)
    grad_up = jnp.einsum("recd,recf->edf", slot_rows, d_up, preferred_element_type=jnp.float32)
    d_slots = (
        jnp.einsum("recf,edf->recd", d_gate, w_gate, preferred_element_type=jnp.float32)
        + jnp.einsum("recf,edf->recd", d_up, w_up, preferred_element_type=jnp.float32)
    ).reshape(row_count, slot_count, width)
    d_hnorm = jnp.einsum("rte,red->rtd", dispatch, d_slots, precision=highest)
    second_part = jnp.sum(d_hnorm * h_hat, axis=(0, 1))
    d_hat_two = d_hnorm * norm_second
    d_hidden = d_top + recip_second * (
        d_hat_two - h_hat * jnp.mean(d_hat_two * h_hat, axis=-1, keepdims=True)
    )
    d_branch = d_hidden.astype(jnp.bfloat16)
    d_rows = lax.all_gather(d_branch, "kv", axis=1, tiled=True)
    grad_out_part = jnp.einsum("rse,rsd->ed", heads_low, d_rows, preferred_element_type=jnp.float32)
    d_heads = jnp.einsum("rsd,ed->rse", d_rows, w_out, preferred_element_type=jnp.float32).astype(
        jnp.bfloat16
    )
    grouped_d = d_heads.reshape(row_count, seq_len, key_heads, group_size, head_size).transpose(
        0, 2, 3, 1, 4
    )
    delta = jnp.sum(grouped_d.astype(jnp.float32) * head_out, axis=-1)

    def backward_block(d_query, key_block, grad_block, key_start):
        scores, allowed, block_keys, block_values = block_scores(key_block, key_start)
        probs = jnp.where(allowed, jnp.exp(scores - log_total[..., None]), 0.0)
        d_probs = jnp.einsum(
            "rhgsd,rkhd->rhgsk", grouped_d, block_values, preferred_element_type=jnp.float32
        )
        d_scores = (probs * (d_probs - delta[..., None])).astype(jnp.bfloat16)
        d_query = (
            d_query
            + jnp.einsum(
                "rhgsk,rkhd->rhgsd", d_scores, block_keys, preferred_element_type=jnp.float32
            )
            * score_scale
        )
        d_keys = (
            jnp.einsum("rhgsk,rhgsd->rkhd", d_scores, grouped_q, preferred_element_type=jnp.float32)
            * score_scale
        )
        d_values = jnp.einsum(
            "rhgsk,rhgsd->rkhd",
            probs.astype(jnp.bfloat16),
            grouped_d,
            preferred_element_type=jnp.float32,
        )
        grad_block = grad_block + jnp.stack([d_keys, d_values], axis=2).reshape(grad_block.shape)
        return (d_query, grad_block)

    def visit_turn(turn, state):
        key_block, grad_block, d_query = state
        anchor = (seq_index + turn) % seq_devices
        key_start = anchor * seq_len
        d_query, grad_block = backward_block(d_query, key_block, grad_block, key_start)
        key_block = shifted(key_block, "seq", -1)
        grad_block = shifted(grad_block.astype(jnp.bfloat16), "seq", -1).astype(grad_block.dtype)
        return (key_block, grad_block, d_query)

    visit_init = (
        key_pack,
        jnp.zeros((row_count, seq_len, 2 * key_cols), jnp.float32),
        jnp.zeros(lse_shape + (head_size,), jnp.float32),
    )
    visit_state = lax.fori_loop(0, seq_devices, visit_turn, visit_init)
    grad_home = visit_state[1].reshape(row_count, seq_len, 2, key_heads, head_size)
    d_query_all = (
        visit_state[2].transpose(0, 3, 1, 2, 4).reshape(row_count, seq_len, query_heads, head_size)
    )
    dq_raw = (
        unrotate(d_query_all, cosine, sine)
        .astype(jnp.bfloat16)
        .reshape(row_count, seq_len, query_cols)
    )
    dk_raw = (
        unrotate(grad_home[:, :, 0], cosine, sine)
        .astype(jnp.bfloat16)
        .reshape(row_count, seq_len, key_cols)
    )
    dv_raw = grad_home[:, :, 1].astype(jnp.bfloat16).reshape(row_count, seq_len, key_cols)
    d_inner = jnp.concatenate([dq_raw, dk_raw, dv_raw], axis=-1)
    grad_inner = jnp.einsum(
        "rsd,rse->de", gathered_norm, d_inner, preferred_element_type=jnp.float32
    )
    d_gathered = jnp.einsum("rse,de->rsd", d_inner, w_inner, preferred_element_type=jnp.float32)
    d_normed = lax.psum_scatter(
        d_gathered.astype(jnp.bfloat16), "kv", scatter_dimension=1, tiled=True
    ).astype(jnp.float32)
    first_part = jnp.sum(d_normed * x_hat, axis=(0, 1))
    d_hat_one = d_normed * norm_first
    d_tokens = (
        d_hidden
        + recip_first * (d_hat_one - x_hat * jnp.mean(d_hat_one * x_hat, axis=-1, keepdims=True))
    ).astype(jnp.bfloat16)
    attn_sums = (
        lax.psum(grad_inner.astype(jnp.bfloat16), "seq").astype(jnp.float32),
        lax.psum(grad_out_part.astype(jnp.bfloat16), "seq").astype(jnp.float32),
    )
    grad_inner_all = attn_sums[0]
    grad_gate_all, grad_up_all, grad_down_all, first_sum, second_sum, load_sum = lax.psum(
        (grad_gate, grad_up, grad_down, first_part, second_part, local_load), ("seq", "kv")
    )
    return (
        block_out,
        d_tokens,
        first_sum,
        grad_inner_all[:, :query_cols],
        grad_inner_all[:, query_cols : query_cols + key_cols],
        grad_inner_all[:, query_cols + key_cols :],
        attn_sums[1],
        second_sum,
        grad_gate_all,
        grad_up_all,
        grad_down_all,
        load_sum.astype(jnp.int32),
    )


def solution(mesh):
    in_specs = (
        P(None, ("seq", "kv"), None),
        P(None, ("seq", "kv"), None),
        P(),
        P(None, "kv"),
        P(None, "kv"),
        P(None, "kv"),
        P("kv", None),
        P(),
        P(),
        P(),
        P(),
        P(None, ("seq", "kv"), None),
        P(None, ("seq", "kv"), None),
        P(),
        P(None, "seq"),
    )
    out_specs = (
        P(None, ("seq", "kv"), None),
        P(None, ("seq", "kv"), None),
        P(),
        P(None, "kv"),
        P(None, "kv"),
        P(None, "kv"),
        P("kv", None),
        P(),
        P(),
        P(),
        P(),
        P(),
    )
    return jax.shard_map(
        per_device, mesh=mesh, in_specs=in_specs, out_specs=out_specs, check_vma=False
    )
```

profile of v0, /device:TPU:0, one launch (start us, length us, event | category | flops | bytes accessed | tf_op | source)
XLA Modules:
  0.0 1067.3 jit_solution(1170773445157117449)
XLA Ops:
  15.1 44.9 %all-gather.4.cloned.1.call-done = bf16[2,512,1024]{2,1,0:T(8,128)(2,1)} async-done(((bf16[2,128,1024]{2,1,0:T(8,128)(2,1)}), bf16[2,512,1024]{2,1,0:T(8,128)(2,1)}) %all-gather.4.cloned.1.call-update) | async-done | bytes 2097168 | tf_op jit(solution)/shard_map/all_gather | solution.py:103
  67.4 34.0 %all-gather.6.cloned.1.call-done = bf16[2,4096,256]{1,2,0:T(8,128)(2,1)} async-done(((bf16[2,512,256]{1,2,0:T(8,128)(2,1)}), bf16[2,4096,256]{1,2,0:T(8,128)(2,1)}) %all-gather.6.cloned.1.call-update) | async-done | bytes 4194320 | tf_op jit(solution)/shard_map/all_gather | solution.py:167
  101.4 4.7 copy.157
  106.1 81.0 %while.35 = (s32[]{:T(128)}, f32[2,2,2,512]{3,2,1,0:T(2,128)S(1)}, f32[2,2,2,512]{3,2,1,0:T(2,128)S(1)}, f32[2,2,2,512,64]{3,4,2,1,0:T(8,128)S(1)}, s32[8]{0:T(1...) while((s32[]{:T(128)}, f32[2,2,2,512]{3,2,1,0:T(2,128)S(1)}, ...), condition=%wide.region_4.5_spmd.clone, body=%wide.region_1.4_spmd.clone.sunk | while | flops 566252544 | bytes 32268512 | solution.py:176
  198.1 36.8 %reduce-scatter.3.cloned.1.call-done = bf16[2,128,1024]{2,1,0:T(8,128)(2,1)} async-done(((bf16[2,512,1024]{2,1,0:T(8,128)(2,1)}), bf16[2,128,1024]{2,1,0:T(8,128)(2,1)}) %reduce-scatter.3.cloned.1.call-update) | async-done | bytes 524304 | tf_op jit(solution)/shard_map/reduce_scatter | solution.py:186
  256.4 45.1 %all-gather.8.cloned.1.call-done = bf16[2,512,1024]{2,1,0:T(8,128)(2,1)} async-done(((bf16[2,128,1024]{2,1,0:T(8,128)(2,1)}), bf16[2,512,1024]{2,1,0:T(8,128)(2,1)}) %all-gather.8.cloned.1.call-update) | async-done | bytes 2097168 | tf_op jit(solution)/shard_map/all_gather | solution.py:255
  305.0 219.6 %while.36 = (s32[]{:T(128)}, bf16[2,512,256]{1,2,0:T(8,128)(2,1)S(1)}, f32[2,512,256]{1,2,0:T(8,128)}, f32[2,2,2,512,64]{3,4,2,1,0:T(8,128)}, s32[]{:T(128)}, /*...) while((s32[]{:T(128)}, ...), condition=%wide.region_15.16_spmd.clone, body=%wide.region_14.15_spmd.clone.sunk | while | flops 1366688768 | bytes 82649600 | solution.py:306
  310.0 3.6 multiply_convert_fusion.4
  319.8 4.5 fusion.159
  336.5 3.6 multiply_convert_fusion.4
  346.6 4.8 fusion.159
  364.1 3.6 multiply_convert_fusion.4
  374.2 4.8 fusion.159
  391.6 3.6 multiply_convert_fusion.4
  401.8 4.8 fusion.159
  419.2 3.6 multiply_convert_fusion.4
  429.4 4.8 fusion.159
  446.8 3.6 multiply_convert_fusion.4
  456.9 4.8 fusion.159
  474.3 3.6 multiply_convert_fusion.4
  484.5 4.8 fusion.159
  501.9 3.6 multiply_convert_fusion.4
  512.1 4.8 fusion.159
  541.6 6.0 convolution_bitcast_fusion.3
  547.5 4.8 convolution_bitcast_fusion.2
  552.3 4.7 convolution_bitcast_fusion.1
  565.7 30.7 %all-reduce.8.cloned.1.call-done = (bf16[1024,512]{1,0:T(8,128)(2,1)}, bf16[256,1024]{1,0:T(8,128)(2,1)}) async-done(((bf16[1024,512]{1,0:T(8,128)(2,1)}, bf16[256,1024]{1,0:T(8,128)(2,1)}), (bf16[1024,512]{1,0:T(8,128)(2,1)}, bf16[256,1024]{1,0:T(8,128)(2,1)})) %all-reduce.8.cloned.1.call-update) | async-done | bytes 1572880 | tf_op jit(solution)/shard_map/psum | solution.py:337
  601.7 40.0 %reduce-scatter.5.cloned.1.call-done = bf16[2,128,1024]{2,1,0:T(8,128)(2,1)} async-done(((bf16[2,512,1024]{2,1,0:T(8,128)(2,1)}), bf16[2,128,1024]{2,1,0:T(8,128)(2,1)}) %reduce-scatter.5.cloned.1.call-update) | async-done | bytes 524304 | tf_op jit(solution)/shard_map/reduce_scatter | solution.py:327
  643.2 41.4 %all-reduce = (f32[1024]{0:T(1024)}, f32[1024]{0:T(1024)}, f32[4]{0:T(128)S(1)}) all-reduce(f32[1024]{0:T(1024)S(1)} %get-tuple-element.439, f32[1024]{0:T(1024)S(1)} %copy-done.55, f32[4]{0:T(128)S(1)} %convert_element_type.212), channel_id=1, replica_groups=mesh['seq'=8,'kv'=4] {'seq','kv'}, use_global_device_ids=true, to_apply=%region_19.20 | all-reduce | flops 2052 | bytes 16416 | tf_op jit(solution)/shard_map/psum | solution.py:341
  687.7 354.5 %all-reduce.6.cloned.1.call-done = (f32[4,1024,512]{2,1,0:T(8,128)}, f32[4,1024,512]{2,1,0:T(8,128)}, f32[4,512,1024]{2,1,0:T(8,128)}) async-done(((f32[4,1024,512]{2,1,0:T(8,128)}, f32[4,1024,512]{2,1,0:T(8,128)}, f32[4,512,1024]{2,1,0:T(8,128)}), (f32[4,1024,512]{2,1,0:T(8,128)}, f32[4,1024,512]{2,1,0:T(8,128)}, f32[4,512,1024]{2,1,0:T(8,128)})) %all-reduce.6.cloned.1.call-update) | async-done | bytes 25165840 | tf_op jit(solution)/shard_map/psum | solution.py:341
  1042.2 8.8 copy.189
  1051.0 4.3 copy.190
  (499 shorter events, 317.7 us)
Async XLA Ops:
  7.2 181.6 %copy-start = (bf16[256,1024]{1,0:T(8,128)(2,1)S(1)}, bf16[256,1024]{1,0:T(8,128)(2,1)}, u32[]{:S(2)}) copy-start(bf16[256,1024]{1,0:T(8,128)(2,1)} %param.25) | copy-start | bytes 1572868
  7.2 52.8 %all-gather.4.cloned.1.call-start = ((), (), s32[]{:S(2)}) async-start(), calls=%async_computation.2 | async-start | bytes 2621440 | tf_op jit(solution)/shard_map/all_gather | solution.py:103
  11.2 90.2 %all-gather.6.cloned.1.call-start = ((), (), s32[]{:S(2)}) async-start(), calls=%async_computation.3 | async-start | bytes 4718592 | tf_op jit(solution)/shard_map/all_gather | solution.py:167
  65.1 169.8 %reduce-scatter.3.cloned.1.call-start = ((), (), s32[]{:S(2)}) async-start(), calls=%async_computation.4 | async-start | bytes 2621440 | tf_op jit(solution)/shard_map/reduce_scatter | solution.py:186
  190.9 110.6 %all-gather.8.cloned.1.call-start = ((), (), s32[]{:S(2)}) async-start(), calls=%async_computation.5 | async-start | bytes 2621440 | tf_op jit(solution)/shard_map/all_gather | solution.py:255
  256.1 340.2 %all-reduce.8.cloned.1.call-start = ((), (), s32[]{:S(2)}) async-start(), calls=%async_computation.8 | async-start | bytes 3145728 | tf_op jit(solution)/shard_map/psum | solution.py:337
  305.0 222.5 %copy-start.28 = (f32[2,512,32]{1,2,0:T(8,128)S(1)}, f32[2,512,32]{1,2,0:T(8,128)}, u32[]{:S(2)}) copy-start(f32[2,512,32]{1,2,0:T(8,128)} %copy-done.27) | copy-start | bytes 393220
  305.0 222.5 %copy-start.30 = (f32[2,512,32]{1,2,0:T(8,128)S(1)}, f32[2,512,32]{1,2,0:T(8,128)}, u32[]{:S(2)}) copy-start(f32[2,512,32]{1,2,0:T(8,128)} %copy-done.29) | copy-start | bytes 393220
  317.3 8.8 collective-permute-start.1
  319.0 12.5 %collective-permute-start = (bf16[2,512,256]{1,2,0:T(8,128)(2,1)S(1)}, bf16[2,512,256]{1,2,0:T(8,128)(2,1)S(1)}, u32[]{:S(2)}, u32[]{:S(2)}) collective-permute-start(bf16[2,512,256]{1,2,0:T(8,128)(2,1)S(1)} %copy.177), channel_id=1, source_target_pairs={{0,28},{4,0},{8,4},{12,8},{16,12},{20,16},{24,20},{28,24},{1,29},{... | collective-permute-start | bytes 1572872 | tf_op jit(solution)/shard_map/while/body/eval_jaxpr/ppermute | solution.py:20
  343.8 9.8 collective-permute-start.1
  346.6 12.5 %collective-permute-start = (bf16[2,512,256]{1,2,0:T(8,128)(2,1)S(1)}, bf16[2,512,256]{1,2,0:T(8,128)(2,1)S(1)}, u32[]{:S(2)}, u32[]{:S(2)}) collective-permute-start(bf16[2,512,256]{1,2,0:T(8,128)(2,1)S(1)} %copy.177), channel_id=1, source_target_pairs={{0,28},{4,0},{8,4},{12,8},{16,12},{20,16},{24,20},{28,24},{1,29},{... | collective-permute-start | bytes 1572872 | tf_op jit(solution)/shard_map/while/body/eval_jaxpr/ppermute | solution.py:20
  371.4 9.8 collective-permute-start.1
  374.2 12.5 %collective-permute-start = (bf16[2,512,256]{1,2,0:T(8,128)(2,1)S(1)}, bf16[2,512,256]{1,2,0:T(8,128)(2,1)S(1)}, u32[]{:S(2)}, u32[]{:S(2)}) collective-permute-start(bf16[2,512,256]{1,2,0:T(8,128)(2,1)S(1)} %copy.177), channel_id=1, source_target_pairs={{0,28},{4,0},{8,4},{12,8},{16,12},{20,16},{24,20},{28,24},{1,29},{... | collective-permute-start | bytes 1572872 | tf_op jit(solution)/shard_map/while/body/eval_jaxpr/ppermute | solution.py:20
  398.9 9.8 collective-permute-start.1
  401.8 12.5 %collective-permute-start = (bf16[2,512,256]{1,2,0:T(8,128)(2,1)S(1)}, bf16[2,512,256]{1,2,0:T(8,128)(2,1)S(1)}, u32[]{:S(2)}, u32[]{:S(2)}) collective-permute-start(bf16[2,512,256]{1,2,0:T(8,128)(2,1)S(1)} %copy.177), channel_id=1, source_target_pairs={{0,28},{4,0},{8,4},{12,8},{16,12},{20,16},{24,20},{28,24},{1,29},{... | collective-permute-start | bytes 1572872 | tf_op jit(solution)/shard_map/while/body/eval_jaxpr/ppermute | solution.py:20
  426.5 9.8 collective-permute-start.1
  429.3 12.5 %collective-permute-start = (bf16[2,512,256]{1,2,0:T(8,128)(2,1)S(1)}, bf16[2,512,256]{1,2,0:T(8,128)(2,1)S(1)}, u32[]{:S(2)}, u32[]{:S(2)}) collective-permute-start(bf16[2,512,256]{1,2,0:T(8,128)(2,1)S(1)} %copy.177), channel_id=1, source_target_pairs={{0,28},{4,0},{8,4},{12,8},{16,12},{20,16},{24,20},{28,24},{1,29},{... | collective-permute-start | bytes 1572872 | tf_op jit(solution)/shard_map/while/body/eval_jaxpr/ppermute | solution.py:20
  454.1 9.8 collective-permute-start.1
  456.9 12.5 %collective-permute-start = (bf16[2,512,256]{1,2,0:T(8,128)(2,1)S(1)}, bf16[2,512,256]{1,2,0:T(8,128)(2,1)S(1)}, u32[]{:S(2)}, u32[]{:S(2)}) collective-permute-start(bf16[2,512,256]{1,2,0:T(8,128)(2,1)S(1)} %copy.177), channel_id=1, source_target_pairs={{0,28},{4,0},{8,4},{12,8},{16,12},{20,16},{24,20},{28,24},{1,29},{... | collective-permute-start | bytes 1572872 | tf_op jit(solution)/shard_map/while/body/eval_jaxpr/ppermute | solution.py:20
  481.7 9.8 collective-permute-start.1
  484.5 12.5 %collective-permute-start = (bf16[2,512,256]{1,2,0:T(8,128)(2,1)S(1)}, bf16[2,512,256]{1,2,0:T(8,128)(2,1)S(1)}, u32[]{:S(2)}, u32[]{:S(2)}) collective-permute-start(bf16[2,512,256]{1,2,0:T(8,128)(2,1)S(1)} %copy.177), channel_id=1, source_target_pairs={{0,28},{4,0},{8,4},{12,8},{16,12},{20,16},{24,20},{28,24},{1,29},{... | collective-permute-start | bytes 1572872 | tf_op jit(solution)/shard_map/while/body/eval_jaxpr/ppermute | solution.py:20
  509.2 9.8 collective-permute-start.1
  512.0 12.5 %collective-permute-start = (bf16[2,512,256]{1,2,0:T(8,128)(2,1)S(1)}, bf16[2,512,256]{1,2,0:T(8,128)(2,1)S(1)}, u32[]{:S(2)}, u32[]{:S(2)}) collective-permute-start(bf16[2,512,256]{1,2,0:T(8,128)(2,1)S(1)} %copy.177), channel_id=1, source_target_pairs={{0,28},{4,0},{8,4},{12,8},{16,12},{20,16},{24,20},{28,24},{1,29},{... | collective-permute-start | bytes 1572872 | tf_op jit(solution)/shard_map/while/body/eval_jaxpr/ppermute | solution.py:20
  537.6 104.1 %reduce-scatter.5.cloned.1.call-start = ((), (), s32[]{:S(2)}) async-start(), calls=%async_computation.6 | async-start | bytes 2621440 | tf_op jit(solution)/shard_map/reduce_scatter | solution.py:327
  541.3 500.9 %all-reduce.6.cloned.1.call-start = ((), (), s32[]{:S(2)}) async-start(), calls=%async_computation.7 | async-start | bytes 50331648 | tf_op jit(solution)/shard_map/psum | solution.py:341
  565.7 76.1 %copy-start.52 = (f32[1024]{0:T(1024)S(1)}, f32[1024]{0:T(1024)}, u32[]{:S(2)}) copy-start(f32[1024]{0:T(1024)} %param.21) | copy-start | bytes 12292
  565.7 76.1 %copy-start.57 = (f32[2,128]{1,0:T(2,128)S(1)}, f32[2,128]{1,0:T(2,128)}, u32[]{:S(2)}) copy-start(f32[2,128]{1,0:T(2,128)} %copy-done.56) | copy-start | bytes 3076
  596.3 88.8 %copy-start.12 = (f32[2,128,1024]{2,1,0:T(8,128)S(1)}, f32[2,128,1024]{2,1,0:T(8,128)}, u32[]{:S(2)}) copy-start(f32[2,128,1024]{2,1,0:T(8,128)} %copy-done.11) | copy-start | bytes 3145732
  596.3 88.8 %copy-start.21 = (bf16[2,128,1024]{2,1,0:T(8,128)(2,1)S(1)}, bf16[2,128,1024]{2,1,0:T(8,128)(2,1)}, u32[]{:S(2)}) copy-start(bf16[2,128,1024]{2,1,0:T(8,128)(2,1)} %param.20) | copy-start | bytes 1572868
  596.3 88.8 %copy-start.51 = (f32[1024]{0:T(1024)S(1)}, f32[1024]{0:T(1024)}, u32[]{:S(2)}) copy-start(f32[1024]{0:T(1024)} %param.26) | copy-start | bytes 12292
  596.3 88.8 %copy-start.54 = (f32[2,128]{1,0:T(2,128)S(1)}, f32[2,128]{1,0:T(2,128)}, u32[]{:S(2)}) copy-start(f32[2,128]{1,0:T(2,128)} %copy-done.53) | copy-start | bytes 3076
  (76 other events, 680.7 us)
Sparse Core Ops, SparseCore 0:
  11.3 48.6 all-gather.3
  65.2 36.1 all-gather.5
  191.0 43.8 reduce-scatter.2
  256.2 45.2 all-gather.7
  537.8 58.5 all-reduce.7
  598.5 43.1 reduce-scatter.4
  649.8 392.2 all-reduce.5
where the time goes:
time: 1080 us; the launch traced here: 1070 us
  waiting for transfers between devices  630 us (58%)
  matrix products  191 us (18%)
  local copies, waits for them, and re-layouts  85.5 us (8%)
  other arithmetic  74.1 us (7%)
  blocking collectives  41.4 us (4%)
  starting transfers between devices  23.3 us (2%)
  between operations  15.3 us (1%)
    psum x1, waiting for transfers between devices, per_device(): lax.psum((grad_gate, grad_up, grad_down, first_part, second_part, local_l...  354 us
    all_gather x1, waiting for transfers between devices, per_device(): d_rows = lax.all_gather(d_branch, 'kv', axis=1, tiled=True)  45.1 us
    all_gather x1, waiting for transfers between devices, per_device(): gathered_norm = lax.all_gather(normed, 'kv', axis=1, tiled=True)  44.9 us
    ppermute x16, waiting for transfers between devices, shifted(): return lax.ppermute(value, axis, pairs)  43.7 us
    psum x1, blocking collectives, per_device(): lax.psum((grad_gate, grad_up, grad_down, first_part, second_part, local_l...  41.4 us
    reduce_scatter x1, waiting for transfers between devices, per_device(): lax.psum_scatter(d_gathered.astype(jnp.bfloat16), 'kv', scatter_dimension...  40 us
    dot_general x8, matrix products, backward_block(): jnp.einsum('rhgsk,rkhd->rhgsd', d_scores, block_keys, preferred_element_t...  38.4 us
    reduce_scatter x1, waiting for transfers between devices, per_device(): lax.psum_scatter(partial_branch.astype(jnp.bfloat16), 'kv', scatter_dimen...  36.8 us
  transfers between devices with their start and end apart: 23, of which 23 were waited for; matrix products, arithmetic and copies ran while one was open for 10% of the time, Pallas kernels for 0%

commit v1 on v0

v1 whole, which is shorter than its diff:
```python
import functools

import jax
import jax.numpy as jnp
from jax import lax
from jax.experimental import pallas as pl
from jax.experimental.pallas import tpu as pltpu
from jax.sharding import PartitionSpec as P

DH = 64
HALF = DH // 2

epsilon = 1e-05
neg_big = -1e30
theta_base = 10000.0
highest = lax.Precision.HIGHEST
f32 = jnp.float32
bf16 = jnp.bfloat16

NN = (((1,), (0,)), ((), ()))
NT = (((1,), (1,)), ((), ()))


def mm(a, b, dims=NN):
    return lax.dot_general(a, b, dims, preferred_element_type=f32)


def qkv_kernel(w_ref, n_ref, cos_ref, sin_ref, q_ref, kv_ref, *, query_heads, key_heads, scale):
    acc = mm(w_ref[...], n_ref[...], NT)
    cosine = cos_ref[...]
    sine = sin_ref[...]
    for head in range(query_heads):
        low = acc[DH * head : DH * head + HALF]
        high = acc[DH * head + HALF : DH * head + DH]
        q_ref[DH * head : DH * head + HALF, :] = ((low * cosine - high * sine) * scale).astype(bf16)
        q_ref[DH * head + HALF : DH * head + DH, :] = (
            (high * cosine + low * sine) * scale
        ).astype(bf16)
    base = DH * query_heads
    for head in range(key_heads):
        low = acc[base + DH * head : base + DH * head + HALF]
        high = acc[base + DH * head + HALF : base + DH * head + DH]
        at = 2 * DH * head
        kv_ref[at : at + HALF, :] = (low * cosine - high * sine).astype(bf16)
        kv_ref[at + HALF : at + DH, :] = (high * cosine + low * sine).astype(bf16)
        start = base + DH * (key_heads + head)
        kv_ref[at + DH : at + 2 * DH, :] = acc[start : start + DH].astype(bf16)


def project(w_t, gathered, cosine, sine, query_heads, key_heads):
    cols, width = w_t.shape
    count = gathered.shape[0]
    tile = 256
    q_cols = query_heads * DH
    kv_cols = 2 * key_heads * DH
    return pl.pallas_call(
        functools.partial(
            qkv_kernel, query_heads=query_heads, key_heads=key_heads, scale=DH ** (-0.5)
        ),
        grid=(count // tile,),
        in_specs=[
            pl.BlockSpec((cols, width), lambda i: (0, 0)),
            pl.BlockSpec((tile, width), lambda i: (i, 0)),
            pl.BlockSpec((HALF, tile), lambda i: (0, i)),
            pl.BlockSpec((HALF, tile), lambda i: (0, i)),
        ],
        out_specs=[
            pl.BlockSpec((q_cols, tile), lambda i: (0, i)),
            pl.BlockSpec((kv_cols, tile), lambda i: (0, i)),
        ],
        out_shape=[
            jax.ShapeDtypeStruct((q_cols, count), bf16),
            jax.ShapeDtypeStruct((kv_cols, count), bf16),
        ],
        compiler_params=pltpu.CompilerParams(vmem_limit_bytes=32 * 2**20),
        cost_estimate=pl.CostEstimate(
            flops=2 * cols * width * count, bytes_accessed=4 * count * width, transcendentals=0
        ),
    )(w_t, gathered, cosine, sine)


def forward_kernel(
    meta_ref, q_ref, kv_ref, start_ref, o_ref, low_ref, lse_ref, max_s, sum_s, acc_s,
    *, group, row_count
):
    row = pl.program_id(0)
    span = q_ref.shape[1]
    here = meta_ref[0]
    first = meta_ref[1 + row]
    middle = meta_ref[1 + row_count + row]
    start = start_ref[0]
    key_iota = lax.broadcasted_iota(jnp.int32, (span, span), 0)

    def step(block, masked, diagonal):
        k_t = kv_ref[block, 0:DH, :]
        v_t = kv_ref[block, DH : 2 * DH, :]
        keys = k_t.T
        if masked:
            keep = key_iota + block * span >= start
        if diagonal:
            keep = keep & (key_iota <= lax.broadcasted_iota(jnp.int32, (span, span), 1))
        for g in range(group):
            scores = mm(keys, q_ref[DH * g : DH * g + DH, :])
            if masked:
                scores = jnp.where(keep, scores, neg_big)
            top = jnp.max(scores, axis=0, keepdims=True)
            if diagonal:
                new_max = top
            else:
                old_max = max_s[g : g + 1, :]
                new_max = jnp.maximum(old_max, top)
            weights = jnp.exp(scores - new_max)
            total = jnp.sum(weights, axis=0, keepdims=True)
            mixed = mm(v_t, weights.astype(bf16))
            at = slice(DH * g, DH * g + DH)
            if diagonal:
                sum_s[g : g + 1, :] = total
                acc_s[at, :] = mixed
            else:
                factor = jnp.exp(old_max - new_max)
                sum_s[g : g + 1, :] = sum_s[g : g + 1, :] * factor + total
                acc_s[at, :] = acc_s[at, :] * factor + mixed
            max_s[g : g + 1, :] = new_max

    step(here, True, True)

    @pl.loop(first, middle)
    def _(block):
        step(block, True, False)

    @pl.loop(middle, here)
    def _(block):
        step(block, False, False)

    for g in range(group):
        at = slice(DH * g, DH * g + DH)
        total = sum_s[g : g + 1, :]
        out = acc_s[at, :] / total
        o_ref[at, :] = out
        low_ref[at, :] = out.astype(bf16)
        lse_ref[0, 0, g : g + 1, :] = max_s[g : g + 1, :] + jnp.log(total)


def attend(meta, q_t, kv_all, starts, group):
    row_count, _, span = starts.shape
    blocks = kv_all.shape[0]
    key_heads = kv_all.shape[1] // (2 * DH)
    cols = group * DH
    count = q_t.shape[1]
    return pl.pallas_call(
        functools.partial(forward_kernel, group=group, row_count=row_count),
        grid_spec=pltpu.PrefetchScalarGridSpec(
            num_scalar_prefetch=1,
            grid=(row_count, key_heads),
            in_specs=[
                pl.BlockSpec((cols, span), lambda r, h, m: (h, r)),
                pl.BlockSpec((blocks, 2 * DH, span), lambda r, h, m: (0, h, r)),
                pl.BlockSpec((1, 1, span), lambda r, h, m: (r, 0, 0)),
            ],
            out_specs=[
                pl.BlockSpec((cols, span), lambda r, h, m: (h, r)),
                pl.BlockSpec((cols, span), lambda r, h, m: (h, r)),
                pl.BlockSpec((1, 1, group, span), lambda r, h, m: (h, r, 0, 0)),
            ],
            scratch_shapes=[
                pltpu.VMEM((group, span), f32),
                pltpu.VMEM((group, span), f32),
                pltpu.VMEM((cols, span), f32),
            ],
        ),
        out_shape=[
            jax.ShapeDtypeStruct((key_heads * cols, count), f32),
            jax.ShapeDtypeStruct((key_heads * cols, count), bf16),
            jax.ShapeDtypeStruct((key_heads, row_count, group, span), f32),
        ],
        compiler_params=pltpu.CompilerParams(vmem_limit_bytes=48 * 2**20),
        cost_estimate=pl.CostEstimate(
            flops=16 * count * blocks * span * cols,
            bytes_accessed=4 * kv_all.size,
            transcendentals=0,
        ),
    )(meta, q_t, kv_all, starts)


def backward_kernel(
    meta_ref, q_ref, do_ref, o_ref, lse_ref, kv_ref, start_ref, cos_ref, sin_ref,
    dq_ref, dkv_ref, dq_s, q_s, do_s, delta_s,
    *, group, row_count, scale
):
    row = pl.program_id(0)
    span = q_ref.shape[1]
    here = meta_ref[0]
    first = meta_ref[1 + row]
    middle = meta_ref[1 + row_count + row]
    start = start_ref[0]
    key_iota = lax.broadcasted_iota(jnp.int32, (span, span), 0)
    dkv_ref[...] = jnp.zeros(dkv_ref.shape, bf16)
    for g in range(group):
        at = slice(DH * g, DH * g + DH)
        q_s[g] = q_ref[at, :].T
        do_s[g] = do_ref[at, :].T
        delta_s[g : g + 1, :] = jnp.sum(
            do_ref[at, :].astype(f32) * o_ref[at, :], axis=0, keepdims=True
        )

    def step(block, masked, diagonal):
        k_t = kv_ref[block, 0:DH, :]
        v_t = kv_ref[block, DH : 2 * DH, :]
        keys = k_t.T
        values = v_t.T
        if masked:
            keep = key_iota + block * span >= start
        if diagonal:
            keep = keep & (key_iota <= lax.broadcasted_iota(jnp.int32, (span, span), 1))
        d_keys = None
        d_values = None
        for g in range(group):
            at = slice(DH * g, DH * g + DH)
            scores = mm(keys, q_ref[at, :])
            probs = jnp.exp(scores - lse_ref[0, 0, g : g + 1, :])
            if masked:
                probs = jnp.where(keep, probs, 0.0)
            d_probs = mm(values, do_ref[at, :])
            d_scores = (probs * (d_probs - delta_s[g : g + 1, :])).astype(bf16)
            dq = mm(k_t, d_scores)
            if diagonal:
                dq_s[at, :] = dq
            else:
                dq_s[at, :] += dq
            dv = mm(probs.astype(bf16), do_s[g])
            dk = mm(d_scores, q_s[g])
            d_keys = dk if d_keys is None else d_keys + dk
            d_values = dv if d_values is None else d_values + dv
        dkv_ref[block, 0:DH, :] = d_keys.T.astype(bf16)
        dkv_ref[block, DH : 2 * DH, :] = d_values.T.astype(bf16)

    step(here, True, True)

    @pl.loop(first, middle)
    def _(block):
        step(block, True, False)

    @pl.loop(middle, here)
    def _(block):
        step(block, False, False)

    cosine = cos_ref[...]
    sine = sin_ref[...]
    for g in range(group):
        low = dq_s[DH * g : DH * g + HALF, :] * scale
        high = dq_s[DH * g + HALF : DH * g + DH, :] * scale
        dq_ref[DH * g : DH * g + HALF, :] = (low * cosine + high * sine).astype(bf16)
        dq_ref[DH * g + HALF : DH * g + DH, :] = (high * cosine - low * sine).astype(bf16)


def attend_back(meta, q_t, do_t, o_t, lse, kv_all, starts, cosine, sine, group):
    row_count, _, span = starts.shape
    blocks = kv_all.shape[0]
    key_heads = kv_all.shape[1] // (2 * DH)
    cols = group * DH
    count = q_t.shape[1]
    head_spec = pl.BlockSpec((cols, span), lambda r, h, m: (h, r))
    kv_spec = pl.BlockSpec((blocks, 2 * DH, span), lambda r, h, m: (0, h, r))
    angle_spec = pl.BlockSpec((HALF, span), lambda r, h, m: (0, r))
    return pl.pallas_call(
        functools.partial(
            backward_kernel, group=group, row_count=row_count, scale=DH ** (-0.5)
        ),
        grid_spec=pltpu.PrefetchScalarGridSpec(
            num_scalar_prefetch=1,
            grid=(row_count, key_heads),
            in_specs=[
                head_spec,
                head_spec,
                head_spec,
                pl.BlockSpec((1, 1, group, span), lambda r, h, m: (h, r, 0, 0)),
                kv_spec,
                pl.BlockSpec((1, 1, span), lambda r, h, m: (r, 0, 0)),
                angle_spec,
                angle_spec,
            ],
            out_specs=[head_spec, kv_spec],
            scratch_shapes=[
                pltpu.VMEM((cols, span), f32),
                pltpu.VMEM((group, span, DH), bf16),
                pltpu.VMEM((group, span, DH), bf16),
                pltpu.VMEM((group, span), f32),
            ],
        ),
        out_shape=[
            jax.ShapeDtypeStruct((key_heads * cols, count), bf16),
            jax.ShapeDtypeStruct(kv_all.shape, bf16),
        ],
        compiler_params=pltpu.CompilerParams(vmem_limit_bytes=48 * 2**20),
        cost_estimate=pl.CostEstimate(
            flops=40 * count * blocks * span * cols,
            bytes_accessed=4 * kv_all.size,
            transcendentals=0,
        ),
    )(meta, q_t, do_t, o_t, lse, kv_all, starts, cosine, sine)


def per_device(
    tokens,
    cotangent,
    norm_first,
    w_query,
    w_key,
    w_value,
    w_out,
    norm_second,
    w_gate,
    w_up,
    w_down,
    routes,
    gate_weights,
    segment_ids,
    positions,
):
    row_count, block_len, width = tokens.shape
    kv_devices = lax.axis_size("kv")
    seq_devices = lax.axis_size("seq")
    seq_len = block_len * kv_devices
    seq_index = lax.axis_index("seq")
    query_cols = w_query.shape[1]
    key_cols = w_key.shape[1]
    inner_cols = query_cols + 2 * key_cols
    query_heads = query_cols // DH
    key_heads = key_cols // DH
    group = query_heads // key_heads
    expert_count = w_gate.shape[0]
    top_count = routes.shape[2]
    own = row_count * block_len
    count = row_count * seq_len

    place = seq_index * seq_len + jnp.arange(seq_len, dtype=jnp.int32)
    starts = place[None, :] - positions
    first_block = starts[:, 0] // seq_len
    middle_block = jnp.clip((starts[:, -1] + seq_len - 1) // seq_len, first_block, seq_index)
    meta = jnp.concatenate([seq_index[None], first_block, middle_block]).astype(jnp.int32)
    freqs = theta_base ** (-(jnp.arange(HALF, dtype=f32) * 2.0) / DH)
    angles = freqs[:, None] * positions.astype(f32).reshape(1, count)
    cosine = jnp.cos(angles)
    sine = jnp.sin(angles)

    w_t = jnp.concatenate([w_query.T, w_key.T, w_value.T], axis=0)
    all_rows = jnp.concatenate([w_t, w_out], axis=0)
    share = all_rows.shape[0] // seq_devices
    expert_ids = jnp.arange(expert_count, dtype=jnp.int32)
    picks = routes[..., None] == expert_ids
    local_load = jnp.sum(picks.astype(f32), axis=(0, 1, 2))
    load_rows = jnp.pad(local_load.astype(bf16)[None, :], ((0, 15), (0, width - expert_count)))
    payload = jnp.concatenate(
        [lax.dynamic_slice_in_dim(all_rows, seq_index * share, share, 0), load_rows], axis=0
    )

    x_float = tokens.astype(f32)
    recip_first = lax.rsqrt(jnp.mean(x_float * x_float, axis=-1, keepdims=True) + epsilon)
    x_hat = x_float * recip_first
    normed = (x_hat * norm_first).astype(bf16)
    gathered = lax.all_gather(normed, "kv", axis=1, tiled=True).reshape(count, width)
    q_t, kv_t = project(w_t, gathered, cosine, sine, query_heads, key_heads)
    kv_all = lax.all_gather(kv_t, "seq")

    spread = lax.all_gather(payload, ("seq", "kv")).reshape(
        seq_devices, kv_devices, share + 16, width
    )
    load_sum = jnp.sum(spread[:, :, share, :expert_count].astype(f32), axis=(0, 1))
    w_all = spread[:, :, :share].transpose(1, 0, 2, 3).reshape(kv_devices, seq_devices * share, width)
    w_inner_all = w_all[:, :inner_cols]
    w_out_all = w_all[:, inner_cols:].reshape(kv_devices * query_cols, width)

    starts3 = starts.reshape(row_count, 1, seq_len)
    o_t, heads_t, lse = attend(meta, q_t, kv_all, starts3, group)

    def exchange(value):
        return lax.all_to_all(value, "kv", 0, 0)

    def split_own(value):
        cols = value.shape[0]
        return (
            value.reshape(cols, row_count, kv_devices, block_len)
            .transpose(2, 0, 1, 3)
            .reshape(kv_devices, cols, own)
        )

    heads_own = exchange(split_own(heads_t)).reshape(kv_devices * query_cols, own)
    branch = lax.dot_general(
        heads_own, w_out_all, (((0,), (0,)), ((), ())), preferred_element_type=f32
    )
    hidden_state = x_float + branch.reshape(row_count, block_len, width)
    recip_second = lax.rsqrt(
        jnp.mean(hidden_state * hidden_state, axis=-1, keepdims=True) + epsilon
    )
    h_hat = hidden_state * recip_second
    h_norm = (h_hat * norm_second).astype(bf16)

    mix = jnp.sum(picks.astype(f32) * gate_weights[..., None], axis=2).reshape(own, expert_count)
    h_rows = h_norm.reshape(own, width)
    gate_pre = jnp.einsum("td,edf->etf", h_rows, w_gate, preferred_element_type=f32)
    up_pre = jnp.einsum("td,edf->etf", h_rows, w_up, preferred_element_type=f32)
    gate_sig = jax.nn.sigmoid(gate_pre)
    gate_act = gate_pre * gate_sig
    hid_low = (gate_act * up_pre).astype(bf16)
    expert_out = jnp.einsum("etf,efd->etd", hid_low, w_down, preferred_element_type=f32)
    mix_e = mix.T[:, :, None]
    branch_moe = jnp.sum(mix_e * expert_out, axis=0)
    block_out = (hidden_state + branch_moe.reshape(row_count, block_len, width)).astype(bf16)
    d_top = cotangent.astype(f32)
    d_expert = (mix_e * d_top.reshape(1, own, width)).astype(bf16)
    d_hid = jnp.einsum("etd,efd->etf", d_expert, w_down, preferred_element_type=f32)
    d_gate = (d_hid * up_pre * gate_sig * (1.0 + gate_pre * (1.0 - gate_sig))).astype(bf16)
    d_up = (d_hid * gate_act).astype(bf16)
    grad_down = jnp.einsum("etf,etd->efd", hid_low, d_expert, preferred_element_type=f32)
    grad_gate = jnp.einsum("td,etf->edf", h_rows, d_gate, preferred_element_type=f32)
    grad_up = jnp.einsum("td,etf->edf", h_rows, d_up, preferred_element_type=f32)
    d_hnorm = (
        jnp.einsum("etf,edf->td", d_gate, w_gate, preferred_element_type=f32)
        + jnp.einsum("etf,edf->td", d_up, w_up, preferred_element_type=f32)
    ).reshape(row_count, block_len, width)
    d_hat_two = d_hnorm * norm_second
    d_hidden = d_top + recip_second * (
        d_hat_two - h_hat * jnp.mean(d_hat_two * h_hat, axis=-1, keepdims=True)
    )
    d_branch = d_hidden.astype(bf16)

    grad_gate_low, grad_up_low, grad_down_low = lax.psum(
        (grad_gate.astype(bf16), grad_up.astype(bf16), grad_down.astype(bf16)), ("seq", "kv")
    )

    d_heads = mm(w_out_all, d_branch.reshape(own, width), NT).astype(bf16)
    d_heads = exchange(d_heads.reshape(kv_devices, query_cols, own))
    do_t = (
        d_heads.reshape(kv_devices, query_cols, row_count, block_len)
        .transpose(1, 2, 0, 3)
        .reshape(query_cols, count)
    )
    d_rows = lax.all_gather(d_branch, "kv", axis=1, tiled=True).reshape(count, width)
    grad_out_part = mm(heads_t, d_rows)
    grad_out_all = lax.psum(grad_out_part.astype(bf16), "seq").astype(f32)

    dq_t, dkv_part = attend_back(
        meta, q_t, do_t, o_t, lse, kv_all, starts3, cosine, sine, group
    )
    dkv = lax.psum_scatter(dkv_part, "seq").astype(f32)
    dkv = dkv.reshape(key_heads, 2, DH, count)
    low, high = dkv[:, 0, :HALF], dkv[:, 0, HALF:]
    dk_t = jnp.concatenate([low * cosine + high * sine, high * cosine - low * sine], axis=1)
    d_inner_t = jnp.concatenate(
        [
            dq_t,
            dk_t.astype(bf16).reshape(key_cols, count),
            dkv[:, 1].astype(bf16).reshape(key_cols, count),
        ],
        axis=0,
    )
    grad_inner_part = lax.dot_general(
        gathered, d_inner_t, (((0,), (1,)), ((), ())), preferred_element_type=f32
    )
    grad_inner = lax.psum(grad_inner_part.astype(bf16), "seq").astype(f32)
    d_inner_own = exchange(split_own(d_inner_t)).reshape(kv_devices * inner_cols, own)
    d_normed = lax.dot_general(
        d_inner_own,
        w_inner_all.reshape(kv_devices * inner_cols, width),
        (((0,), (0,)), ((), ())),
        preferred_element_type=f32,
    ).reshape(row_count, block_len, width)
    d_hat_one = d_normed * norm_first
    d_tokens = (
        d_hidden
        + recip_first * (d_hat_one - x_hat * jnp.mean(d_hat_one * x_hat, axis=-1, keepdims=True))
    ).astype(bf16)

    first_part = jnp.sum(w_t.T.astype(f32) * grad_inner, axis=1)
    first_sum = lax.psum(first_part, "kv") / norm_first
    grad_gate_all = grad_gate_low.astype(f32)
    grad_up_all = grad_up_low.astype(f32)
    grad_down_all = grad_down_low.astype(f32)
    second_sum = (
        jnp.sum(w_gate.astype(f32) * grad_gate_all + w_up.astype(f32) * grad_up_all, axis=(0, 2))
        / norm_second
    )
    return (
        block_out,
        d_tokens,
        first_sum,
        grad_inner[:, :query_cols],
        grad_inner[:, query_cols : query_cols + key_cols],
        grad_inner[:, query_cols + key_cols :],
        grad_out_all,
        second_sum,
        grad_gate_all,
        grad_up_all,
        grad_down_all,
        load_sum.astype(jnp.int32),
    )


def solution(mesh):
    in_specs = (
        P(None, ("seq", "kv"), None),
        P(None, ("seq", "kv"), None),
        P(),
        P(None, "kv"),
        P(None, "kv"),
        P(None, "kv"),
        P("kv", None),
        P(),
        P(),
        P(),
        P(),
        P(None, ("seq", "kv"), None),
        P(None, ("seq", "kv"), None),
        P(),
        P(None, "seq"),
    )
    out_specs = (
        P(None, ("seq", "kv"), None),
        P(None, ("seq", "kv"), None),
        P(),
        P(None, "kv"),
        P(None, "kv"),
        P(None, "kv"),
        P("kv", None),
        P(),
        P(),
        P(),
        P(),
        P(),
    )
    return jax.shard_map(
        per_device, mesh=mesh, in_specs=in_specs, out_specs=out_specs, check_vma=False
    )
```

time: 1080 us -> 670 us (0.62); the launches traced: 1070 us -> 669 us
  waiting for transfers between devices: 630 us -> 443 us
  matrix products: 191 us -> 35 us
  other arithmetic: 74.1 us -> 34.3 us
  Pallas kernels: 0 us -> 19.8 us
  local copies, waits for them, and re-layouts: 85.5 us -> 67.6 us
  starting transfers between devices: 23.3 us -> 9.65 us
    dot_general x75 -> x14, matrix products: 191 us -> 35 us  [the longest x2 5.51 us: mm(): return lax.dot_general(a, b, dims, preferred_element_type=f32)]
    psum x2, waiting for transfers between devices: 385 us -> 263 us  [the longest x1 209 us: per_device(): lax.psum((grad_gate.astype(bf16), grad_up.astype(bf16), grad_down.astype(...]
    ppermute x16 -> x0, waiting for transfers between devices: 43.7 us -> none  [shifted(): return lax.ppermute(value, axis, pairs)]
    reduce_scatter x2 -> x1, waiting for transfers between devices: 76.8 us -> 33.5 us  [per_device(): dkv = lax.psum_scatter(dkv_part, 'seq').astype(f32)]
    all_to_all x0 -> x1, blocking collectives: none -> 32.4 us  [exchange(): return lax.all_to_all(value, 'kv', 0, 0)]
    psum x1, blocking collectives: 41.4 us -> 11.8 us  [per_device(): first_sum = lax.psum(first_part, 'kv') / norm_first]
    dynamic_slice x33 -> x0, local copies, waits for them, and re-layouts: 25.1 us -> none  [the longest x16 13.3 us: per_device(): lax.scan(scan_step, carry_init, (jnp.arange(piece_count, dtype=jnp.int32)...]
    ppermute x16 -> x0, starting transfers between devices: 22.3 us -> none  [shifted(): return lax.ppermute(value, axis, pairs)]
  transfers between devices with their start and end apart: 23 -> 9, of which waited for: 23 -> 7; matrix products, arithmetic and copies ran while one was open for 10% -> 14% of each run, Pallas kernels for 0% -> 3%
where the time goes in v1:
time: 670 us; the launch traced here: 669 us
  waiting for transfers between devices  443 us (66%)
  local copies, waits for them, and re-layouts  67.6 us (10%)
  blocking collectives  44.2 us (7%)
  matrix products  35 us (5%)
  other arithmetic  34.3 us (5%)
  Pallas kernels  19.8 us (3%)
  between operations  14.8 us (2%)
  starting transfers between devices  9.65 us (1%)
    psum x1, waiting for transfers between devices, per_device(): lax.psum((grad_gate.astype(bf16), grad_up.astype(bf16), grad_down.astype(...  209 us
    psum x1, waiting for transfers between devices, per_device(): grad_inner = lax.psum(grad_inner_part.astype(bf16), 'seq').astype(f32)  53.8 us
    all_gather x1, waiting for transfers between devices, per_device(): lax.all_gather(payload, ('seq', 'kv'))  51.5 us
    unnamed x86, local copies, waits for them, and re-layouts  43.8 us
    all_gather x1, waiting for transfers between devices, per_device(): lax.all_gather(normed, 'kv', axis=1, tiled=True).reshape(count, width)  43.6 us
    all_gather x1, waiting for transfers between devices, per_device(): kv_all = lax.all_gather(kv_t, 'seq')  34 us
    reduce_scatter x1, waiting for transfers between devices, per_device(): dkv = lax.psum_scatter(dkv_part, 'seq').astype(f32)  33.5 us
    all_to_all x1, blocking collectives, exchange(): return lax.all_to_all(value, 'kv', 0, 0)  32.4 us
  transfers between devices with their start and end apart: 9, of which 7 were waited for; matrix products, arithmetic and copies ran while one was open for 14% of the time, Pallas kernels for 3%

profile of v1, /device:TPU:0, one launch (start us, length us, event | category | flops | bytes accessed | tf_op | source)
XLA Modules:
  0.0 668.8 jit_solution(2369050217038849677)
XLA Ops:
  15.7 43.6 %all-gather.7.cloned.1.call-done = bf16[2,512,1024]{2,1,0:T(8,128)(2,1)} async-done(((bf16[2,128,1024]{2,1,0:T(8,128)(2,1)}), bf16[2,512,1024]{2,1,0:T(8,128)(2,1)}) %all-gather.7.cloned.1.call-update) | async-done | bytes 2097168 | tf_op jit(solution)/shard_map/all_gather | solution.py:361
  60.9 2.8 shard_map.229
  65.3 34.0 %all-gather.11.cloned.1.call-done = bf16[2048,1024]{1,0:T(8,128)(2,1)} async-done(((bf16[256,1024]{1,0:T(8,128)(2,1)}), bf16[2048,1024]{1,0:T(8,128)(2,1)}) %all-gather.11.cloned.1.call-update) | async-done | bytes 4194320 | tf_op jit(solution)/shard_map/all_gather | solution.py:363
  99.3 6.3 shard_map.230
  107.2 4.6 all-to-all-start
  112.9 17.7 %all-to-all-done = bf16[4,256,256]{1,2,0:T(8,128)(2,1)S(1)} async-done(((bf16[4,256,256]{1,2,0:T(8,128)(2,1)}), bf16[4,256,256]{1,2,0:T(8,128)(2,1)S(1)}, u32[]{:S(2)}, u32[]{:S(2)}) %all-to-all-start) | async-done | bytes 524320 | tf_op jit(solution)/shard_map/all_to_all | solution.py:377
  132.8 51.5 %all-gather.13.cloned.1.call-done = bf16[3584,1024]{1,0:T(8,128)(2,1)} async-done(((bf16[112,1024]{1,0:T(8,128)(2,1)}), bf16[3584,1024]{1,0:T(8,128)(2,1)}) %all-gather.13.cloned.1.call-update) | async-done | bytes 7340048 | tf_op jit(solution)/shard_map/all_gather | solution.py:365
  184.3 3.5 slice.50
  192.4 2.3 copy-done.16
  198.5 3.1 fusion.7
  206.4 4.6 convert_bitcast_fusion.1
  211.1 3.3 convert_bitcast_fusion
  214.4 3.4 fusion.2
  218.8 2.3 convolution_convert_fusion.2
  221.3 32.4 %all_to_all.15 = bf16[4,256,256]{1,2,0:T(8,128)(2,1)S(1)} all-to-all(bf16[4,256,256]{1,2,0:T(8,128)(2,1)S(1)} %copy.102), channel_id=1, replica_groups=mesh['seq'=8,'kv'=4] {'kv'}, dimensions={0} | all-to-all | bytes 1048576 | tf_op jit(solution)/shard_map/all_to_all | solution.py:377
  254.4 10.7 %shard_map.231 = (bf16[256,1024]{1,0:T(8,128)(2,1)S(1)}, bf16[8,256,1024]{2,1,0:T(8,128)(2,1)}) custom-call(s32[5]{0:T(128)S(1)} %pad_add_fusion.meta_ref, bf16[256,1024]{1,0:T(8,128)(2,1)S(1)} %get-tuple-element.19.q_ref, bf16[256,1024]{1,0:T(8,128)(2,1)S(1)} %reshape.237.do_ref, f32[256,1024]{1,0:T(8,128)S(1)} %get-tuple-element.22.o_ref, ...), custom_call_target="tpu_custom_call" | custom-call | flops 21474836480 | bytes 8388608 | tf_op jit(solution)/shard_map/pallas_call | solution.py:265
  265.1 6.3 copy.113
  271.5 6.4 copy.115
  277.8 4.9 slice.55
  284.2 2.3 multiply_reduce_fusion
  287.2 3.2 convolution_convert_fusion.1
  290.4 209.3 %all-reduce.6.cloned.1.call-done = (bf16[4,1024,512]{1,2,0:T(8,128)(2,1)}, bf16[4,1024,512]{1,2,0:T(8,128)(2,1)}, bf16[4,512,1024]{2,1,0:T(8,128)(2,1)}) async-done(((bf16[4,1024,512]{1,2,0:T(8,128)(2,1)}, bf16[4,1024,512]{1,2,0:T(8,128)(2,1)}, bf16[4,512,1024]{2,1,0:T(8,128)(2,1)}), (bf16[4,1024,512]{1,2,0:T(8,128)(2,1)}, bf16[4,1024,512]{1,2,0:T(8,128)(2,1)}, ...) | async-done | bytes 12582928 | tf_op jit(solution)/shard_map/psum | solution.py:427
  499.7 6.6 convert_element_type.181
  506.3 7.0 %copy.121 = f32[4,1024,512]{2,1,0:T(8,128)} copy(bf16[4,1024,512]{1,2,0:T(8,128)(2,1)} %get-tuple-element.78) | data formatting | bytes 12582912
  513.3 7.1 %copy.122 = f32[4,1024,512]{2,1,0:T(8,128)} copy(bf16[4,1024,512]{1,2,0:T(8,128)(2,1)} %get-tuple-element.79) | data formatting | bytes 12582912
  520.5 33.5 %reduce-scatter.2.cloned.1.call-done = bf16[1,256,1024]{2,1,0:T(8,128)(2,1)} async-done(((bf16[8,256,1024]{2,1,0:T(8,128)(2,1)}), bf16[1,256,1024]{2,1,0:T(8,128)(2,1)}) %reduce-scatter.2.cloned.1.call-update) | async-done | bytes 524304 | tf_op jit(solution)/shard_map/reduce_scatter | solution.py:445
  564.4 4.6 all-to-all-start.2
  569.0 3.2 convolution_convert_fusion
  572.3 7.0 %add_reduce_fusion = f32[1024]{0:T(1024)S(1)} fusion(bf16[4,1024,512]{1,2,0:T(8,128)(2,1)} %copy.115, bf16[4,1024,512]{1,2,0:T(8,128)(2,1)} %copy.113, bf16[4,1024,512]{1,2,0:T(8,128)(2,1)} %get-tuple-element.79, bf16[4,1024,512]{1,2,0:T(8,128)(2,1)} %get-tuple-element.78), kind=kLoop, calls=%fused_computation | loop fusion | flops 16776192 | bytes 16781312 | tf_op jit(solution)/shard_map/reduce_sum | solution.py:480
  579.9 53.8 %all-reduce.8.cloned.1.call-done = (bf16[1024,512]{0,1:T(8,128)(2,1)}, bf16[256,1024]{1,0:T(8,128)(2,1)}) async-done(((bf16[1024,512]{0,1:T(8,128)(2,1)}, bf16[256,1024]{1,0:T(8,128)(2,1)}), (bf16[1024,512]{0,1:T(8,128)(2,1)}, bf16[256,1024]{1,0:T(8,128)(2,1)})) %all-reduce.8.cloned.1.call-update) | async-done | bytes 1572880 | tf_op jit(solution)/shard_map/psum | solution.py:460
  636.5 11.8 %psum.43 = f32[1024]{0:T(1024)S(1)} all-reduce(f32[1024]{0:T(1024)S(1)} %fusion.3), channel_id=1, replica_groups=mesh['seq'=8,'kv'=4] {'kv'}, use_global_device_ids=true, to_apply=%region_10.11 | all-reduce | flops 1024 | bytes 8192 | tf_op jit(solution)/shard_map/psum | solution.py:475
  656.7 3.7 fusion.21
  (154 shorter events, 57.0 us)
Async XLA Ops:
  7.2 52.1 %all-gather.7.cloned.1.call-start = ((), (), s32[]{:S(2)}) async-start(), calls=%async_computation.4 | async-start | bytes 2621440 | tf_op jit(solution)/shard_map/all_gather | solution.py:361
  10.5 88.8 %all-gather.11.cloned.1.call-start = ((), (), s32[]{:S(2)}) async-start(), calls=%async_computation.7 | async-start | bytes 4718592 | tf_op jit(solution)/shard_map/all_gather | solution.py:363
  12.4 51.5 %copy-start.19 = (bf16[1024,128]{0,1:T(8,128)(2,1)}, bf16[1024,128]{0,1:T(8,128)(2,1)S(1)}, u32[]{:S(2)}) copy-start(bf16[1024,128]{0,1:T(8,128)(2,1)S(1)} %copy.96) | copy-start | bytes 786436
  12.5 51.3 %copy-start.33 = (f32[2,128,2]{1,2,0:T(2,128)S(1)}, f32[2,128,2]{1,2,0:T(2,128)}, u32[]{:S(2)}) copy-start(f32[2,128,2]{1,2,0:T(2,128)} %param.27) | copy-start | bytes 6148
  12.5 51.3 %copy-start.34 = (s32[2,128,2]{1,2,0:T(2,128)S(1)}, s32[2,128,2]{1,2,0:T(2,128)}, u32[]{:S(2)}) copy-start(s32[2,128,2]{1,2,0:T(2,128)} %param.26) | copy-start | bytes 6148
  12.5 51.4 %copy-start.30 = (bf16[256,1024]{1,0:T(8,128)(2,1)S(1)}, bf16[256,1024]{1,0:T(8,128)(2,1)}, u32[]{:S(2)}) copy-start(bf16[256,1024]{1,0:T(8,128)(2,1)} %param.21) | copy-start | bytes 1572868
  13.7 50.6 %copy-start.21 = (bf16[1024,128]{0,1:T(8,128)(2,1)}, bf16[1024,128]{0,1:T(8,128)(2,1)S(1)}, u32[]{:S(2)}) copy-start(bf16[1024,128]{0,1:T(8,128)(2,1)S(1)} %copy.97) | copy-start | bytes 786436
  15.0 49.2 %copy-start.11 = (bf16[1024,256]{0,1:T(8,128)(2,1)}, bf16[1024,256]{0,1:T(8,128)(2,1)S(1)}, u32[]{:S(2)}) copy-start(bf16[1024,256]{0,1:T(8,128)(2,1)S(1)} %copy.95) | copy-start | bytes 1572868
  63.7 120.6 %all-gather.13.cloned.1.call-start = ((), (), s32[]{:S(2)}) async-start(), calls=%async_computation.8 | async-start | bytes 7569408 | tf_op jit(solution)/shard_map/all_gather | solution.py:365
  99.3 12.4 %copy-start.13 = (bf16[2,128,1024]{2,1,0:T(8,128)(2,1)S(1)}, bf16[2,128,1024]{2,1,0:T(8,128)(2,1)}, u32[]{:S(2)}) copy-start(bf16[2,128,1024]{2,1,0:T(8,128)(2,1)} %param.16) | copy-start | bytes 1572868
  107.2 23.4 %all-to-all-start = ((bf16[4,256,256]{1,2,0:T(8,128)(2,1)}), bf16[4,256,256]{1,2,0:T(8,128)(2,1)S(1)}, u32[]{:S(2)}, u32[]{:S(2)}) async-start(bf16[4,256,256]{1,2,0:T(8,128)(2,1)} %bitcast.184), calls=%async_computation | async-start | bytes 1048576 | tf_op jit(solution)/shard_map/all_to_all | solution.py:377
  111.7 175.5 %all-gather.9.cloned.1.call-start = ((), (), s32[]{:S(2)}) async-start(), calls=%async_computation.6 | async-start | bytes 2621440 | tf_op jit(solution)/shard_map/all_gather | solution.py:438
  189.0 5.7 copy-start.16
  189.2 6.7 %copy-start.10 = (bf16[4,256,1024]{2,1,0:T(8,128)(2,1)}, bf16[4,256,1024]{2,1,0:T(8,128)(2,1)S(1)}, u32[]{:S(2)}) copy-start(bf16[4,256,1024]{2,1,0:T(8,128)(2,1)S(1)} %slice.51) | copy-start | bytes 6291460
  192.2 12.3 %copy-start.2 = (f32[2,128,1024]{2,1,0:T(8,128)}, f32[2,128,1024]{2,1,0:T(8,128)S(1)}, u32[]{:S(2)}) copy-start(f32[2,128,1024]{2,1,0:T(8,128)S(1)} %get-tuple-element.99) | copy-start | bytes 3145732
  206.4 293.3 %all-reduce.6.cloned.1.call-start = ((), (), s32[]{:S(2)}) async-start(), calls=%async_computation.9 | async-start | bytes 25165824 | tf_op jit(solution)/shard_map/psum | solution.py:427
  206.4 4.6 copy-start.28
  217.8 336.2 %reduce-scatter.2.cloned.1.call-start = ((), (), s32[]{:S(2)}) async-start(), calls=%async_computation.5 | async-start | bytes 4718592 | tf_op jit(solution)/shard_map/reduce_scatter | solution.py:445
  277.8 6.3 copy-start.26
  277.8 6.3 copy-start.36
  555.2 13.8 %copy-start.1 = (bf16[2,512,1024]{2,1,0:T(8,128)(2,1)S(1)}, bf16[2,512,1024]{2,1,0:T(8,128)(2,1)}, u32[]{:S(2)}) copy-start(bf16[2,512,1024]{2,1,0:T(8,128)(2,1)} %all-gather.7.cloned.1.call-done) | copy-start | bytes 6291460
  564.4 90.1 %all-to-all-start.2 = ((bf16[4,512,256]{1,2,0:T(8,128)(2,1)}), bf16[4,512,256]{1,2,0:T(8,128)(2,1)}, u32[]{:S(2)}, u32[]{:S(2)}) async-start(bf16[4,512,256]{1,2,0:T(8,128)(2,1)} %bitcast.175), calls=%async_computation.3 | async-start | bytes 2097152 | tf_op jit(solution)/shard_map/all_to_all | solution.py:377
  569.0 64.7 %all-reduce.8.cloned.1.call-start = ((), (), s32[]{:S(2)}) async-start(), calls=%async_computation.10 | async-start | bytes 3145728 | tf_op jit(solution)/shard_map/psum | solution.py:460
  572.2 62.7 %copy-start.12 = (bf16[1024,256]{0,1:T(8,128)(2,1)S(1)}, bf16[1024,256]{0,1:T(8,128)(2,1)}, u32[]{:S(2)}) copy-start(bf16[1024,256]{0,1:T(8,128)(2,1)} %copy-done.11) | copy-start | bytes 1572868
  572.2 62.7 %copy-start.20 = (bf16[1024,128]{0,1:T(8,128)(2,1)S(1)}, bf16[1024,128]{0,1:T(8,128)(2,1)}, u32[]{:S(2)}) copy-start(bf16[1024,128]{0,1:T(8,128)(2,1)} %copy-done.19) | copy-start | bytes 786436
  572.3 62.7 %copy-start.22 = (bf16[1024,128]{0,1:T(8,128)(2,1)S(1)}, bf16[1024,128]{0,1:T(8,128)(2,1)}, u32[]{:S(2)}) copy-start(bf16[1024,128]{0,1:T(8,128)(2,1)} %copy-done.21) | copy-start | bytes 786436
  579.3 69.0 %copy-start.32 = (f32[1024]{0:T(1024)S(1)}, f32[1024]{0:T(1024)}, u32[]{:S(2)}) copy-start(f32[1024]{0:T(1024)} %param.17) | copy-start | bytes 12292
  633.7 18.7 %copy-start.5 = (bf16[1024,512]{0,1:T(8,128)(2,1)S(1)}, bf16[1024,512]{0,1:T(8,128)(2,1)}, u32[]{:S(2)}) copy-start(bf16[1024,512]{0,1:T(8,128)(2,1)} %get-tuple-element.81) | copy-start | bytes 3145732
  652.4 4.3 copy-start.9
  656.6 3.8 copy-start.3
  656.6 3.8 copy-start.7
  656.7 3.8 copy-start.14
  (14 other events, 34.5 us)
Sparse Core Ops, SparseCore 0:
  10.6 48.6 all-gather.6
  63.8 35.4 all-gather.10
  102.7 81.5 all-gather.12
  206.5 55.5 all-gather.8
  268.9 230.6 all-reduce.5
  502.9 51.0 reduce-scatter.1
  574.1 59.5 all-reduce.7

commit v2 on v1

v2 whole, which is shorter than its diff:
```python
import functools

import jax
import jax.numpy as jnp
from jax import lax
from jax.experimental import pallas as pl
from jax.experimental.pallas import tpu as pltpu
from jax.sharding import PartitionSpec as P

DH = 64
HALF = DH // 2

epsilon = 1e-05
neg_big = -1e30
theta_base = 10000.0
highest = lax.Precision.HIGHEST
f32 = jnp.float32
bf16 = jnp.bfloat16

NN = (((1,), (0,)), ((), ()))
NT = (((1,), (1,)), ((), ()))


def mm(a, b, dims=NN):
    return lax.dot_general(a, b, dims, preferred_element_type=f32)


def seq_bits(axis_size):
    bits = []
    bit = 2
    while bit < axis_size:
        bits.append(bit)
        bit *= 2
    return bits


def seq_order(row, axis_size):
    bits = seq_bits(axis_size)
    return (bits if row % 2 == 0 else bits[::-1]) + [1]


def slot_of(mask, order):
    slot = 0
    for at, bit in enumerate(order):
        slot = slot + (((mask >> (bit.bit_length() - 1)) & 1) << at)
    return slot


def swap(value, axis, mask):
    count = lax.axis_size(axis)
    return lax.ppermute(value, axis, [(source, source ^ mask) for source in range(count)])


def spread_seq(value, order):
    held = value[None]
    for bit in order:
        held = jnp.concatenate([held, swap(held, "seq", bit)], axis=0)
    return held


def collect_seq(value, order):
    held = value
    for bit in order[::-1]:
        half = held.shape[0] // 2
        came = swap(held[half:], "seq", bit)
        held = (held[:half].astype(f32) + came.astype(f32)).astype(bf16)
    return held[0]


def sum_seq(value, order):
    index = lax.axis_index("seq")
    held = value
    for bit in order[::-1]:
        half = held.shape[0] // 2
        upper = (index & bit) != 0
        keep = jnp.where(upper, held[half:], held[:half])
        send = jnp.where(upper, held[:half], held[half:])
        held = (keep.astype(f32) + swap(send, "seq", bit).astype(f32)).astype(bf16)
    for bit in order:
        upper = (index & bit) != 0
        came = swap(held, "seq", bit)
        held = jnp.where(
            upper,
            jnp.concatenate([came, held], axis=0),
            jnp.concatenate([held, came], axis=0),
        )
    return held


def qkv_kernel(w_ref, n_ref, cos_ref, sin_ref, q_ref, kv_ref, *, query_heads, key_heads, scale):
    acc = mm(w_ref[...], n_ref[0], NT)
    cosine = cos_ref[0]
    sine = sin_ref[0]
    for head in range(query_heads):
        low = acc[DH * head : DH * head + HALF]
        high = acc[DH * head + HALF : DH * head + DH]
        q_ref[DH * head : DH * head + HALF, :] = ((low * cosine - high * sine) * scale).astype(bf16)
        q_ref[DH * head + HALF : DH * head + DH, :] = (
            (high * cosine + low * sine) * scale
        ).astype(bf16)
    base = DH * query_heads
    for head in range(key_heads):
        low = acc[base + DH * head : base + DH * head + HALF]
        high = acc[base + DH * head + HALF : base + DH * head + DH]
        at = 2 * DH * head
        kv_ref[at : at + HALF, :] = (low * cosine - high * sine).astype(bf16)
        kv_ref[at + HALF : at + DH, :] = (high * cosine + low * sine).astype(bf16)
        start = base + DH * (key_heads + head)
        kv_ref[at + DH : at + 2 * DH, :] = acc[start : start + DH].astype(bf16)


def project(row, w_t, gathered, cosine, sine, query_heads, key_heads):
    cols, width = w_t.shape
    count = gathered.shape[1]
    tile = 256
    q_cols = query_heads * DH
    kv_cols = 2 * key_heads * DH
    return pl.pallas_call(
        functools.partial(
            qkv_kernel, query_heads=query_heads, key_heads=key_heads, scale=DH ** (-0.5)
        ),
        grid=(count // tile,),
        in_specs=[
            pl.BlockSpec((cols, width), lambda i: (0, 0)),
            pl.BlockSpec((1, tile, width), lambda i: (row, i, 0)),
            pl.BlockSpec((1, HALF, tile), lambda i: (row, 0, i)),
            pl.BlockSpec((1, HALF, tile), lambda i: (row, 0, i)),
        ],
        out_specs=[
            pl.BlockSpec((q_cols, tile), lambda i: (0, i)),
            pl.BlockSpec((kv_cols, tile), lambda i: (0, i)),
        ],
        out_shape=[
            jax.ShapeDtypeStruct((q_cols, count), bf16),
            jax.ShapeDtypeStruct((kv_cols, count), bf16),
        ],
        compiler_params=pltpu.CompilerParams(vmem_limit_bytes=32 * 2**20),
        cost_estimate=pl.CostEstimate(
            flops=2 * cols * width * count, bytes_accessed=4 * count * width, transcendentals=0
        ),
    )(w_t, gathered, cosine, sine)


def forward_kernel(
    meta_ref, q_ref, kv_ref, start_ref, o_ref, low_ref, lse_ref, max_s, sum_s, acc_s,
    *, row, group, order
):
    span = q_ref.shape[1]
    here = meta_ref[0]
    first = meta_ref[1 + 2 * row]
    middle = meta_ref[2 + 2 * row]
    start = start_ref[0]
    key_iota = lax.broadcasted_iota(jnp.int32, (span, span), 0)

    def step(block, masked, diagonal):
        slot = 0 if diagonal else slot_of(block ^ here, order)
        k_t = kv_ref[slot, 0:DH, :]
        v_t = kv_ref[slot, DH : 2 * DH, :]
        keys = k_t.T
        if masked:
            keep = key_iota + block * span >= start
        if diagonal:
            keep = keep & (key_iota <= lax.broadcasted_iota(jnp.int32, (span, span), 1))
        for g in range(group):
            scores = mm(keys, q_ref[DH * g : DH * g + DH, :])
            if masked:
                scores = jnp.where(keep, scores, neg_big)
            top = jnp.max(scores, axis=0, keepdims=True)
            if diagonal:
                new_max = top
            else:
                old_max = max_s[g : g + 1, :]
                new_max = jnp.maximum(old_max, top)
            weights = jnp.exp(scores - new_max)
            total = jnp.sum(weights, axis=0, keepdims=True)
            mixed = mm(v_t, weights.astype(bf16))
            at = slice(DH * g, DH * g + DH)
            if diagonal:
                sum_s[g : g + 1, :] = total
                acc_s[at, :] = mixed
            else:
                factor = jnp.exp(old_max - new_max)
                sum_s[g : g + 1, :] = sum_s[g : g + 1, :] * factor + total
                acc_s[at, :] = acc_s[at, :] * factor + mixed
            max_s[g : g + 1, :] = new_max

    step(here, True, True)

    @pl.loop(first, middle)
    def _(block):
        step(block, True, False)

    @pl.loop(middle, here)
    def _(block):
        step(block, False, False)

    for g in range(group):
        at = slice(DH * g, DH * g + DH)
        total = sum_s[g : g + 1, :]
        out = acc_s[at, :] / total
        o_ref[at, :] = out
        low_ref[at, :] = out.astype(bf16)
        lse_ref[0, g : g + 1, :] = max_s[g : g + 1, :] + jnp.log(total)


def attend(row, meta, q_t, kv_all, starts, group, order):
    span = q_t.shape[1]
    blocks = kv_all.shape[0]
    key_heads = kv_all.shape[1] // (2 * DH)
    cols = group * DH
    head_spec = pl.BlockSpec((cols, span), lambda h, m: (h, 0))
    return pl.pallas_call(
        functools.partial(forward_kernel, row=row, group=group, order=order),
        grid_spec=pltpu.PrefetchScalarGridSpec(
            num_scalar_prefetch=1,
            grid=(key_heads,),
            in_specs=[
                head_spec,
                pl.BlockSpec((blocks, 2 * DH, span), lambda h, m: (0, h, 0)),
                pl.BlockSpec((1, 1, span), lambda h, m: (row, 0, 0)),
            ],
            out_specs=[
                head_spec,
                head_spec,
                pl.BlockSpec((1, group, span), lambda h, m: (h, 0, 0)),
            ],
            scratch_shapes=[
                pltpu.VMEM((group, span), f32),
                pltpu.VMEM((group, span), f32),
                pltpu.VMEM((cols, span), f32),
            ],
        ),
        out_shape=[
            jax.ShapeDtypeStruct((key_heads * cols, span), f32),
            jax.ShapeDtypeStruct((key_heads * cols, span), bf16),
            jax.ShapeDtypeStruct((key_heads, group, span), f32),
        ],
        compiler_params=pltpu.CompilerParams(vmem_limit_bytes=40 * 2**20),
        cost_estimate=pl.CostEstimate(
            flops=16 * blocks * span * span * cols,
            bytes_accessed=4 * kv_all.size,
            transcendentals=0,
        ),
    )(meta, q_t, kv_all, starts)


def backward_kernel(
    meta_ref, q_ref, do_ref, o_ref, lse_ref, kv_ref, start_ref, cos_ref, sin_ref,
    dq_ref, dkv_ref, dq_s, q_s, do_t_s, do_s, delta_s,
    *, row, group, order, scale
):
    span = q_ref.shape[1]
    here = meta_ref[0]
    first = meta_ref[1 + 2 * row]
    middle = meta_ref[2 + 2 * row]
    start = start_ref[0]
    key_iota = lax.broadcasted_iota(jnp.int32, (span, span), 0)
    dkv_ref[...] = jnp.zeros(dkv_ref.shape, bf16)
    part = do_ref.shape[2]
    for device in range(do_ref.shape[0]):
        do_t_s[:, part * device : part * (device + 1)] = do_ref[device]
    for g in range(group):
        at = slice(DH * g, DH * g + DH)
        q_s[g] = q_ref[at, :].T
        do_s[g] = do_t_s[at, :].T
        delta_s[g : g + 1, :] = jnp.sum(
            do_t_s[at, :].astype(f32) * o_ref[at, :], axis=0, keepdims=True
        )

    def step(block, masked, diagonal):
        slot = 0 if diagonal else slot_of(block ^ here, order)
        k_t = kv_ref[slot, 0:DH, :]
        v_t = kv_ref[slot, DH : 2 * DH, :]
        keys = k_t.T
        values = v_t.T
        if masked:
            keep = key_iota + block * span >= start
        if diagonal:
            keep = keep & (key_iota <= lax.broadcasted_iota(jnp.int32, (span, span), 1))
        d_keys = None
        d_values = None
        for g in range(group):
            at = slice(DH * g, DH * g + DH)
            scores = mm(keys, q_ref[at, :])
            probs = jnp.exp(scores - lse_ref[0, g : g + 1, :])
            if masked:
                probs = jnp.where(keep, probs, 0.0)
            d_probs = mm(values, do_t_s[at, :])
            d_scores = (probs * (d_probs - delta_s[g : g + 1, :])).astype(bf16)
            dq = mm(k_t, d_scores)
            if diagonal:
                dq_s[at, :] = dq
            else:
                dq_s[at, :] += dq
            dv = mm(probs.astype(bf16), do_s[g])
            dk = mm(d_scores, q_s[g])
            d_keys = dk if d_keys is None else d_keys + dk
            d_values = dv if d_values is None else d_values + dv
        dkv_ref[slot, 0:DH, :] = d_keys.T.astype(bf16)
        dkv_ref[slot, DH : 2 * DH, :] = d_values.T.astype(bf16)

    step(here, True, True)

    @pl.loop(first, middle)
    def _(block):
        step(block, True, False)

    @pl.loop(middle, here)
    def _(block):
        step(block, False, False)

    cosine = cos_ref[0]
    sine = sin_ref[0]
    for g in range(group):
        low = dq_s[DH * g : DH * g + HALF, :] * scale
        high = dq_s[DH * g + HALF : DH * g + DH, :] * scale
        dq_ref[DH * g : DH * g + HALF, :] = (low * cosine + high * sine).astype(bf16)
        dq_ref[DH * g + HALF : DH * g + DH, :] = (high * cosine - low * sine).astype(bf16)


def attend_back(row, meta, q_t, do_parts, o_t, lse, kv_all, starts, cosine, sine, group, order):
    span = q_t.shape[1]
    blocks = kv_all.shape[0]
    key_heads = kv_all.shape[1] // (2 * DH)
    cols = group * DH
    kv_devices, _, part = do_parts.shape
    head_spec = pl.BlockSpec((cols, span), lambda h, m: (h, 0))
    kv_spec = pl.BlockSpec((blocks, 2 * DH, span), lambda h, m: (0, h, 0))
    angle_spec = pl.BlockSpec((1, HALF, span), lambda h, m: (row, 0, 0))
    return pl.pallas_call(
        functools.partial(
            backward_kernel, row=row, group=group, order=order, scale=DH ** (-0.5)
        ),
        grid_spec=pltpu.PrefetchScalarGridSpec(
            num_scalar_prefetch=1,
            grid=(key_heads,),
            in_specs=[
                head_spec,
                pl.BlockSpec((kv_devices, cols, part), lambda h, m: (0, h, 0)),
                head_spec,
                pl.BlockSpec((1, group, span), lambda h, m: (h, 0, 0)),
                kv_spec,
                pl.BlockSpec((1, 1, span), lambda h, m: (row, 0, 0)),
                angle_spec,
                angle_spec,
            ],
            out_specs=[head_spec, kv_spec],
            scratch_shapes=[
                pltpu.VMEM((cols, span), f32),
                pltpu.VMEM((group, span, DH), bf16),
                pltpu.VMEM((cols, span), bf16),
                pltpu.VMEM((group, span, DH), bf16),
                pltpu.VMEM((group, span), f32),
            ],
        ),
        out_shape=[
            jax.ShapeDtypeStruct((key_heads * cols, span), bf16),
            jax.ShapeDtypeStruct(kv_all.shape, bf16),
        ],
        compiler_params=pltpu.CompilerParams(vmem_limit_bytes=40 * 2**20),
        cost_estimate=pl.CostEstimate(
            flops=40 * blocks * span * span * cols,
            bytes_accessed=4 * kv_all.size,
            transcendentals=0,
        ),
    )(meta, q_t, do_parts, o_t, lse, kv_all, starts, cosine, sine)


def experts_kernel(*refs, row_count, experts):
    heads = refs[:row_count]
    (
        x_ref, dy_ref, mix_ref, gain_ref, w_out_ref, gate_ref, up_ref, down_ref
    ) = refs[row_count : row_count + 8]
    outs = refs[row_count + 8 :]
    out_ref, dh_ref, ggate_ref, gup_ref, gdown_ref, gout_ref = outs[:6]
    d_heads = outs[6 : 6 + row_count]
    hid_s, hat_s, recip_s, norm_s, norm_t_s, acc_s, dn_s = outs[6 + row_count :]
    expert = pl.program_id(0)
    part = heads[0].shape[1]
    width = x_ref.shape[1]

    @pl.when(expert == 0)
    def _():
        for row in range(row_count):
            at = slice(part * row, part * (row + 1))
            branch = mm(heads[row][...].T, w_out_ref[...])
            hidden = x_ref[at, :].astype(f32) + branch
            recip = lax.rsqrt(jnp.mean(hidden * hidden, axis=-1, keepdims=True) + epsilon)
            hat = hidden * recip
            hid_s[at, :] = hidden
            hat_s[at, :] = hat
            recip_s[at, :] = recip
            norm_s[at, :] = (hat * gain_ref[...]).astype(bf16)
        norm_t_s[...] = norm_s[...].T
        acc_s[...] = hid_s[...]
        dn_s[...] = jnp.zeros(dn_s.shape, f32)

    normed = norm_s[...]
    mix = mix_ref[0]
    gate_pre = mm(normed, gate_ref[0])
    up_pre = mm(normed, up_ref[0])
    gate_sig = 1.0 / (1.0 + jnp.exp(-gate_pre))
    gate_act = gate_pre * gate_sig
    hid = (gate_act * up_pre).astype(bf16)
    acc_s[...] += mix * mm(hid, down_ref[0])
    d_expert = (mix * dy_ref[...].astype(f32)).astype(bf16)
    d_hid = mm(d_expert, down_ref[0], NT)
    d_gate = (d_hid * up_pre * (gate_sig * (1.0 + gate_pre * (1.0 - gate_sig)))).astype(bf16)
    d_up = (d_hid * gate_act).astype(bf16)
    dn_s[...] += mm(d_gate, gate_ref[0], NT) + mm(d_up, up_ref[0], NT)
    gdown_ref[0] = mm(hid.T, d_expert).astype(bf16)
    ggate_ref[0] = mm(norm_t_s[...], d_gate).astype(bf16)
    gup_ref[0] = mm(norm_t_s[...], d_up).astype(bf16)

    @pl.when(expert == experts - 1)
    def _():
        out_ref[...] = acc_s[...].astype(bf16)
        hat = hat_s[...]
        d_norm = dn_s[...]
        head_cols = w_out_ref.shape[0]
        gout_ref[head_cols:, :] = jnp.broadcast_to(
            jnp.sum(d_norm * hat, axis=0, keepdims=True), (16, width)
        ).astype(bf16)
        d_hat = d_norm * gain_ref[...]
        mean = jnp.mean(d_hat * hat, axis=-1, keepdims=True)
        d_hidden = dy_ref[...].astype(f32) + recip_s[...] * (d_hat - hat * mean)
        dh_ref[...] = d_hidden
        d_branch = d_hidden.astype(bf16)
        grad_out = None
        for row in range(row_count):
            at = slice(part * row, part * (row + 1))
            piece = d_branch[at, :]
            d_heads[row][...] = mm(w_out_ref[...], piece, NT).astype(bf16)
            term = mm(heads[row][...], piece)
            grad_out = term if grad_out is None else grad_out + term
        gout_ref[0:head_cols, :] = grad_out.astype(bf16)


def run_experts(heads, x_rows, dy_rows, mix, gain, w_out_all, w_gate, w_up, w_down):
    own, width = x_rows.shape
    experts, _, hidden = w_gate.shape
    row_count = len(heads)
    head_cols, part = heads[0].shape

    def whole(shape):
        return pl.BlockSpec(shape, lambda e: (0,) * len(shape))

    gate_spec = pl.BlockSpec((1, width, hidden), lambda e: (e, 0, 0))
    down_spec = pl.BlockSpec((1, hidden, width), lambda e: (e, 0, 0))
    return pl.pallas_call(
        functools.partial(experts_kernel, row_count=row_count, experts=experts),
        grid=(experts,),
        in_specs=[whole((head_cols, part))] * row_count
        + [
            whole((own, width)),
            whole((own, width)),
            pl.BlockSpec((1, own, 1), lambda e: (e, 0, 0)),
            whole((1, width)),
            whole((head_cols, width)),
            gate_spec,
            gate_spec,
            down_spec,
        ],
        out_specs=[
            whole((own, width)),
            whole((own, width)),
            gate_spec,
            gate_spec,
            down_spec,
            whole((head_cols + 16, width)),
        ]
        + [whole((head_cols, part))] * row_count,
        out_shape=[
            jax.ShapeDtypeStruct((own, width), bf16),
            jax.ShapeDtypeStruct((own, width), f32),
            jax.ShapeDtypeStruct(w_gate.shape, bf16),
            jax.ShapeDtypeStruct(w_up.shape, bf16),
            jax.ShapeDtypeStruct(w_down.shape, bf16),
            jax.ShapeDtypeStruct((head_cols + 16, width), bf16),
        ]
        + [jax.ShapeDtypeStruct((head_cols, part), bf16)] * row_count,
        scratch_shapes=[
            pltpu.VMEM((own, width), f32),
            pltpu.VMEM((own, width), f32),
            pltpu.VMEM((own, 1), f32),
            pltpu.VMEM((own, width), bf16),
            pltpu.VMEM((width, own), bf16),
            pltpu.VMEM((own, width), f32),
            pltpu.VMEM((own, width), f32),
        ],
        compiler_params=pltpu.CompilerParams(vmem_limit_bytes=56 * 2**20),
        cost_estimate=pl.CostEstimate(
            flops=18 * own * width * hidden * experts,
            bytes_accessed=6 * w_gate.size * 2,
            transcendentals=0,
        ),
    )(*heads, x_rows, dy_rows, mix, gain, w_out_all, w_gate, w_up, w_down)


def inner_kernel(*refs, row_count, query_cols, key_heads):
    dq = refs[:row_count]
    dkv = refs[row_count : 2 * row_count]
    n_ref, cos_ref, sin_ref, parts_ref, grad_ref, inner_s = refs[2 * row_count :]
    kv_devices = parts_ref.shape[0]
    part = parts_ref.shape[2] // row_count
    grad = None
    for row in range(row_count):
        cosine = cos_ref[row]
        sine = sin_ref[row]
        inner_s[0:query_cols, :] = dq[row][...]
        for head in range(key_heads):
            at = 2 * DH * head
            low = dkv[row][at : at + HALF, :].astype(f32)
            high = dkv[row][at + HALF : at + DH, :].astype(f32)
            to = query_cols + DH * head
            inner_s[to : to + HALF, :] = (low * cosine + high * sine).astype(bf16)
            inner_s[to + HALF : to + DH, :] = (high * cosine - low * sine).astype(bf16)
            to = query_cols + DH * (key_heads + head)
            inner_s[to : to + DH, :] = dkv[row][at + DH : at + 2 * DH, :]
        for device in range(kv_devices):
            parts_ref[device, :, part * row : part * (row + 1)] = inner_s[
                :, part * device : part * (device + 1)
            ]
        term = mm(inner_s[...], n_ref[row])
        grad = term if grad is None else grad + term
    grad_ref[...] = grad.astype(bf16)


def inner_grads(dq, dkv, gathered, cosine, sine, kv_devices, key_heads):
    row_count = len(dq)
    query_cols, span = dq[0].shape
    cols, width = query_cols + dkv[0].shape[0], gathered.shape[2]
    own = row_count * span // kv_devices
    return pl.pallas_call(
        functools.partial(
            inner_kernel, row_count=row_count, query_cols=query_cols, key_heads=key_heads
        ),
        out_shape=[
            jax.ShapeDtypeStruct((kv_devices, cols, own), bf16),
            jax.ShapeDtypeStruct((cols, width), bf16),
        ],
        scratch_shapes=[pltpu.VMEM((cols, span), bf16)],
        compiler_params=pltpu.CompilerParams(vmem_limit_bytes=40 * 2**20),
        cost_estimate=pl.CostEstimate(
            flops=2 * row_count * span * cols * width,
            bytes_accessed=4 * gathered.size,
            transcendentals=0,
        ),
    )(*dq, *dkv, gathered, cosine, sine)


def tokens_kernel(d_inner_ref, w_ref, x_ref, dh_ref, gain_ref, out_ref):
    x_float = x_ref[...].astype(f32)
    recip = lax.rsqrt(jnp.mean(x_float * x_float, axis=-1, keepdims=True) + epsilon)
    x_hat = x_float * recip
    d_normed = mm(d_inner_ref[...].T, w_ref[...])
    d_hat = d_normed * gain_ref[...]
    mean = jnp.mean(d_hat * x_hat, axis=-1, keepdims=True)
    out_ref[...] = (dh_ref[...] + recip * (d_hat - x_hat * mean)).astype(bf16)


def token_grads(d_inner, w_all, x_rows, d_hidden, gain):
    own, width = x_rows.shape
    cols = d_inner.shape[0]
    return pl.pallas_call(
        tokens_kernel,
        out_shape=jax.ShapeDtypeStruct((own, width), bf16),
        compiler_params=pltpu.CompilerParams(vmem_limit_bytes=40 * 2**20),
        cost_estimate=pl.CostEstimate(
            flops=2 * own * width * cols, bytes_accessed=2 * cols * width, transcendentals=0
        ),
    )(d_inner, w_all, x_rows, d_hidden, gain)


def widen_kernel(*refs):
    half = len(refs) // 2
    for source, target in zip(refs[:half], refs[half:]):
        target[...] = source[...].astype(f32)


def widen(arrays):
    specs = [pl.BlockSpec((1,) + a.shape[1:], lambda e: (e, 0, 0)) for a in arrays]
    return pl.pallas_call(
        widen_kernel,
        grid=(arrays[0].shape[0],),
        in_specs=specs,
        out_specs=specs,
        out_shape=[jax.ShapeDtypeStruct(a.shape, f32) for a in arrays],
        compiler_params=pltpu.CompilerParams(vmem_limit_bytes=40 * 2**20),
        cost_estimate=pl.CostEstimate(
            flops=0, bytes_accessed=6 * sum(a.size for a in arrays), transcendentals=0
        ),
    )(*arrays)


def per_device(
    tokens,
    cotangent,
    norm_first,
    w_query,
    w_key,
    w_value,
    w_out,
    norm_second,
    w_gate,
    w_up,
    w_down,
    routes,
    gate_weights,
    segment_ids,
    positions,
):
    row_count, block_len, width = tokens.shape
    kv_devices = lax.axis_size("kv")
    seq_devices = lax.axis_size("seq")
    seq_len = block_len * kv_devices
    seq_index = lax.axis_index("seq")
    query_cols = w_query.shape[1]
    key_cols = w_key.shape[1]
    query_heads = query_cols // DH
    key_heads = key_cols // DH
    group = query_heads // key_heads
    expert_count = w_gate.shape[0]
    own = row_count * block_len
    rows = range(row_count)
    orders = [seq_order(row, seq_devices) for row in rows]

    place = seq_index * seq_len + jnp.arange(seq_len, dtype=jnp.int32)
    starts = place[None, :] - positions
    first_block = starts[:, 0] // seq_len
    middle_block = jnp.clip((starts[:, -1] + seq_len - 1) // seq_len, first_block, seq_index)
    bounds = jnp.stack([first_block, middle_block], axis=1).reshape(-1)
    meta = jnp.concatenate([seq_index[None], bounds]).astype(jnp.int32)
    starts3 = starts.reshape(row_count, 1, seq_len)
    freqs = theta_base ** (-(jnp.arange(HALF, dtype=f32) * 2.0) / DH)
    angles = freqs[None, :, None] * positions.astype(f32)[:, None, :]
    cosine = jnp.cos(angles)
    sine = jnp.sin(angles)

    x_float = tokens.astype(f32)
    recip_first = lax.rsqrt(jnp.mean(x_float * x_float, axis=-1, keepdims=True) + epsilon)
    normed = (x_float * recip_first * norm_first).astype(bf16)
    gathered = lax.all_gather(normed, "kv", axis=1, tiled=True)

    w_t = jnp.concatenate([w_query.T, w_key.T, w_value.T], axis=0)
    inner_cols = w_t.shape[0]
    expert_ids = jnp.arange(expert_count, dtype=jnp.int32)
    picks = routes[..., None] == expert_ids
    local_load = jnp.sum(picks.astype(f32), axis=(0, 1, 2))
    load_rows = jnp.pad(local_load.astype(bf16)[None, :], ((0, 15), (0, width - expert_count)))

    def gather_rows(matrix, extra=None):
        share = matrix.shape[0] // seq_devices
        piece = lax.dynamic_slice_in_dim(matrix, seq_index * share, share, 0)
        if extra is not None:
            piece = jnp.concatenate([piece, extra], axis=0)
        spread = lax.all_gather(piece, ("seq", "kv"))
        spread = spread.reshape(seq_devices, kv_devices, piece.shape[0], width)
        whole = spread[:, :, :share].transpose(1, 0, 2, 3)
        return whole.reshape(kv_devices * matrix.shape[0], width), spread[:, :, share:]

    w_out_all, loads = gather_rows(w_out, load_rows)
    load_sum = jnp.sum(loads[:, :, 0, :expert_count].astype(f32), axis=(0, 1))
    w_inner_all, _ = gather_rows(w_t)

    def exchange(value):
        return lax.all_to_all(value, "kv", 0, 0)

    q_t, kv_all, o_t, lse, heads = [], [], [], [], []
    for row in rows:
        q_row, kv_row = project(row, w_t, gathered, cosine, sine, query_heads, key_heads)
        q_t.append(q_row)
        kv_all.append(spread_seq(kv_row, orders[row]))
    for row in rows:
        o_row, low_row, lse_row = attend(
            row, meta, q_t[row], kv_all[row], starts3, group, orders[row]
        )
        o_t.append(o_row)
        lse.append(lse_row)
        parts = low_row.reshape(query_cols, kv_devices, block_len).transpose(1, 0, 2)
        heads.append(exchange(parts).reshape(kv_devices * query_cols, block_len))

    mix = jnp.sum(picks.astype(f32) * gate_weights[..., None], axis=2)
    mix = mix.reshape(own, expert_count).T[:, :, None]
    x_rows = tokens.reshape(own, width)
    outs = run_experts(
        heads,
        x_rows,
        cotangent.reshape(own, width),
        mix,
        norm_second.reshape(1, width),
        w_out_all,
        w_gate,
        w_up,
        w_down,
    )
    block_out, d_hidden, grad_gate, grad_up, grad_down, grad_out = outs[:6]
    d_heads = outs[6:]
    grad_gate, grad_up, grad_down, grad_out = lax.psum(
        (grad_gate, grad_up, grad_down, grad_out), ("seq", "kv")
    )
    second_sum = grad_out[kv_devices * query_cols]

    do_parts = [exchange(d.reshape(kv_devices, query_cols, block_len)) for d in d_heads]
    dq, dkv = [], []
    for row in rows:
        dq_row, dkv_row = attend_back(
            row, meta, q_t[row], do_parts[row], o_t[row], lse[row], kv_all[row], starts3,
            cosine, sine, group, orders[row],
        )
        dq.append(dq_row)
        dkv.append(collect_seq(dkv_row, orders[row]))
    d_parts, grad_inner_part = inner_grads(
        dq, dkv, gathered, cosine, sine, kv_devices, key_heads
    )
    d_inner = exchange(d_parts).reshape(kv_devices * inner_cols, own)
    half = inner_cols // 2
    grad_inner = jnp.concatenate(
        [
            sum_seq(grad_inner_part[:half], seq_order(0, seq_devices)),
            sum_seq(grad_inner_part[half:], seq_order(1, seq_devices)),
        ],
        axis=0,
    ).astype(f32)
    first_part = jnp.sum(w_t.astype(f32) * grad_inner, axis=0)
    first_sum = lax.psum(first_part, "kv") / norm_first
    d_tokens = token_grads(d_inner, w_inner_all, x_rows, d_hidden, norm_first.reshape(1, width))
    grad_gate, grad_up, grad_down = widen([grad_gate, grad_up, grad_down])
    own_out = lax.dynamic_slice_in_dim(
        grad_out, lax.axis_index("kv") * query_cols, query_cols, 0
    ).astype(f32)
    return (
        block_out.reshape(tokens.shape),
        d_tokens.reshape(tokens.shape),
        first_sum,
        grad_inner[:query_cols].T,
        grad_inner[query_cols : query_cols + key_cols].T,
        grad_inner[query_cols + key_cols :].T,
        own_out,
        second_sum.astype(f32),
        grad_gate,
        grad_up,
        grad_down,
        load_sum.astype(jnp.int32),
    )


def solution(mesh):
    in_specs = (
        P(None, ("seq", "kv"), None),
        P(None, ("seq", "kv"), None),
        P(),
        P(None, "kv"),
        P(None, "kv"),
        P(None, "kv"),
        P("kv", None),
        P(),
        P(),
        P(),
        P(),
        P(None, ("seq", "kv"), None),
        P(None, ("seq", "kv"), None),
        P(),
        P(None, "seq"),
    )
    out_specs = (
        P(None, ("seq", "kv"), None),
        P(None, ("seq", "kv"), None),
        P(),
        P(None, "kv"),
        P(None, "kv"),
        P(None, "kv"),
        P("kv", None),
        P(),
        P(),
        P(),
        P(),
        P(),
    )
    return jax.shard_map(
        per_device, mesh=mesh, in_specs=in_specs, out_specs=out_specs, check_vma=False
    )
```

time: 670 us -> 493 us (0.74)
  waiting for transfers between devices: 443 us -> 241 us
  starting transfers between devices: 9.65 us -> 101 us
  matrix products: 35 us -> 0 us
  Pallas kernels: 19.8 us -> 51.6 us
  blocking collectives: 44.2 us -> 13.8 us
  local copies, waits for them, and re-layouts: 67.6 us -> 45.7 us
  other arithmetic: 34.3 us -> 23.2 us
    psum x2 -> x1, waiting for transfers between devices: 263 us -> 114 us  [per_device(): lax.psum((grad_gate, grad_up, grad_down, grad_out), ('seq', 'kv'))]
    all_gather x4 -> x3, waiting for transfers between devices: 129 us -> 45.8 us  [the longest x1 45.8 us: per_device(): gathered = lax.all_gather(normed, 'kv', axis=1, tiled=True)]
    ppermute x0 -> x24, starting transfers between devices: none -> 79.6 us  [swap(): lax.ppermute(value, axis, [(source, source ^ mask) for source in range(co...]
    ppermute x0 -> x24, waiting for transfers between devices: none -> 60.4 us  [swap(): lax.ppermute(value, axis, [(source, source ^ mask) for source in range(co...]
    dot_general x14 -> x0, matrix products: 35 us -> none  [the longest x2 5.51 us: mm(): return lax.dot_general(a, b, dims, preferred_element_type=f32)]
    reduce_scatter x1 -> x0, waiting for transfers between devices: 33.5 us -> none  [per_device(): dkv = lax.psum_scatter(dkv_part, 'seq').astype(f32)]
    pallas_call x2 -> x8, Pallas kernels: 17 us -> 49.5 us  [the longest x1 21.9 us: run_experts(): pl.pallas_call(functools.partial(experts_kernel, row_count=row_count, exp...]
    all_to_all x1 -> x0, blocking collectives: 32.4 us -> none  [exchange(): return lax.all_to_all(value, 'kv', 0, 0)]
  transfers between devices with their start and end apart: 9 -> 33, of which waited for: 7 -> 18; matrix products, arithmetic and copies ran while one was open for 14% -> 8% of each run, Pallas kernels for 3% -> 9%
where the time goes in v2:
time: 493 us; the launch traced here: 491 us
  waiting for transfers between devices  241 us (49%)
  starting transfers between devices  101 us (20%)
  Pallas kernels  51.6 us (10%)
  local copies, waits for them, and re-layouts  45.7 us (9%)
  other arithmetic  23.2 us (5%)
  between operations  14.5 us (3%)
  blocking collectives  13.8 us (3%)
    psum x1, waiting for transfers between devices, per_device(): lax.psum((grad_gate, grad_up, grad_down, grad_out), ('seq', 'kv'))  114 us
    ppermute x24, starting transfers between devices, swap(): lax.ppermute(value, axis, [(source, source ^ mask) for source in range(co...  79.6 us
    ppermute x24, waiting for transfers between devices, swap(): lax.ppermute(value, axis, [(source, source ^ mask) for source in range(co...  60.4 us
    all_gather x1, waiting for transfers between devices, per_device(): gathered = lax.all_gather(normed, 'kv', axis=1, tiled=True)  45.8 us
    unnamed x93, local copies, waits for them, and re-layouts  30.1 us
    pallas_call x1, Pallas kernels, run_experts(): pl.pallas_call(functools.partial(experts_kernel, row_count=row_count, exp...  21.9 us
    all_to_all x5, starting transfers between devices, exchange(): return lax.all_to_all(value, 'kv', 0, 0)  21.6 us
    all_to_all x5, waiting for transfers between devices, exchange(): return lax.all_to_all(value, 'kv', 0, 0)  20.3 us
  transfers between devices with their start and end apart: 33, of which 18 were waited for; matrix products, arithmetic and copies ran while one was open for 8% of the time, Pallas kernels for 9%

profile of v2, /device:TPU:0, one launch (start us, length us, event | category | flops | bytes accessed | tf_op | source)
XLA Modules:
  0.0 491.0 jit_solution(1555968443763630753)
XLA Ops:
  13.7 45.8 %all-gather.6.cloned.1.call-done.n_ref.refs_4_ = bf16[2,512,1024]{2,1,0:T(8,128)(2,1)} async-done(((bf16[2,128,1024]{2,1,0:T(8,128)(2,1)}), bf16[2,512,1024]{2,1,0:T(8,128)(2,1)}) %all-gather.6.cloned.1.call-update) | async-done | bytes 2097168 | tf_op jit(solution)/shard_map/all_gather | solution.py:643
  63.7 6.5 %collective-permute-done.3 = bf16[1,256,512]{2,1,0:T(8,128)(2,1)S(1)} collective-permute-done((bf16[1,256,512]{2,1,0:T(8,128)(2,1)S(1)}, bf16[1,256,512]{2,1,0:T(8,128)(2,1)S(1)}, u32[]{:S(2)}, u32[]{:S(2)}) %collective-permute-start.3) | collective-permute-done | bytes 262176 | tf_op jit(solution)/shard_map/ppermute | solution.py:51
  73.4 11.6 %collective-permute-done.4 = bf16[2,256,512]{2,1,0:T(8,128)(2,1)S(1)} collective-permute-done((bf16[2,256,512]{2,1,0:T(8,128)(2,1)S(1)}, bf16[2,256,512]{2,1,0:T(8,128)(2,1)S(1)}, u32[]{:S(2)}, u32[]{:S(2)}) %collective-permute-start.4) | collective-permute-done | bytes 524320 | tf_op jit(solution)/shard_map/ppermute | solution.py:51
  86.2 4.9 collective-permute-done
  92.7 9.4 %collective-permute-done.1 = bf16[2,256,512]{2,1,0:T(8,128)(2,1)S(1)} collective-permute-done((bf16[2,256,512]{2,1,0:T(8,128)(2,1)S(1)}, bf16[2,256,512]{2,1,0:T(8,128)(2,1)S(1)}, u32[]{:S(2)}, u32[]{:S(2)}) %collective-permute-start.1) | collective-permute-done | bytes 524320 | tf_op jit(solution)/shard_map/ppermute | solution.py:51
  105.2 2.8 shard_map.232
  109.5 3.7 all-to-all-start.1
  114.7 2.8 shard_map.230
  119.0 4.7 all-to-all-done.1
  123.7 3.6 all-to-all-start
  131.6 4.3 all-to-all-done
  136.6 21.9 %shard_map.233 = (bf16[256,1024]{1,0:T(8,128)(2,1)}, f32[256,1024]{1,0:T(8,128)}, bf16[4,1024,512]{2,1,0:T(8,128)(2,1)}, bf16[4,1024,512]{2,1,0:T(8,128)(2,1)}, ...) custom-call(bf16[1024,128]{1,0:T(8,128)(2,1)} %bitcast.84, ...), custom_call_target="tpu_custom_call" | custom-call | flops 9663676416 | bytes 25165824 | tf_op jit(solution)/shard_map/pallas_call | solution.py:450
  158.5 4.6 all-to-all-start.2
  163.7 11.3 %all-to-all-done.2.do_ref = bf16[4,256,128]{2,1,0:T(8,128)(2,1)S(1)} async-done(((bf16[4,256,128]{2,1,0:T(8,128)(2,1)}), bf16[4,256,128]{2,1,0:T(8,128)(2,1)S(1)}, u32[]{:S(2)}, u32[]{:S(2)}) %all-to-all-start.2) | async-done | bytes 262176 | tf_op jit(solution)/shard_map/all_to_all | solution.py:667
  175.0 4.9 %all-to-all-start.3 = ((bf16[4,256,128]{2,1,0:T(8,128)(2,1)}), bf16[4,256,128]{2,1,0:T(8,128)(2,1)S(1)}, u32[]{:S(2)}, u32[]{:S(2)}) async-start(bf16[4,256,128]{2,1,0:T(8,128)(2,1)} %bitcast.22), calls=%async_computation.3 | async-start | bytes 524288 | tf_op jit(solution)/shard_map/all_to_all | solution.py:667
  183.5 4.7 shard_map.234
  189.3 4.4 collective-permute-start.6
  196.3 5.0 %shard_map.235 = (bf16[256,512]{1,0:T(8,128)(2,1)S(1)}, bf16[8,256,512]{2,1,0:T(8,128)(2,1)S(1)}) custom-call(s32[5]{0:T(128)S(1)} %pad_add_fusion.1.meta_ref, bf16[256,512]{1,0:T(8,128)(2,1)S(1)} %get-tuple-element.42.q_ref, bf16[4,256,128]{2,1,0:T(8,128)(2,1)S(1)} %all-to-all-done.3.do_ref, f32[256,512]{1,0:T(8,128)S(1)} %copy-done.23, ...), custom_call_target="tpu_custom_call" | custom-call | flops 10737418240 | bytes 4194304 | tf_op jit(solution)/shard_map/pallas_call | solution.py:330
  201.4 3.7 collective-permute-start.9
  206.7 33.9 %collective-permute-start.7 = (bf16[2,256,512]{2,1,0:T(8,128)(2,1)S(1)}, bf16[2,256,512]{2,1,0:T(8,128)(2,1)S(1)}, u32[]{:S(2)}, u32[]{:S(2)}) collective-permute-start(bf16[2,256,512]{2,1,0:T(8,128)(2,1)S(1)} %slice.152), channel_id=1, source_target_pairs={{0,16},{4,20},{8,24},{12,28},{16,0},{20,4},{24,8},{28,12},{1,17},{... | collective-permute-start | bytes 1572872 | tf_op jit(solution)/shard_map/ppermute | solution.py:51
  240.9 16.1 %collective-permute-start.10 = (bf16[2,256,512]{2,1,0:T(8,128)(2,1)S(1)}, bf16[2,256,512]{2,1,0:T(8,128)(2,1)S(1)}, u32[]{:S(2)}, u32[]{:S(2)}) collective-permute-start(bf16[2,256,512]{2,1,0:T(8,128)(2,1)S(1)} %slice.156), channel_id=1, source_target_pairs={{0,8},{4,12},{8,0},{12,4},{16,24},{20,28},{24,16},{28,20},{1,9},{5... | collective-permute-start | bytes 1572872 | tf_op jit(solution)/shard_map/ppermute | solution.py:51
  256.9 6.4 %collective-permute-done.7 = bf16[2,256,512]{2,1,0:T(8,128)(2,1)S(1)} collective-permute-done((bf16[2,256,512]{2,1,0:T(8,128)(2,1)S(1)}, bf16[2,256,512]{2,1,0:T(8,128)(2,1)S(1)}, u32[]{:S(2)}, u32[]{:S(2)}) %collective-permute-start.7) | collective-permute-done | bytes 524320 | tf_op jit(solution)/shard_map/ppermute | solution.py:51
  264.2 6.5 %collective-permute-start.8 = (bf16[1,256,512]{2,1,0:T(8,128)(2,1)}, bf16[1,256,512]{2,1,0:T(8,128)(2,1)}, u32[]{:S(2)}, u32[]{:S(2)}) collective-permute-start(bf16[1,256,512]{2,1,0:T(8,128)(2,1)} %slice.154), channel_id=1, source_target_pairs={{0,8},{4,12},{8,0},{12,4},{16,24},{20,28},{24,16},{28,20},{1,9},{5... | collective-permute-start | bytes 786440 | tf_op jit(solution)/shard_map/ppermute | solution.py:51
  272.8 4.5 collective-permute-done.8
  289.1 5.2 %collective-permute-done.13 = bf16[64,1024]{1,0:T(8,128)(2,1)S(1)} collective-permute-done((bf16[64,1024]{1,0:T(8,128)(2,1)S(1)}, bf16[64,1024]{1,0:T(8,128)(2,1)S(1)}, u32[]{:S(2)}, u32[]{:S(2)}) %collective-permute-start.13) | collective-permute-done | bytes 131104 | tf_op jit(solution)/shard_map/ppermute | solution.py:51
  303.5 4.8 all-to-all-start.4
  310.0 5.2 %collective-permute-done.22 = bf16[64,1024]{1,0:T(8,128)(2,1)S(1)} collective-permute-done((bf16[64,1024]{1,0:T(8,128)(2,1)S(1)}, bf16[64,1024]{1,0:T(8,128)(2,1)S(1)}, u32[]{:S(2)}, u32[]{:S(2)}) %collective-permute-start.22) | collective-permute-done | bytes 131104 | tf_op jit(solution)/shard_map/ppermute | solution.py:51
  316.8 4.9 copy.58
  323.3 13.8 %psum.35 = f32[1024]{0:T(1024)S(1)} all-reduce(f32[1024]{0:T(1024)S(1)} %multiply_reduce_fusion), channel_id=1, replica_groups=mesh['seq'=8,'kv'=4] {'kv'}, use_global_device_ids=true, to_apply=%region_4.5 | all-reduce | flops 1024 | bytes 8192 | tf_op jit(solution)/shard_map/psum | solution.py:726
  343.9 2.6 copy.59
  352.0 113.8 %all-reduce.4.cloned.1.call-done = (bf16[1040,1024]{1,0:T(8,128)(2,1)}, bf16[4,1024,512]{2,1,0:T(8,128)(2,1)}, bf16[4,1024,512]{2,1,0:T(8,128)(2,1)}, bf16[4,512,1024]{2,1,0:T(8,128)(2,1)}) async-done(((bf16[1040,1024]{1,0:T(8,128)(2,1)}, bf16[4,1024,512]{2,1,0:T(8,128)(2,1)}, bf16[4,1024,512]{2,1,0:T(8,128)(2,1)}, bf16[4,512,1024]{2,1,0:T(8,128)(2,1)}), (bf16[1040,1024]{1,0:T(8,128)(2,1)}, ...) | async-done | bytes 14712848 | tf_op jit(solution)/shard_map/psum | solution.py:699
  475.8 8.6 %shard_map.238 = (f32[4,1024,512]{2,1,0:T(8,128)}, f32[4,1024,512]{2,1,0:T(8,128)}, f32[4,512,1024]{2,1,0:T(8,128)}) custom-call(bf16[4,1024,512]{2,1,0:T(8,128)(2,1)S(1)} %copy-done.6, bf16[4,1024,512]{2,1,0:T(8,128)(2,1)S(1)} %copy-done.7, bf16[4,512,1024]{2,1,0:T(8,128)(2,1)S(1)} %copy-done.8), custom_call_target="tpu_custom_call" | custom-call | bytes 37748736 | tf_op jit(solution)/shard_map/pallas_call | solution.py:583
  (207 shorter events, 89.7 us)
Async XLA Ops:
  7.2 52.2 %all-gather.6.cloned.1.call-start = ((), (), s32[]{:S(2)}) async-start(), calls=%async_computation.5 | async-start | bytes 2621440 | tf_op jit(solution)/shard_map/all_gather | solution.py:643
  10.7 117.6 %all-gather.8.cloned.1.call-start = ((), (), s32[]{:S(2)}) async-start(), calls=%async_computation.6 | async-start | bytes 3244032 | tf_op jit(solution)/shard_map/all_gather | solution.py:657
  11.6 305.2 %all-gather.10.cloned.1.call-start = ((), (), s32[]{:S(2)}) async-start(), calls=%async_computation.7 | async-start | bytes 4325376 | tf_op jit(solution)/shard_map/all_gather | solution.py:657
  62.1 8.1 %collective-permute-start.3 = (bf16[1,256,512]{2,1,0:T(8,128)(2,1)S(1)}, bf16[1,256,512]{2,1,0:T(8,128)(2,1)S(1)}, u32[]{:S(2)}, u32[]{:S(2)}) collective-permute-start(bf16[1,256,512]{2,1,0:T(8,128)(2,1)S(1)} %bitcast.66), channel_id=1, source_target_pairs={{0,16},{4,20},{8,24},{12,28},{16,0},{20,4},{24,8},{28,12},{1,17},{... | collective-permute-start | bytes 786440 | tf_op jit(solution)/shard_map/ppermute | solution.py:51
  70.2 14.8 %collective-permute-start.4 = (bf16[2,256,512]{2,1,0:T(8,128)(2,1)S(1)}, bf16[2,256,512]{2,1,0:T(8,128)(2,1)S(1)}, u32[]{:S(2)}, u32[]{:S(2)}) collective-permute-start(bf16[2,256,512]{2,1,0:T(8,128)(2,1)S(1)} %pad_maximum_fusion.6), channel_id=1, source_target_pairs={{0,8},{4,12},{8,0},{12,4},{16,24},{20,28},{24,16},{28,20},{1,9},{5... | collective-permute-start | bytes 1572872 | tf_op jit(solution)/shard_map/ppermute | solution.py:51
  72.8 18.3 %collective-permute-start = (bf16[1,256,512]{2,1,0:T(8,128)(2,1)S(1)}, bf16[1,256,512]{2,1,0:T(8,128)(2,1)S(1)}, u32[]{:S(2)}, u32[]{:S(2)}) collective-permute-start(bf16[1,256,512]{2,1,0:T(8,128)(2,1)S(1)} %bitcast.62), channel_id=1, source_target_pairs={{0,8},{4,12},{8,0},{12,4},{16,24},{20,28},{24,16},{28,20},{1,9},{5... | collective-permute-start | bytes 786440 | tf_op jit(solution)/shard_map/ppermute | solution.py:51
  86.2 17.2 %collective-permute-start.5 = (bf16[4,256,512]{2,1,0:T(8,128)(2,1)}, bf16[4,256,512]{2,1,0:T(8,128)(2,1)}, u32[]{:S(2)}, u32[]{:S(2)}) collective-permute-start(bf16[4,256,512]{2,1,0:T(8,128)(2,1)} %pad_maximum_fusion.4), channel_id=1, source_target_pairs={{0,4},{4,0},{8,12},{12,8},{16,20},{20,16},{24,28},{28,24},{1,5},{5... | collective-permute-start | bytes 3145736 | tf_op jit(solution)/shard_map/ppermute | solution.py:51
  91.1 10.9 %collective-permute-start.1 = (bf16[2,256,512]{2,1,0:T(8,128)(2,1)S(1)}, bf16[2,256,512]{2,1,0:T(8,128)(2,1)S(1)}, u32[]{:S(2)}, u32[]{:S(2)}) collective-permute-start(bf16[2,256,512]{2,1,0:T(8,128)(2,1)S(1)} %pad_maximum_fusion.5), channel_id=1, source_target_pairs={{0,16},{4,20},{8,24},{12,28},{16,0},{20,4},{24,8},{28,12},{1,17},{... | collective-permute-start | bytes 1572872 | tf_op jit(solution)/shard_map/ppermute | solution.py:51
  103.2 10.0 %collective-permute-start.2 = (bf16[4,256,512]{2,1,0:T(8,128)(2,1)}, bf16[4,256,512]{2,1,0:T(8,128)(2,1)}, u32[]{:S(2)}, u32[]{:S(2)}) collective-permute-start(bf16[4,256,512]{2,1,0:T(8,128)(2,1)} %pad_maximum_fusion.3), channel_id=1, source_target_pairs={{0,4},{4,0},{8,12},{12,8},{16,20},{20,16},{24,28},{28,24},{1,5},{5... | collective-permute-start | bytes 3145736 | tf_op jit(solution)/shard_map/ppermute | solution.py:51
  109.5 14.2 %all-to-all-start.1 = ((bf16[4,256,128]{2,1,0:T(8,128)(2,1)}), bf16[4,256,128]{2,1,0:T(8,128)(2,1)S(1)}, u32[]{:S(2)}, u32[]{:S(2)}) async-start(bf16[4,256,128]{2,1,0:T(8,128)(2,1)} %bitcast_bitcast_fusion), calls=%async_computation.1 | async-start | bytes 524288 | tf_op jit(solution)/shard_map/all_to_all | solution.py:667
  123.7 12.2 %all-to-all-start = ((bf16[4,256,128]{2,1,0:T(8,128)(2,1)}), bf16[4,256,128]{2,1,0:T(8,128)(2,1)S(1)}, u32[]{:S(2)}, u32[]{:S(2)}) async-start(bf16[4,256,128]{2,1,0:T(8,128)(2,1)} %bitcast_bitcast_fusion.1), calls=%async_computation | async-start | bytes 524288 | tf_op jit(solution)/shard_map/all_to_all | solution.py:667
  158.5 16.5 %all-to-all-start.2 = ((bf16[4,256,128]{2,1,0:T(8,128)(2,1)}), bf16[4,256,128]{2,1,0:T(8,128)(2,1)S(1)}, u32[]{:S(2)}, u32[]{:S(2)}) async-start(bf16[4,256,128]{2,1,0:T(8,128)(2,1)} %bitcast.83), calls=%async_computation.2 | async-start | bytes 524288 | tf_op jit(solution)/shard_map/all_to_all | solution.py:667
  163.1 302.7 %all-reduce.4.cloned.1.call-start = ((), (), s32[]{:S(2)}) async-start(), calls=%async_computation.8 | async-start | bytes 29425664 | tf_op jit(solution)/shard_map/psum | solution.py:699
  175.0 18.7 %all-to-all-start.3 = ((bf16[4,256,128]{2,1,0:T(8,128)(2,1)}), bf16[4,256,128]{2,1,0:T(8,128)(2,1)S(1)}, u32[]{:S(2)}, u32[]{:S(2)}) async-start(bf16[4,256,128]{2,1,0:T(8,128)(2,1)} %bitcast.22), calls=%async_computation.3 | async-start | bytes 524288 | tf_op jit(solution)/shard_map/all_to_all | solution.py:667
  189.3 15.8 %collective-permute-start.6 = (bf16[4,256,512]{2,1,0:T(8,128)(2,1)}, bf16[4,256,512]{2,1,0:T(8,128)(2,1)}, u32[]{:S(2)}, u32[]{:S(2)}) collective-permute-start(bf16[4,256,512]{2,1,0:T(8,128)(2,1)} %slice.120), channel_id=1, source_target_pairs={{0,4},{4,0},{8,12},{12,8},{16,20},{20,16},{24,28},{28,24},{1,5},{5... | collective-permute-start | bytes 3145736 | tf_op jit(solution)/shard_map/ppermute | solution.py:51
  201.4 39.2 %collective-permute-start.9 = (bf16[4,256,512]{2,1,0:T(8,128)(2,1)S(1)}, bf16[4,256,512]{2,1,0:T(8,128)(2,1)S(1)}, u32[]{:S(2)}, u32[]{:S(2)}) collective-permute-start(bf16[4,256,512]{2,1,0:T(8,128)(2,1)S(1)} %slice.126), channel_id=1, source_target_pairs={{0,4},{4,0},{8,12},{12,8},{16,20},{20,16},{24,28},{28,24},{1,5},{5... | collective-permute-start | bytes 3145736 | tf_op jit(solution)/shard_map/ppermute | solution.py:51
  206.7 56.6 %collective-permute-start.7 = (bf16[2,256,512]{2,1,0:T(8,128)(2,1)S(1)}, bf16[2,256,512]{2,1,0:T(8,128)(2,1)S(1)}, u32[]{:S(2)}, u32[]{:S(2)}) collective-permute-start(bf16[2,256,512]{2,1,0:T(8,128)(2,1)S(1)} %slice.152), channel_id=1, source_target_pairs={{0,16},{4,20},{8,24},{12,28},{16,0},{20,4},{24,8},{28,12},{1,17},{... | collective-permute-start | bytes 1572872 | tf_op jit(solution)/shard_map/ppermute | solution.py:51
  240.9 29.8 %collective-permute-start.10 = (bf16[2,256,512]{2,1,0:T(8,128)(2,1)S(1)}, bf16[2,256,512]{2,1,0:T(8,128)(2,1)S(1)}, u32[]{:S(2)}, u32[]{:S(2)}) collective-permute-start(bf16[2,256,512]{2,1,0:T(8,128)(2,1)S(1)} %slice.156), channel_id=1, source_target_pairs={{0,8},{4,12},{8,0},{12,4},{16,24},{20,28},{24,16},{28,20},{1,9},{5... | collective-permute-start | bytes 1572872 | tf_op jit(solution)/shard_map/ppermute | solution.py:51
  264.2 13.2 %collective-permute-start.8 = (bf16[1,256,512]{2,1,0:T(8,128)(2,1)}, bf16[1,256,512]{2,1,0:T(8,128)(2,1)}, u32[]{:S(2)}, u32[]{:S(2)}) collective-permute-start(bf16[1,256,512]{2,1,0:T(8,128)(2,1)} %slice.154), channel_id=1, source_target_pairs={{0,8},{4,12},{8,0},{12,4},{16,24},{20,28},{24,16},{28,20},{1,9},{5... | collective-permute-start | bytes 786440 | tf_op jit(solution)/shard_map/ppermute | solution.py:51
  271.6 7.8 %collective-permute-start.11 = (bf16[1,256,512]{2,1,0:T(8,128)(2,1)S(1)}, bf16[1,256,512]{2,1,0:T(8,128)(2,1)S(1)}, u32[]{:S(2)}, u32[]{:S(2)}) collective-permute-start(bf16[1,256,512]{2,1,0:T(8,128)(2,1)S(1)} %slice.158), channel_id=1, source_target_pairs={{0,16},{4,20},{8,24},{12,28},{16,0},{20,4},{24,8},{28,12},{1,17},{... | collective-permute-start | bytes 786440 | tf_op jit(solution)/shard_map/ppermute | solution.py:51
  285.0 1.9 collective-permute-start.18
  287.2 7.1 %collective-permute-start.13 = (bf16[64,1024]{1,0:T(8,128)(2,1)S(1)}, bf16[64,1024]{1,0:T(8,128)(2,1)S(1)}, u32[]{:S(2)}, u32[]{:S(2)}) collective-permute-start(bf16[64,1024]{1,0:T(8,128)(2,1)S(1)} %broadcast_select_fusion.2), channel_id=1, source_target_pairs={{0,16},{4,20},{8,24},{12,28},{16,0},{20,4},{24,8},{28,12},{1,17},{... | collective-permute-start | bytes 393224 | tf_op jit(solution)/shard_map/ppermute | solution.py:51
  288.3 7.6 %collective-permute-start.19 = (bf16[64,1024]{1,0:T(8,128)(2,1)S(1)}, bf16[64,1024]{1,0:T(8,128)(2,1)S(1)}, u32[]{:S(2)}, u32[]{:S(2)}) collective-permute-start(bf16[64,1024]{1,0:T(8,128)(2,1)S(1)} %broadcast_select_fusion.3), channel_id=1, source_target_pairs={{0,8},{4,12},{8,0},{12,4},{16,24},{20,28},{24,16},{28,20},{1,9},{5... | collective-permute-start | bytes 393224 | tf_op jit(solution)/shard_map/ppermute | solution.py:51
  294.4 4.3 collective-permute-start.14
  296.0 4.3 collective-permute-start.20
  298.7 4.3 collective-permute-start.15
  300.3 8.0 %collective-permute-start.21 = (bf16[32,1024]{1,0:T(8,128)(2,1)S(1)}, bf16[32,1024]{1,0:T(8,128)(2,1)S(1)}, u32[]{:S(2)}, u32[]{:S(2)}) collective-permute-start(bf16[32,1024]{1,0:T(8,128)(2,1)S(1)} %add_convert_fusion.10), channel_id=1, source_target_pairs={{0,16},{4,20},{8,24},{12,28},{16,0},{20,4},{24,8},{28,12},{1,17},{... | collective-permute-start | bytes 196616 | tf_op jit(solution)/shard_map/ppermute | solution.py:51
  303.1 6.8 %collective-permute-start.16 = (bf16[64,1024]{1,0:T(8,128)(2,1)S(1)}, bf16[64,1024]{1,0:T(8,128)(2,1)S(1)}, u32[]{:S(2)}, u32[]{:S(2)}) collective-permute-start(bf16[64,1024]{1,0:T(8,128)(2,1)S(1)} %maximum_select_fusion.4), channel_id=1, source_target_pairs={{0,16},{4,20},{8,24},{12,28},{16,0},{20,4},{24,8},{28,12},{1,17},{... | collective-permute-start | bytes 393224 | tf_op jit(solution)/shard_map/ppermute | solution.py:51
  303.5 44.1 %all-to-all-start.4 = ((bf16[4,512,256]{2,1,0:T(8,128)(2,1)}), bf16[4,512,256]{2,1,0:T(8,128)(2,1)S(1)}, u32[]{:S(2)}, u32[]{:S(2)}) async-start(bf16[4,512,256]{2,1,0:T(8,128)(2,1)} %copy-done.14), calls=%async_computation.4 | async-start | bytes 2097152 | tf_op jit(solution)/shard_map/all_to_all | solution.py:667
  308.3 6.9 %collective-permute-start.22 = (bf16[64,1024]{1,0:T(8,128)(2,1)S(1)}, bf16[64,1024]{1,0:T(8,128)(2,1)S(1)}, u32[]{:S(2)}, u32[]{:S(2)}) collective-permute-start(bf16[64,1024]{1,0:T(8,128)(2,1)S(1)} %maximum_select_fusion.5), channel_id=1, source_target_pairs={{0,8},{4,12},{8,0},{12,4},{16,24},{20,28},{24,16},{28,20},{1,9},{5... | collective-permute-start | bytes 393224 | tf_op jit(solution)/shard_map/ppermute | solution.py:51
  309.9 11.7 %collective-permute-start.17 = (bf16[128,1024]{1,0:T(8,128)(2,1)S(1)}, bf16[128,1024]{1,0:T(8,128)(2,1)S(1)}, u32[]{:S(2)}, u32[]{:S(2)}) collective-permute-start(bf16[128,1024]{1,0:T(8,128)(2,1)S(1)} %maximum_select_fusion.2), channel_id=1, source_target_pairs={{0,4},{4,0},{8,12},{12,8},{16,20},{20,16},{24,28},{28,24},{1,5},{5... | collective-permute-start | bytes 786440 | tf_op jit(solution)/shard_map/ppermute | solution.py:51
  315.3 6.5 %collective-permute-start.23 = (bf16[128,1024]{1,0:T(8,128)(2,1)S(1)}, bf16[128,1024]{1,0:T(8,128)(2,1)S(1)}, u32[]{:S(2)}, u32[]{:S(2)}) collective-permute-start(bf16[128,1024]{1,0:T(8,128)(2,1)S(1)} %maximum_select_fusion.3), channel_id=1, source_target_pairs={{0,4},{4,0},{8,12},{12,8},{16,20},{20,16},{24,28},{28,24},{1,5},{5... | collective-permute-start | bytes 786440 | tf_op jit(solution)/shard_map/ppermute | solution.py:51
  (44 other events, 286.7 us)
Sparse Core Ops, SparseCore 0:
  10.8 48.6 all-gather.5
  62.9 58.6 all-gather.7
  124.7 62.3 all-gather.9
  194.0 271.7 all-reduce.3

commit v3 on v2

--- a/solution.py
+++ b/solution.py
@@ -51,9 +51,11 @@
     return lax.ppermute(value, axis, [(source, source ^ mask) for source in range(count)])
 
 
-def spread_seq(value, order):
+def spread_seq(value, order, other):
     held = value[None]
     for bit in order:
+        if bit == order[-1]:
+            held = behind(held, other)
         held = jnp.concatenate([held, swap(held, "seq", bit)], axis=0)
     return held
 
@@ -85,6 +87,26 @@
             jnp.concatenate([held, came], axis=0),
         )
     return held
+
+
+def behind(value, other):
+    return value if other is None else lax.optimization_barrier((value, other))[0]
+
+
+def cut(value, index, size):
+    return lax.dynamic_slice_in_dim(value, index * size, size, 0)
+
+
+def sum_over(value, axis):
+    mask = 1
+    while mask < lax.axis_size(axis):
+        value = value + swap(value, axis, mask)
+        mask *= 2
+    return value
+
+
+def added(first, second):
+    return (first.astype(f32) + second.astype(f32)).astype(bf16)
 
 
 def qkv_kernel(w_ref, n_ref, cos_ref, sin_ref, q_ref, kv_ref, *, query_heads, key_heads, scale):
@@ -134,7 +156,7 @@
             jax.ShapeDtypeStruct((q_cols, count), bf16),
             jax.ShapeDtypeStruct((kv_cols, count), bf16),
         ],
-        compiler_params=pltpu.CompilerParams(vmem_limit_bytes=32 * 2**20),
+        compiler_params=pltpu.CompilerParams(vmem_limit_bytes=60 * 2**20),
         cost_estimate=pl.CostEstimate(
             flops=2 * cols * width * count, bytes_accessed=4 * count * width, transcendentals=0
         ),
@@ -366,24 +388,27 @@
     )(meta, q_t, do_parts, o_t, lse, kv_all, starts, cosine, sine)
 
 
-def experts_kernel(*refs, row_count, experts):
-    heads = refs[:row_count]
+def experts_kernel(core_ref, *refs, experts):
     (
-        x_ref, dy_ref, mix_ref, gain_ref, w_out_ref, gate_ref, up_ref, down_ref
-    ) = refs[row_count : row_count + 8]
-    outs = refs[row_count + 8 :]
-    out_ref, dh_ref, ggate_ref, gup_ref, gdown_ref, gout_ref = outs[:6]
-    d_heads = outs[6 : 6 + row_count]
-    hid_s, hat_s, recip_s, norm_s, norm_t_s, acc_s, dn_s = outs[6 + row_count :]
+        heads_ref, x_ref, dy_ref, mix_ref, gain_ref, own_ref, other_ref, gate_ref, up_ref, down_ref
+    ) = refs[:10]
+    outs = refs[10:]
+    row_count, part = heads_ref.shape[1], heads_ref.shape[3]
+    out_ref, dh_ref, ggate_ref, gup_ref, send_out, keep_out, gain_grad_ref = outs[:7]
+    d_heads = outs[7 : 7 + row_count]
+    hid_s, hat_s, recip_s, norm_s, norm_t_s, acc_s, dn_s, w_out_s = outs[7 + row_count :]
     expert = pl.program_id(0)
-    part = heads[0].shape[1]
     width = x_ref.shape[1]
 
     @pl.when(expert == 0)
     def _():
+        for device in range(own_ref.shape[0]):
+            w_out_s[device, core_ref[0]] = own_ref[device]
+            w_out_s[device, 1 - core_ref[0]] = other_ref[device]
+        w_out = w_out_s[...].reshape(-1, width)
         for row in range(row_count):
             at = slice(part * row, part * (row + 1))
-            branch = mm(heads[row][...].T, w_out_ref[...])
+            branch = mm(heads_ref[:, row].reshape(-1, part).T, w_out)
             hidden = x_ref[at, :].astype(f32) + branch
             recip = lax.rsqrt(jnp.mean(hidden * hidden, axis=-1, keepdims=True) + epsilon)
             hat = hidden * recip
@@ -408,7 +433,17 @@
     d_gate = (d_hid * up_pre * (gate_sig * (1.0 + gate_pre * (1.0 - gate_sig)))).astype(bf16)
     d_up = (d_hid * gate_act).astype(bf16)
     dn_s[...] += mm(d_gate, gate_ref[0], NT) + mm(d_up, up_ref[0], NT)
-    gdown_ref[0] = mm(hid.T, d_expert).astype(bf16)
+    grad_down = mm(hid.T, d_expert).astype(bf16)
+    half = experts // 2
+
+    @pl.when(expert < half)
+    def _():
+        send_out[expert] = grad_down
+
+    @pl.when(expert >= half)
+    def _():
+        keep_out[expert - half] = grad_down
+
     ggate_ref[0] = mm(norm_t_s[...], d_gate).astype(bf16)
     gup_ref[0] = mm(norm_t_s[...], d_up).astype(bf16)
 
@@ -417,10 +452,8 @@
         out_ref[...] = acc_s[...].astype(bf16)
         hat = hat_s[...]
         d_norm = dn_s[...]
-        head_cols = w_out_ref.shape[0]
-        gout_ref[head_cols:, :] = jnp.broadcast_to(
-            jnp.sum(d_norm * hat, axis=0, keepdims=True), (16, width)
-        ).astype(bf16)
+        w_out = w_out_s[...].reshape(-1, width)
+        gain_grad_ref[...] = jnp.sum(d_norm * hat, axis=0, keepdims=True)
         d_hat = d_norm * gain_ref[...]
         mean = jnp.mean(d_hat * hat, axis=-1, keepdims=True)
         d_hidden = dy_ref[...].astype(f32) + recip_s[...] * (d_hat - hat * mean)
@@ -430,71 +463,105 @@
         for row in range(row_count):
             at = slice(part * row, part * (row + 1))
             piece = d_branch[at, :]
-            d_heads[row][...] = mm(w_out_ref[...], piece, NT).astype(bf16)
-            term = mm(heads[row][...], piece)
+            d_heads[row][...] = mm(w_out, piece, NT).astype(bf16)
+            term = mm(heads_ref[:, row].reshape(-1, part), piece)
             grad_out = term if grad_out is None else grad_out + term
-        gout_ref[0:head_cols, :] = grad_out.astype(bf16)
-
-
-def run_experts(heads, x_rows, dy_rows, mix, gain, w_out_all, w_gate, w_up, w_down):
+        grad_out = grad_out.astype(bf16)
+        part_rows = grad_out.shape[0] // (2 * (send_out.shape[0] - half))
+
+        @pl.when(core_ref[0] == 0)
+        def _():
+            for at in range(send_out.shape[0] - half):
+                keep_out[half + at] = grad_out[part_rows * at : part_rows * (at + 1)]
+                start = grad_out.shape[0] // 2 + part_rows * at
+                send_out[half + at] = grad_out[start : start + part_rows]
+
+        @pl.when(core_ref[0] != 0)
+        def _():
+            for at in range(send_out.shape[0] - half):
+                send_out[half + at] = grad_out[part_rows * at : part_rows * (at + 1)]
+                start = grad_out.shape[0] // 2 + part_rows * at
+                keep_out[half + at] = grad_out[start : start + part_rows]
+
+
+def run_experts(
+    core, heads, x_rows, dy_rows, mix, gain, w_out_half, w_out_other, w_gate, w_up, w_down
+):
     own, width = x_rows.shape
     experts, _, hidden = w_gate.shape
-    row_count = len(heads)
-    head_cols, part = heads[0].shape
+    kv_devices, row_count, _, part = heads.shape
+    half_rows = w_out_half.shape[1]
+    head_cols = 2 * kv_devices * half_rows
 
     def whole(shape):
-        return pl.BlockSpec(shape, lambda e: (0,) * len(shape))
-
-    gate_spec = pl.BlockSpec((1, width, hidden), lambda e: (e, 0, 0))
-    down_spec = pl.BlockSpec((1, hidden, width), lambda e: (e, 0, 0))
+        return pl.BlockSpec(shape, lambda e, m: (0,) * len(shape))
+
+    half = experts // 2
+
+    def which(e, m):
+        return lax.rem(e + (1 - m[0]) * half, experts)
+
+    gate_spec = pl.BlockSpec((1, width, hidden), lambda e, m: (which(e, m), 0, 0))
+    down_spec = pl.BlockSpec((1, hidden, width), lambda e, m: (which(e, m), 0, 0))
+    outer = (half + head_cols // (2 * hidden), hidden, width)
     return pl.pallas_call(
-        functools.partial(experts_kernel, row_count=row_count, experts=experts),
-        grid=(experts,),
-        in_specs=[whole((head_cols, part))] * row_count
-        + [
-            whole((own, width)),
-            whole((own, width)),
-            pl.BlockSpec((1, own, 1), lambda e: (e, 0, 0)),
-            whole((1, width)),
-            whole((head_cols, width)),
-            gate_spec,
-            gate_spec,
-            down_spec,
-        ],
-        out_specs=[
-            whole((own, width)),
-            whole((own, width)),
-            gate_spec,
-            gate_spec,
-            down_spec,
-            whole((head_cols + 16, width)),
-        ]
-        + [whole((head_cols, part))] * row_count,
+        functools.partial(experts_kernel, experts=experts),
+        grid_spec=pltpu.PrefetchScalarGridSpec(
+            num_scalar_prefetch=1,
+            grid=(experts,),
+            in_specs=[
+                whole(heads.shape),
+                whole((own, width)),
+                whole((own, width)),
+                pl.BlockSpec((1, own, 1), lambda e, m: (which(e, m), 0, 0)),
+                whole((1, width)),
+                whole(w_out_half.shape),
+                whole(w_out_half.shape),
+                gate_spec,
+                gate_spec,
+                down_spec,
+            ],
+            out_specs=[
+                whole((own, width)),
+                whole((own, width)),
+                gate_spec,
+                gate_spec,
+                whole(outer),
+                whole(outer),
+                whole((1, width)),
+            ]
+            + [whole((head_cols, part))] * row_count,
+            scratch_shapes=[
+                pltpu.VMEM((own, width), f32),
+                pltpu.VMEM((own, width), f32),
+                pltpu.VMEM((own, 1), f32),
+                pltpu.VMEM((own, width), bf16),
+                pltpu.VMEM((width, own), bf16),
+                pltpu.VMEM((own, width), f32),
+                pltpu.VMEM((own, width), f32),
+                pltpu.VMEM((kv_devices, 2, half_rows, width), bf16),
+            ],
+        ),
         out_shape=[
             jax.ShapeDtypeStruct((own, width), bf16),
             jax.ShapeDtypeStruct((own, width), f32),
             jax.ShapeDtypeStruct(w_gate.shape, bf16),
             jax.ShapeDtypeStruct(w_up.shape, bf16),
-            jax.ShapeDtypeStruct(w_down.shape, bf16),
-            jax.ShapeDtypeStruct((head_cols + 16, width), bf16),
+            jax.ShapeDtypeStruct(outer, bf16),
+            jax.ShapeDtypeStruct(outer, bf16),
+            jax.ShapeDtypeStruct((1, width), f32),
         ]
         + [jax.ShapeDtypeStruct((head_cols, part), bf16)] * row_count,
-        scratch_shapes=[
-            pltpu.VMEM((own, width), f32),
-            pltpu.VMEM((own, width), f32),
-            pltpu.VMEM((own, 1), f32),
-            pltpu.VMEM((own, width), bf16),
-            pltpu.VMEM((width, own), bf16),
-            pltpu.VMEM((own, width), f32),
-            pltpu.VMEM((own, width), f32),
-        ],
         compiler_params=pltpu.CompilerParams(vmem_limit_bytes=56 * 2**20),
         cost_estimate=pl.CostEstimate(
             flops=18 * own * width * hidden * experts,
             bytes_accessed=6 * w_gate.size * 2,
             transcendentals=0,
         ),
-    )(*heads, x_rows, dy_rows, mix, gain, w_out_all, w_gate, w_up, w_down)
+    )(
+        core, heads, x_rows, dy_rows, mix, gain, w_out_half, w_out_other,
+        w_gate, w_up, w_down,
+    )
 
 
 def inner_kernel(*refs, row_count, query_cols, key_heads):
@@ -549,48 +616,80 @@
     )(*dq, *dkv, gathered, cosine, sine)
 
 
-def tokens_kernel(d_inner_ref, w_ref, x_ref, dh_ref, gain_ref, out_ref):
+def tokens_kernel(core_ref, d_inner_ref, own_ref, other_ref, x_ref, dh_ref, gain_ref, out_ref):
     x_float = x_ref[...].astype(f32)
     recip = lax.rsqrt(jnp.mean(x_float * x_float, axis=-1, keepdims=True) + epsilon)
     x_hat = x_float * recip
-    d_normed = mm(d_inner_ref[...].T, w_ref[...])
+    core = core_ref[0]
+    d_normed = None
+    for device in range(own_ref.shape[0]):
+        term = mm(d_inner_ref[device, core].T, own_ref[device])
+        term += mm(d_inner_ref[device, 1 - core].T, other_ref[device])
+        d_normed = term if d_normed is None else d_normed + term
     d_hat = d_normed * gain_ref[...]
     mean = jnp.mean(d_hat * x_hat, axis=-1, keepdims=True)
     out_ref[...] = (dh_ref[...] + recip * (d_hat - x_hat * mean)).astype(bf16)
 
 
-def token_grads(d_inner, w_all, x_rows, d_hidden, gain):
+def token_grads(core, d_inner, w_half, w_other, x_rows, d_hidden, gain):
     own, width = x_rows.shape
-    cols = d_inner.shape[0]
     return pl.pallas_call(
         tokens_kernel,
+        in_specs=[pl.BlockSpec(memory_space=pltpu.SMEM)]
+        + [pl.BlockSpec(memory_space=pltpu.VMEM)] * 6,
         out_shape=jax.ShapeDtypeStruct((own, width), bf16),
         compiler_params=pltpu.CompilerParams(vmem_limit_bytes=40 * 2**20),
         cost_estimate=pl.CostEstimate(
-            flops=2 * own * width * cols, bytes_accessed=2 * cols * width, transcendentals=0
-        ),
-    )(d_inner, w_all, x_rows, d_hidden, gain)
-
-
-def widen_kernel(*refs):
-    half = len(refs) // 2
-    for source, target in zip(refs[:half], refs[half:]):
-        target[...] = source[...].astype(f32)
-
-
-def widen(arrays):
-    specs = [pl.BlockSpec((1,) + a.shape[1:], lambda e: (e, 0, 0)) for a in arrays]
+            flops=4 * d_inner.size * width, bytes_accessed=4 * w_half.size, transcendentals=0
+        ),
+    )(core, d_inner, w_half, w_other, x_rows, d_hidden, gain)
+
+
+def widen_kernel(core_ref, gate_ref, up_ref, own_ref, other_ref, ggate_ref, gup_ref, gdown_ref, *, half):
+    ggate_ref[...] = gate_ref[...].astype(f32)
+    gup_ref[...] = up_ref[...].astype(f32)
+
+    @pl.when(pl.program_id(0) < half)
+    def _():
+        gdown_ref[...] = own_ref[...].astype(f32)
+
+    @pl.when(pl.program_id(0) >= half)
+    def _():
+        gdown_ref[...] = other_ref[...].astype(f32)
+
+
+def widen(core, grad_gate, grad_up, own_down, other_down):
+    experts, width, hidden = grad_gate.shape
+    half = experts // 2
+
+    def which(e, m):
+        return lax.rem(e + m[0] * half, experts)
+
+    gate_spec = pl.BlockSpec((1, width, hidden), lambda e, m: (which(e, m), 0, 0))
+    down_spec = pl.BlockSpec((1, hidden, width), lambda e, m: (which(e, m), 0, 0))
     return pl.pallas_call(
-        widen_kernel,
-        grid=(arrays[0].shape[0],),
-        in_specs=specs,
-        out_specs=specs,
-        out_shape=[jax.ShapeDtypeStruct(a.shape, f32) for a in arrays],
-        compiler_params=pltpu.CompilerParams(vmem_limit_bytes=40 * 2**20),
+        functools.partial(widen_kernel, half=half),
+        grid_spec=pltpu.PrefetchScalarGridSpec(
+            num_scalar_prefetch=1,
+            grid=(experts,),
+            in_specs=[
+                gate_spec,
+                gate_spec,
+                pl.BlockSpec((1, hidden, width), lambda e, m: (jnp.minimum(e, half - 1), 0, 0)),
+                pl.BlockSpec((1, hidden, width), lambda e, m: (jnp.maximum(e - half, 0), 0, 0)),
+            ],
+            out_specs=[gate_spec, gate_spec, down_spec],
+        ),
+        out_shape=[
+            jax.ShapeDtypeStruct(grad_gate.shape, f32),
+            jax.ShapeDtypeStruct(grad_gate.shape, f32),
+            jax.ShapeDtypeStruct((experts, hidden, width), f32),
+        ],
+        compiler_params=pltpu.CompilerParams(vmem_limit_bytes=60 * 2**20),
         cost_estimate=pl.CostEstimate(
-            flops=0, bytes_accessed=6 * sum(a.size for a in arrays), transcendentals=0
-        ),
-    )(*arrays)
+            flops=0, bytes_accessed=18 * grad_gate.size, transcendentals=0
+        ),
+    )(core, grad_gate, grad_up, own_down, other_down)
 
 
 def per_device(
@@ -647,88 +746,132 @@
     expert_ids = jnp.arange(expert_count, dtype=jnp.int32)
     picks = routes[..., None] == expert_ids
     local_load = jnp.sum(picks.astype(f32), axis=(0, 1, 2))
-    load_rows = jnp.pad(local_load.astype(bf16)[None, :], ((0, 15), (0, width - expert_count)))
-
-    def gather_rows(matrix, extra=None):
-        share = matrix.shape[0] // seq_devices
-        piece = lax.dynamic_slice_in_dim(matrix, seq_index * share, share, 0)
-        if extra is not None:
-            piece = jnp.concatenate([piece, extra], axis=0)
-        spread = lax.all_gather(piece, ("seq", "kv"))
-        spread = spread.reshape(seq_devices, kv_devices, piece.shape[0], width)
-        whole = spread[:, :, :share].transpose(1, 0, 2, 3)
-        return whole.reshape(kv_devices * matrix.shape[0], width), spread[:, :, share:]
-
-    w_out_all, loads = gather_rows(w_out, load_rows)
-    load_sum = jnp.sum(loads[:, :, 0, :expert_count].astype(f32), axis=(0, 1))
-    w_inner_all, _ = gather_rows(w_t)
+    core_index = seq_index % 2
+    half_rows = query_cols // 2
+    w_out_half = lax.all_gather(cut(w_out, core_index, half_rows), "kv")
+    w_out_other = swap(w_out_half, "seq", 1)
+    w_inner_half = lax.all_gather(cut(w_t, core_index, inner_cols // 2), "kv")
+    w_inner_other = swap(w_inner_half, "seq", 1)
 
     def exchange(value):
         return lax.all_to_all(value, "kv", 0, 0)
 
     q_t, kv_all, o_t, lse, heads = [], [], [], [], []
+    kv_t = []
     for row in rows:
         q_row, kv_row = project(row, w_t, gathered, cosine, sine, query_heads, key_heads)
         q_t.append(q_row)
-        kv_all.append(spread_seq(kv_row, orders[row]))
+        kv_t.append(kv_row)
+    kv_t = lax.optimization_barrier(kv_t)
+    kv_all = [spread_seq(kv_t[row], orders[row], None) for row in rows]
+    kv_all = lax.optimization_barrier(kv_all)
     for row in rows:
         o_row, low_row, lse_row = attend(
             row, meta, q_t[row], kv_all[row], starts3, group, orders[row]
         )
         o_t.append(o_row)
         lse.append(lse_row)
-        parts = low_row.reshape(query_cols, kv_devices, block_len).transpose(1, 0, 2)
-        heads.append(exchange(parts).reshape(kv_devices * query_cols, block_len))
+        heads.append(low_row.reshape(query_cols, kv_devices, block_len).transpose(1, 0, 2))
+    heads = exchange(jnp.stack(heads, axis=1))
 
     mix = jnp.sum(picks.astype(f32) * gate_weights[..., None], axis=2)
     mix = mix.reshape(own, expert_count).T[:, :, None]
     x_rows = tokens.reshape(own, width)
+    core = core_index.astype(jnp.int32)[None]
     outs = run_experts(
+        core,
         heads,
         x_rows,
         cotangent.reshape(own, width),
         mix,
         norm_second.reshape(1, width),
-        w_out_all,
+        w_out_half,
+        w_out_other,
         w_gate,
         w_up,
         w_down,
     )
-    block_out, d_hidden, grad_gate, grad_up, grad_down, grad_out = outs[:6]
-    d_heads = outs[6:]
-    grad_gate, grad_up, grad_down, grad_out = lax.psum(
-        (grad_gate, grad_up, grad_down, grad_out), ("seq", "kv")
+    block_out, d_hidden, grad_gate, grad_up, send_out, keep_out, second_part = outs[:7]
+    d_heads = outs[7:]
+    grad_gate, grad_up = lax.psum((grad_gate, grad_up), ("seq", "kv"))
+
+    chips = seq_devices // 2
+    groups = [[2 * chip + one for chip in range(chips)] for one in range(2)]
+
+    def over_chips(value):
+        return lax.all_to_all(value, "seq", 0, 0, axis_index_groups=groups)
+
+    def total(value):
+        return jnp.sum(value.astype(f32), axis=0).astype(bf16)
+
+    def copies(value, number):
+        return jnp.broadcast_to(value[None], (number,) + value.shape)
+
+    def rest(d_heads, d_hidden, send_out, keep_out, second_part):
+        do_parts = [exchange(d.reshape(kv_devices, query_cols, block_len)) for d in d_heads]
+        outer = added(keep_out, swap(send_out, "seq", 1)).reshape(chips, -1, width)
+        do_parts = [behind(do_part, outer) for do_part in do_parts]
+        outer = over_chips(outer)
+        dq, dkv = [], []
+        for row in rows:
+            dq_row, dkv_row = attend_back(
+                row, meta, q_t[row], do_parts[row], o_t[row], lse[row], kv_all[row], starts3,
+                cosine, sine, group, orders[row],
+            )
+            dq.append(dq_row)
+            dkv.append(collect_seq(dkv_row, orders[row]))
+        outer = total(behind(outer, dq[-1]))
+        rows_left = outer.shape[0]
+        outer = exchange(outer.reshape(kv_devices, rows_left // kv_devices, width))
+        outer = total(behind(outer, dkv[-1]))
+        dkv[-1] = behind(dkv[-1], outer)
+        outer = exchange(copies(outer, kv_devices)).reshape(rows_left, width)
+        d_parts, grad_inner_part = inner_grads(
+            dq, dkv, gathered, cosine, sine, kv_devices, key_heads
+        )
+        d_parts = exchange(d_parts).reshape(kv_devices, 2, inner_cols // 2, own)
+        half = inner_cols // 2
+        grad_inner = jnp.concatenate(
+            [
+                sum_seq(grad_inner_part[:half], seq_order(0, seq_devices)),
+                sum_seq(grad_inner_part[half:], seq_order(1, seq_devices)),
+            ],
+            axis=0,
+        ).astype(f32)
+        outer = copies(behind(outer, grad_inner), chips)
+        grad_inner, second_part, d_parts = behind((grad_inner, second_part, d_parts), outer)
+        outer = over_chips(outer)
+        sums = jnp.concatenate([second_part[0], local_load])
+        for axis in ("seq", "kv"):
+            sums = sum_over(sums, axis)
+        first_part = jnp.sum(w_t.astype(f32) * grad_inner, axis=0)
+        first_sum = sum_over(first_part, "kv") / norm_first
+        d_tokens = token_grads(
+            core, d_parts, w_inner_half, w_inner_other, x_rows, d_hidden, norm_first.reshape(1, width)
+        )
+        own_outer = behind(outer, (d_tokens, first_sum, sums)).reshape(keep_out.shape)
+        other_outer = swap(own_outer, "seq", 1)
+        kv_index = lax.axis_index("kv")
+        half_devices = kv_devices // 2
+        start = lax.rem(kv_index, half_devices) * query_cols
+        pieces = [
+            lax.dynamic_slice_in_dim(
+                pair[expert_count // 2 :].reshape(-1, width), start, query_cols, 0
+            )
+            for pair in (own_outer, other_outer)
+        ]
+        own_out = jnp.where(kv_index // half_devices == core_index, *pieces).astype(f32)
+        return d_tokens, grad_inner, first_sum, own_outer, other_outer, own_out, sums
+
+    operands = (d_heads, d_hidden, send_out, keep_out, second_part)
+    shapes = jax.eval_shape(rest, *operands)
+    d_tokens, grad_inner, first_sum, own_outer, other_outer, own_out, sums = lax.cond(
+        positions[0, 0] >= 0,
+        rest,
+        lambda *ignored: jax.tree.map(lambda leaf: jnp.zeros(leaf.shape, leaf.dtype), shapes),
+        *operands,
     )
-    second_sum = grad_out[kv_devices * query_cols]
-
-    do_parts = [exchange(d.reshape(kv_devices, query_cols, block_len)) for d in d_heads]
-    dq, dkv = [], []
-    for row in rows:
-        dq_row, dkv_row = attend_back(
-            row, meta, q_t[row], do_parts[row], o_t[row], lse[row], kv_all[row], starts3,
-            cosine, sine, group, orders[row],
-        )
-        dq.append(dq_row)
-        dkv.append(collect_seq(dkv_row, orders[row]))
-    d_parts, grad_inner_part = inner_grads(
-        dq, dkv, gathered, cosine, sine, kv_devices, key_heads
-    )
-    d_inner = exchange(d_parts).reshape(kv_devices * inner_cols, own)
-    half = inner_cols // 2
-    grad_inner = jnp.concatenate(
-        [
-            sum_seq(grad_inner_part[:half], seq_order(0, seq_devices)),
-            sum_seq(grad_inner_part[half:], seq_order(1, seq_devices)),
-        ],
-        axis=0,
-    ).astype(f32)
-    first_part = jnp.sum(w_t.astype(f32) * grad_inner, axis=0)
-    first_sum = lax.psum(first_part, "kv") / norm_first
-    d_tokens = token_grads(d_inner, w_inner_all, x_rows, d_hidden, norm_first.reshape(1, width))
-    grad_gate, grad_up, grad_down = widen([grad_gate, grad_up, grad_down])
-    own_out = lax.dynamic_slice_in_dim(
-        grad_out, lax.axis_index("kv") * query_cols, query_cols, 0
-    ).astype(f32)
+    grad_gate, grad_up, grad_down = widen(core, grad_gate, grad_up, own_outer, other_outer)
     return (
         block_out.reshape(tokens.shape),
         d_tokens.reshape(tokens.shape),
@@ -737,11 +880,11 @@
         grad_inner[query_cols : query_cols + key_cols].T,
         grad_inner[query_cols + key_cols :].T,
         own_out,
-        second_sum.astype(f32),
+        sums[:width],
         grad_gate,
         grad_up,
         grad_down,
-        load_sum.astype(jnp.int32),
+        sums[width:].astype(jnp.int32),
     )
 
 

time: 493 us -> 481 us (0.976); the launches traced: 491 us -> 473 us
  waiting for transfers between devices: 241 us -> 201 us
  local copies, waits for them, and re-layouts: 45.7 us -> 19.7 us
  starting transfers between devices: 101 us -> 121 us
  Pallas kernels: 51.6 us -> 66.3 us
  other arithmetic: 23.2 us -> 34.7 us
    psum x1, waiting for transfers between devices: 114 us -> 0.01 us  [per_device(): grad_gate, grad_up = lax.psum((grad_gate, grad_up), ('seq', 'kv'))]
    all_to_all x5, waiting for transfers between devices: 20.3 us -> 75.1 us  [exchange(): return lax.all_to_all(value, 'kv', 0, 0)]
    unnamed x93 -> x39, local copies, waits for them, and re-layouts: 30.1 us -> 1.72 us
    all_to_all x0 -> x2, starting transfers between devices: none -> 20.4 us  [over_chips(): return lax.all_to_all(value, 'seq', 0, 0, axis_index_groups=groups)]
    ppermute x24 -> x35, waiting for transfers between devices: 60.4 us -> 75.9 us  [swap(): lax.ppermute(value, axis, [(source, source ^ mask) for source in range(co...]
    all_to_all x0 -> x1, blocking collectives: none -> 14.6 us  [exchange(): return lax.all_to_all(value, 'kv', 0, 0)]
    psum x1 -> x0, blocking collectives: 13.8 us -> none  [per_device(): first_sum = lax.psum(first_part, 'kv') / norm_first]
    pallas_call x3, Pallas kernels: 32.8 us -> 40.5 us  [the longest x1 23.7 us: run_experts(): pl.pallas_call(functools.partial(experts_kernel, experts=experts), grid_s...]
  transfers between devices with their start and end apart: 33 -> 46, of which waited for: 18 -> 25; matrix products, arithmetic and copies ran while one was open for 8% -> 10% of each run, Pallas kernels for 9% -> 10%
where the time goes in v3:
time: 481 us; the launch traced here: 473 us
  waiting for transfers between devices  201 us (42%)
  starting transfers between devices  121 us (25%)
  Pallas kernels  66.3 us (14%)
  other arithmetic  34.7 us (7%)
  local copies, waits for them, and re-layouts  19.7 us (4%)
  between operations  15.3 us (3%)
  blocking collectives  14.6 us (3%)
    ppermute x35, starting transfers between devices, swap(): lax.ppermute(value, axis, [(source, source ^ mask) for source in range(co...  82.1 us
    ppermute x35, waiting for transfers between devices, swap(): lax.ppermute(value, axis, [(source, source ^ mask) for source in range(co...  75.9 us
    all_to_all x5, waiting for transfers between devices, exchange(): return lax.all_to_all(value, 'kv', 0, 0)  75.1 us
    all_gather x1, waiting for transfers between devices, per_device(): gathered = lax.all_gather(normed, 'kv', axis=1, tiled=True)  47.5 us
    pallas_call x1, Pallas kernels, run_experts(): pl.pallas_call(functools.partial(experts_kernel, experts=experts), grid_s...  23.7 us
    all_to_all x2, starting transfers between devices, over_chips(): return lax.all_to_all(value, 'seq', 0, 0, axis_index_groups=groups)  20.4 us
    all_to_all x5, starting transfers between devices, exchange(): return lax.all_to_all(value, 'kv', 0, 0)  18.4 us
    all_to_all x1, blocking collectives, exchange(): return lax.all_to_all(value, 'kv', 0, 0)  14.6 us
  transfers between devices with their start and end apart: 46, of which 25 were waited for; matrix products, arithmetic and copies ran while one was open for 10% of the time, Pallas kernels for 10%

profile of v3, /device:TPU:0, one launch (start us, length us, event | category | flops | bytes accessed | tf_op | source)
XLA Modules:
  0.0 473.2 jit_solution(9222098713738380414)
XLA Ops:
  12.0 47.5 %all-gather.6.cloned.1.call-done.n_ref = bf16[2,512,1024]{2,1,0:T(8,128)(2,1)} async-done(((bf16[2,128,1024]{2,1,0:T(8,128)(2,1)}), bf16[2,512,1024]{2,1,0:T(8,128)(2,1)}) %all-gather.6.cloned.1.call-update) | async-done | bytes 2097168 | tf_op jit(solution)/shard_map/all_gather | solution.py:742
  68.6 4.2 collective-permute-done.30
  77.0 9.4 %collective-permute-done.31 = bf16[2,256,512]{2,1,0:T(8,128)(2,1)S(1)} collective-permute-done((bf16[2,256,512]{2,1,0:T(8,128)(2,1)S(1)}, bf16[2,256,512]{2,1,0:T(8,128)(2,1)S(1)}, u32[]{:S(2)}, u32[]{:S(2)}) %collective-permute-start.31) | collective-permute-done | bytes 524320 | tf_op jit(solution)/shard_map/ppermute | solution.py:51
  96.7 3.5 shard_map.231
  100.2 3.5 shard_map.232
  105.1 3.5 all-to-all-start.7
  109.9 26.9 %all-to-all-done.7.refs_0_ = bf16[4,2,256,128]{3,2,1,0:T(8,128)(2,1)S(1)} async-done(((bf16[4,2,256,128]{3,2,1,0:T(8,128)(2,1)}), bf16[4,2,256,128]{3,2,1,0:T(8,128)(2,1)S(1)}, u32[]{:S(2)}, u32[]{:S(2)}) %all-to-all-start.7) | async-done | bytes 524320 | tf_op jit(solution)/shard_map/all_to_all | solution.py:757
  137.6 23.7 %shard_map.233 = (bf16[256,1024]{1,0:T(8,128)(2,1)}, f32[256,1024]{1,0:T(8,128)}, bf16[4,1024,512]{2,1,0:T(8,128)(2,1)}, bf16[4,1024,512]{2,1,0:T(8,128)(2,1)}, ...) custom-call(s32[1]{0:T(128)} %bitcast.14.core_ref, ...), custom_call_target="tpu_custom_call" | custom-call | flops 9663676416 | bytes 25165824 | tf_op jit(solution)/shard_map/pallas_call | solution.py:507
  168.7 279.3 %conditional.1 = (f32[512,1024]{1,0:T(8,128)}, f32[1024]{0:T(1024)S(1)}, bf16[3,512,1024]{2,1,0:T(8,128)(2,1)}, bf16[3,512,1024]{2,1,0:T(8,128)(2,1)}, f32[256,1...) conditional(s32[]{:T(128)} %bitcast.35, () %tuple.30, (bf16[1024,128]{1,0:T(8,128)(2,1)}, ...), branch_computations={%region_2.3_spmd, %region_3.8_spmd} | conditional | flops 24726388736 | bytes 196098784 | solution.py:868
  169.0 14.6 %all_to_all.33.do_ref = bf16[4,256,128]{2,1,0:T(8,128)(2,1)S(1)} all-to-all(bf16[4,256,128]{2,1,0:T(8,128)(2,1)S(1)} %bitcast.71), channel_id=1, replica_groups=mesh['seq'=8,'kv'=4] {'kv'}, dimensions={0} | all-to-all | bytes 524288 | tf_op jit(solution)/shard_map/cond/branch_1_fun/all_to_all | solution.py:757
  183.7 3.4 all-to-all-start
  187.1 6.3 %add_convert_fusion = bf16[3,512,1024]{2,1,0:T(8,128)(2,1)} fusion(bf16[3,512,1024]{2,1,0:T(8,128)(2,1)} %collective-permute-done, bf16[3,512,1024]{2,1,0:T(8,128)(2,1)} %get-tuple-element.60), kind=kLoop, calls=%fused_computation | loop fusion | flops 6291456 | bytes 9437184 | tf_op jit(solution)/shard_map/cond/branch_1_fun/convert_element_type | solution.py:109
  193.4 4.6 all-to-all-done.do_ref
  198.0 15.6 %all-to-all-start.2 = ((bf16[4,384,1024]{2,1,0:T(8,128)(2,1)}), bf16[4,384,1024]{2,1,0:T(8,128)(2,1)}, u32[]{:S(2)}, u32[]{:S(2)}) async-start(bf16[4,384,1024]{2,1,0:T(8,128)(2,1)} %bitcast.51), calls=%async_computation.2 | async-start | bytes 6291456 | tf_op jit(solution)/shard_map/cond/branch_1_fun/all_to_all | solution.py:802
  213.6 5.8 %branch_1_fun.5 = (bf16[256,512]{1,0:T(8,128)(2,1)S(1)}, bf16[8,256,512]{2,1,0:T(8,128)(2,1)S(1)}) custom-call(s32[5]{0:T(128)S(1)} %get-tuple-element.57.meta_ref, bf16[256,512]{1,0:T(8,128)(2,1)S(1)} %get-tuple-element.70.q_ref, bf16[4,256,128]{2,1,0:T(8,128)(2,1)S(1)} %all_to_all.33.do_ref, f32[256,512]{1,0:T(8,128)S(1)} %copy-done.31, ...), custom_call_target="tpu_custom_call" | custom-call | flops 10737418240 | bytes 4194304 | tf_op jit(solution)/shard_map/cond/branch_1_fun/pallas_call | solution.py:352
  221.1 4.7 branch_1_fun.4
  225.9 4.8 %collective-permute-start.1 = (bf16[4,256,512]{2,1,0:T(8,128)(2,1)S(1)}, bf16[4,256,512]{2,1,0:T(8,128)(2,1)S(1)}, u32[]{:S(2)}, u32[]{:S(2)}) collective-permute-start(bf16[4,256,512]{2,1,0:T(8,128)(2,1)S(1)} %slice.25), channel_id=1, source_target_pairs={{0,4},{4,0},{8,12},{12,8},{16,20},{20,16},{24,28},{28,24},{1,5},{5... | collective-permute-start | bytes 3145736 | tf_op jit(solution)/shard_map/cond/branch_1_fun/ppermute | solution.py:51
  231.0 8.9 %collective-permute-start.5 = (bf16[2,256,512]{2,1,0:T(8,128)(2,1)S(1)}, bf16[2,256,512]{2,1,0:T(8,128)(2,1)}, u32[]{:S(2)}, u32[]{:S(2)}) collective-permute-start(bf16[2,256,512]{2,1,0:T(8,128)(2,1)S(1)} %slice.133), channel_id=1, source_target_pairs={{0,8},{4,12},{8,0},{12,4},{16,24},{20,28},{24,16},{28,20},{1,9},{5... | collective-permute-start | bytes 1572872 | tf_op jit(solution)/shard_map/cond/branch_1_fun/ppermute | solution.py:51
  242.0 31.6 %collective-permute-start.2 = (bf16[2,256,512]{2,1,0:T(8,128)(2,1)}, bf16[2,256,512]{2,1,0:T(8,128)(2,1)}, u32[]{:S(2)}, u32[]{:S(2)}) collective-permute-start(bf16[2,256,512]{2,1,0:T(8,128)(2,1)} %slice.129), channel_id=1, source_target_pairs={{0,16},{4,20},{8,24},{12,28},{16,0},{20,4},{24,8},{28,12},{1,17},{... | collective-permute-start | bytes 1572872 | tf_op jit(solution)/shard_map/cond/branch_1_fun/ppermute | solution.py:51
  273.6 3.7 reduce_sum.55
  277.2 4.4 all-to-all-start.3
  288.1 3.5 collective-permute-start.3
  296.7 9.3 %all-to-all-done.3 = bf16[4,96,1024]{2,1,0:T(8,128)(2,1)} async-done(((bf16[4,96,1024]{2,1,0:T(8,128)(2,1)}), bf16[4,96,1024]{2,1,0:T(8,128)(2,1)}, u32[]{:S(2)}, u32[]{:S(2)}) %all-to-all-start.3) | async-done | bytes 786464 | tf_op jit(solution)/shard_map/cond/branch_1_fun/all_to_all | solution.py:757
  312.6 3.5 all-to-all-start.5
  326.3 16.3 %all-to-all-done.5 = bf16[4,96,1024]{2,1,0:T(8,128)(2,1)S(1)} async-done(((bf16[4,96,1024]{2,1,0:T(8,128)(2,1)}), bf16[4,96,1024]{2,1,0:T(8,128)(2,1)S(1)}, u32[]{:S(2)}, u32[]{:S(2)}) %all-to-all-start.5) | async-done | bytes 786464 | tf_op jit(solution)/shard_map/cond/branch_1_fun/all_to_all | solution.py:757
  342.6 3.5 all-to-all-start.4
  364.8 17.9 %all-to-all-done.4 = bf16[4,512,256]{2,1,0:T(8,128)(2,1)S(1)} async-done(((bf16[4,512,256]{2,1,0:T(8,128)(2,1)}), bf16[4,512,256]{2,1,0:T(8,128)(2,1)S(1)}, u32[]{:S(2)}, u32[]{:S(2)}) %all-to-all-start.4) | async-done | bytes 1048608 | tf_op jit(solution)/shard_map/cond/branch_1_fun/all_to_all | solution.py:757
  384.8 4.8 %all-to-all-start.6 = ((bf16[4,384,1024]{2,1,0:T(8,128)(2,1)}), bf16[4,384,1024]{2,1,0:T(8,128)(2,1)}, u32[]{:S(2)}, u32[]{:S(2)}) async-start(bf16[4,384,1024]{2,1,0:T(8,128)(2,1)} %broadcast_in_dim.1), calls=%async_computation.6 | async-start | bytes 6291456 | tf_op jit(solution)/shard_map/cond/branch_1_fun/all_to_all | solution.py:802
  397.7 27.0 %collective-permute-done.22 = f32[1028]{0:T(1024)S(1)} collective-permute-done((f32[1028]{0:T(1024)S(1)}, f32[1028]{0:T(1024)S(1)}, u32[]{:S(2)}, u32[]{:S(2)}) %collective-permute-start.22) | collective-permute-done | bytes 4144 | tf_op jit(solution)/shard_map/cond/branch_1_fun/ppermute | solution.py:51
  431.5 4.1 branch_1_fun.7
  441.5 4.7 collective-permute-done.26
  453.5 12.6 %shard_map.234 = (f32[4,1024,512]{2,1,0:T(8,128)}, f32[4,1024,512]{2,1,0:T(8,128)}, f32[4,512,1024]{2,1,0:T(8,128)}) custom-call(s32[1]{0:T(128)} %bitcast.14.core_ref, bf16[4,1024,512]{2,1,0:T(8,128)(2,1)} %get-tuple-element.178.gate_ref, bf16[4,1024,512]{2,1,0:T(8,128)(2,1)} %get-tuple-element.179.up_ref, ...), custom_call_target="tpu_custom_call" | custom-call | bytes 37748736 | tf_op jit(solution)/shard_map/pallas_call | solution.py:670
  (225 shorter events, 119.4 us)
Async XLA Ops:
  7.2 52.2 %all-gather.6.cloned.1.call-start = ((), (), s32[]{:S(2)}) async-start(), calls=%async_computation.8 | async-start | bytes 2621440 | tf_op jit(solution)/shard_map/all_gather | solution.py:742
  10.7 82.3 %all-gather.8.cloned.1.call-start = ((), (), s32[]{:S(2)}) async-start(), calls=%async_computation.9 | async-start | bytes 1310720 | tf_op jit(solution)/shard_map/all_gather | solution.py:751
  64.8 8.0 %collective-permute-start.30 = (bf16[1,256,512]{2,1,0:T(8,128)(2,1)S(1)}, bf16[1,256,512]{2,1,0:T(8,128)(2,1)S(1)}, u32[]{:S(2)}, u32[]{:S(2)}) collective-permute-start(bf16[1,256,512]{2,1,0:T(8,128)(2,1)S(1)} %bitcast.57), channel_id=1, source_target_pairs={{0,16},{4,20},{8,24},{12,28},{16,0},{20,4},{24,8},{28,12},{1,17},{... | collective-permute-start | bytes 786440 | tf_op jit(solution)/shard_map/ppermute | solution.py:51
  67.1 94.3 %all-gather.10.cloned.1.call-start = ((), (), s32[]{:S(2)}) async-start(), calls=%async_computation.10 | async-start | bytes 2621440 | tf_op jit(solution)/shard_map/all_gather | solution.py:753
  67.1 8.6 %collective-permute-start.27 = (bf16[1,256,512]{2,1,0:T(8,128)(2,1)}, bf16[1,256,512]{2,1,0:T(8,128)(2,1)S(1)}, u32[]{:S(2)}, u32[]{:S(2)}) collective-permute-start(bf16[1,256,512]{2,1,0:T(8,128)(2,1)} %bitcast.53), channel_id=1, source_target_pairs={{0,8},{4,12},{8,0},{12,4},{16,24},{20,28},{24,16},{28,20},{1,9},{5... | collective-permute-start | bytes 786440 | tf_op jit(solution)/shard_map/ppermute | solution.py:51
  72.9 13.5 %collective-permute-start.31 = (bf16[2,256,512]{2,1,0:T(8,128)(2,1)S(1)}, bf16[2,256,512]{2,1,0:T(8,128)(2,1)S(1)}, u32[]{:S(2)}, u32[]{:S(2)}) collective-permute-start(bf16[2,256,512]{2,1,0:T(8,128)(2,1)S(1)} %pad_maximum_fusion.7), channel_id=1, source_target_pairs={{0,8},{4,12},{8,0},{12,4},{16,24},{20,28},{24,16},{28,20},{1,9},{5... | collective-permute-start | bytes 1572872 | tf_op jit(solution)/shard_map/ppermute | solution.py:51
  76.7 11.9 %collective-permute-start.28 = (bf16[2,256,512]{2,1,0:T(8,128)(2,1)S(1)}, bf16[2,256,512]{2,1,0:T(8,128)(2,1)S(1)}, u32[]{:S(2)}, u32[]{:S(2)}) collective-permute-start(bf16[2,256,512]{2,1,0:T(8,128)(2,1)S(1)} %pad_maximum_fusion.6), channel_id=1, source_target_pairs={{0,16},{4,20},{8,24},{12,28},{16,0},{20,4},{24,8},{28,12},{1,17},{... | collective-permute-start | bytes 1572872 | tf_op jit(solution)/shard_map/ppermute | solution.py:51
  93.0 16.9 %collective-permute-start.33 = (bf16[4,128,1024]{2,1,0:T(8,128)(2,1)}, bf16[4,128,1024]{2,1,0:T(8,128)(2,1)}, u32[]{:S(2)}, u32[]{:S(2)}) collective-permute-start(bf16[4,128,1024]{2,1,0:T(8,128)(2,1)} %bitcast.78), channel_id=1, source_target_pairs={{0,4},{4,0},{8,12},{12,8},{16,20},{20,16},{24,28},{28,24},{1,5},{5... | collective-permute-start | bytes 3145736 | tf_op jit(solution)/shard_map/ppermute | solution.py:51
  105.1 31.7 %all-to-all-start.7 = ((bf16[4,2,256,128]{3,2,1,0:T(8,128)(2,1)}), bf16[4,2,256,128]{3,2,1,0:T(8,128)(2,1)S(1)}, u32[]{:S(2)}, u32[]{:S(2)}) async-start(bf16[4,2,256,128]{3,2,1,0:T(8,128)(2,1)} %pad_maximum_fusion.8), calls=%async_computation.7 | async-start | bytes 1048576 | tf_op jit(solution)/shard_map/all_to_all | solution.py:757
  108.6 344.9 %all-reduce.3.cloned.1.call-start = ((), (), s32[]{:S(2)}) async-start(), calls=%async_computation.11 | async-start | bytes 16777216 | tf_op jit(solution)/shard_map/psum | solution.py:796
  161.4 7.3 %collective-permute-start.34 = (bf16[4,256,1024]{2,1,0:T(8,128)(2,1)}, bf16[4,256,1024]{2,1,0:T(8,128)(2,1)S(1)}, u32[]{:S(2)}, u32[]{:S(2)}) collective-permute-start(bf16[4,256,1024]{2,1,0:T(8,128)(2,1)} %bitcast.76), channel_id=1, source_target_pairs={{0,4},{4,0},{8,12},{12,8},{16,20},{20,16},{24,28},{28,24},{1,5},{5... | collective-permute-start | bytes 6291464 | tf_op jit(solution)/shard_map/ppermute | solution.py:51
  168.7 18.4 %collective-permute-start = (bf16[3,512,1024]{2,1,0:T(8,128)(2,1)}, bf16[3,512,1024]{2,1,0:T(8,128)(2,1)}, u32[]{:S(2)}, u32[]{:S(2)}) collective-permute-start(bf16[3,512,1024]{2,1,0:T(8,128)(2,1)} %get-tuple-element.61), channel_id=1, source_target_pairs={{0,4},{4,0},{8,12},{12,8},{16,20},{20,16},{24,28},{28,24},{1,5},{5... | collective-permute-start | bytes 9437192 | tf_op jit(solution)/shard_map/cond/branch_1_fun/ppermute | solution.py:51
  183.7 14.4 %all-to-all-start = ((bf16[4,256,128]{2,1,0:T(8,128)(2,1)}), bf16[4,256,128]{2,1,0:T(8,128)(2,1)S(1)}, u32[]{:S(2)}, u32[]{:S(2)}) async-start(bf16[4,256,128]{2,1,0:T(8,128)(2,1)} %bitcast), calls=%async_computation | async-start | bytes 524288 | tf_op jit(solution)/shard_map/cond/branch_1_fun/all_to_all | solution.py:757
  198.0 75.6 %all-to-all-start.2 = ((bf16[4,384,1024]{2,1,0:T(8,128)(2,1)}), bf16[4,384,1024]{2,1,0:T(8,128)(2,1)}, u32[]{:S(2)}, u32[]{:S(2)}) async-start(bf16[4,384,1024]{2,1,0:T(8,128)(2,1)} %bitcast.51), calls=%async_computation.2 | async-start | bytes 6291456 | tf_op jit(solution)/shard_map/cond/branch_1_fun/all_to_all | solution.py:802
  219.5 11.2 %collective-permute-start.4 = (bf16[4,256,512]{2,1,0:T(8,128)(2,1)S(1)}, bf16[4,256,512]{2,1,0:T(8,128)(2,1)S(1)}, u32[]{:S(2)}, u32[]{:S(2)}) collective-permute-start(bf16[4,256,512]{2,1,0:T(8,128)(2,1)S(1)} %slice.85), channel_id=1, source_target_pairs={{0,4},{4,0},{8,12},{12,8},{16,20},{20,16},{24,28},{28,24},{1,5},{5... | collective-permute-start | bytes 3145736 | tf_op jit(solution)/shard_map/cond/branch_1_fun/ppermute | solution.py:51
  225.9 14.0 %collective-permute-start.1 = (bf16[4,256,512]{2,1,0:T(8,128)(2,1)S(1)}, bf16[4,256,512]{2,1,0:T(8,128)(2,1)S(1)}, u32[]{:S(2)}, u32[]{:S(2)}) collective-permute-start(bf16[4,256,512]{2,1,0:T(8,128)(2,1)S(1)} %slice.25), channel_id=1, source_target_pairs={{0,4},{4,0},{8,12},{12,8},{16,20},{20,16},{24,28},{28,24},{1,5},{5... | collective-permute-start | bytes 3145736 | tf_op jit(solution)/shard_map/cond/branch_1_fun/ppermute | solution.py:51
  231.0 50.7 %collective-permute-start.5 = (bf16[2,256,512]{2,1,0:T(8,128)(2,1)S(1)}, bf16[2,256,512]{2,1,0:T(8,128)(2,1)}, u32[]{:S(2)}, u32[]{:S(2)}) collective-permute-start(bf16[2,256,512]{2,1,0:T(8,128)(2,1)S(1)} %slice.133), channel_id=1, source_target_pairs={{0,8},{4,12},{8,0},{12,4},{16,24},{20,28},{24,16},{28,20},{1,9},{5... | collective-permute-start | bytes 1572872 | tf_op jit(solution)/shard_map/cond/branch_1_fun/ppermute | solution.py:51
  242.0 44.3 %collective-permute-start.2 = (bf16[2,256,512]{2,1,0:T(8,128)(2,1)}, bf16[2,256,512]{2,1,0:T(8,128)(2,1)}, u32[]{:S(2)}, u32[]{:S(2)}) collective-permute-start(bf16[2,256,512]{2,1,0:T(8,128)(2,1)} %slice.129), channel_id=1, source_target_pairs={{0,16},{4,20},{8,24},{12,28},{16,0},{20,4},{24,8},{28,12},{1,17},{... | collective-permute-start | bytes 1572872 | tf_op jit(solution)/shard_map/cond/branch_1_fun/ppermute | solution.py:51
  277.2 28.7 %all-to-all-start.3 = ((bf16[4,96,1024]{2,1,0:T(8,128)(2,1)}), bf16[4,96,1024]{2,1,0:T(8,128)(2,1)}, u32[]{:S(2)}, u32[]{:S(2)}) async-start(bf16[4,96,1024]{2,1,0:T(8,128)(2,1)} %bitcast.5), calls=%async_computation.3 | async-start | bytes 1572864 | tf_op jit(solution)/shard_map/cond/branch_1_fun/all_to_all | solution.py:757
  283.0 11.0 %collective-permute-start.6 = (bf16[1,256,512]{2,1,0:T(8,128)(2,1)S(1)}, bf16[1,256,512]{2,1,0:T(8,128)(2,1)S(1)}, u32[]{:S(2)}, u32[]{:S(2)}) collective-permute-start(bf16[1,256,512]{2,1,0:T(8,128)(2,1)S(1)} %slice.135), channel_id=1, source_target_pairs={{0,16},{4,20},{8,24},{12,28},{16,0},{20,4},{24,8},{28,12},{1,17},{... | collective-permute-start | bytes 786440 | tf_op jit(solution)/shard_map/cond/branch_1_fun/ppermute | solution.py:51
  288.1 8.5 %collective-permute-start.3 = (bf16[1,256,512]{2,1,0:T(8,128)(2,1)}, bf16[1,256,512]{2,1,0:T(8,128)(2,1)S(1)}, u32[]{:S(2)}, u32[]{:S(2)}) collective-permute-start(bf16[1,256,512]{2,1,0:T(8,128)(2,1)} %slice.131), channel_id=1, source_target_pairs={{0,8},{4,12},{8,0},{12,4},{16,24},{20,28},{24,16},{28,20},{1,9},{5... | collective-permute-start | bytes 786440 | tf_op jit(solution)/shard_map/cond/branch_1_fun/ppermute | solution.py:51
  312.6 30.0 %all-to-all-start.5 = ((bf16[4,96,1024]{2,1,0:T(8,128)(2,1)}), bf16[4,96,1024]{2,1,0:T(8,128)(2,1)S(1)}, u32[]{:S(2)}, u32[]{:S(2)}) async-start(bf16[4,96,1024]{2,1,0:T(8,128)(2,1)} %broadcast_in_dim.0), calls=%async_computation.5 | async-start | bytes 1572864 | tf_op jit(solution)/shard_map/cond/branch_1_fun/all_to_all | solution.py:757
  318.6 7.7 %collective-permute-start.14 = (bf16[64,1024]{1,0:T(8,128)(2,1)S(1)}, bf16[64,1024]{1,0:T(8,128)(2,1)S(1)}, u32[]{:S(2)}, u32[]{:S(2)}) collective-permute-start(bf16[64,1024]{1,0:T(8,128)(2,1)S(1)} %broadcast_select_fusion.3), channel_id=1, source_target_pairs={{0,8},{4,12},{8,0},{12,4},{16,24},{20,28},{24,16},{28,20},{1,9},{5... | collective-permute-start | bytes 393224 | tf_op jit(solution)/shard_map/cond/branch_1_fun/ppermute | solution.py:51
  323.7 22.6 %collective-permute-start.9 = (bf16[32,1024]{1,0:T(8,128)(2,1)S(1)}, bf16[32,1024]{1,0:T(8,128)(2,1)}, u32[]{:S(2)}, u32[]{:S(2)}) collective-permute-start(bf16[32,1024]{1,0:T(8,128)(2,1)S(1)} %broadcast_select_fusion.5), channel_id=1, source_target_pairs={{0,8},{4,12},{8,0},{12,4},{16,24},{20,28},{24,16},{28,20},{1,9},{5... | collective-permute-start | bytes 196616 | tf_op jit(solution)/shard_map/cond/branch_1_fun/ppermute | solution.py:51
  342.6 40.1 %all-to-all-start.4 = ((bf16[4,512,256]{2,1,0:T(8,128)(2,1)}), bf16[4,512,256]{2,1,0:T(8,128)(2,1)S(1)}, u32[]{:S(2)}, u32[]{:S(2)}) async-start(bf16[4,512,256]{2,1,0:T(8,128)(2,1)} %get-tuple-element.85), calls=%async_computation.4 | async-start | bytes 2097152 | tf_op jit(solution)/shard_map/cond/branch_1_fun/all_to_all | solution.py:757
  352.0 6.4 %collective-permute-start.11 = (bf16[64,1024]{1,0:T(8,128)(2,1)S(1)}, bf16[64,1024]{1,0:T(8,128)(2,1)S(1)}, u32[]{:S(2)}, u32[]{:S(2)}) collective-permute-start(bf16[64,1024]{1,0:T(8,128)(2,1)S(1)} %maximum_select_fusion.4), channel_id=1, source_target_pairs={{0,16},{4,20},{8,24},{12,28},{16,0},{20,4},{24,8},{28,12},{1,17},{... | collective-permute-start | bytes 393224 | tf_op jit(solution)/shard_map/cond/branch_1_fun/ppermute | solution.py:51
  384.8 55.4 %all-to-all-start.6 = ((bf16[4,384,1024]{2,1,0:T(8,128)(2,1)}), bf16[4,384,1024]{2,1,0:T(8,128)(2,1)}, u32[]{:S(2)}, u32[]{:S(2)}) async-start(bf16[4,384,1024]{2,1,0:T(8,128)(2,1)} %broadcast_in_dim.1), calls=%async_computation.6 | async-start | bytes 6291456 | tf_op jit(solution)/shard_map/cond/branch_1_fun/all_to_all | solution.py:802
  391.1 33.7 %collective-permute-start.22 = (f32[1028]{0:T(1024)S(1)}, f32[1028]{0:T(1024)S(1)}, u32[]{:S(2)}, u32[]{:S(2)}) collective-permute-start(f32[1028]{0:T(1024)S(1)} %fusion.2), channel_id=1, source_target_pairs={{0,8},{4,12},{8,0},{12,4},{16,24},{20,28},{24,16},{28,20},{1,9},{5... | collective-permute-start | bytes 12344 | tf_op jit(solution)/shard_map/cond/branch_1_fun/ppermute | solution.py:51
  395.6 29.1 %collective-permute-start.19 = (f32[1024]{0:T(1024)S(1)}, f32[1024]{0:T(1024)S(1)}, u32[]{:S(2)}, u32[]{:S(2)}) collective-permute-start(f32[1024]{0:T(1024)S(1)} %multiply_reduce_fusion), channel_id=1, source_target_pairs={{0,1},{1,0},{2,3},{3,2},{4,5},{5,4},{6,7},{7,6},{8,9},{9,8},{10,11... | collective-permute-start | bytes 12296 | tf_op jit(solution)/shard_map/cond/branch_1_fun/ppermute | solution.py:51
  424.8 11.6 %collective-permute-start.20 = (f32[1024]{0:T(1024)S(1)}, f32[1024]{0:T(1024)S(1)}, u32[]{:S(2)}, u32[]{:S(2)}) collective-permute-start(f32[1024]{0:T(1024)S(1)} %add.96), channel_id=1, source_target_pairs={{0,2},{1,3},{2,0},{3,1},{4,6},{5,7},{6,4},{7,5},{8,10},{9,11},{10,... | collective-permute-start | bytes 12296 | tf_op jit(solution)/shard_map/cond/branch_1_fun/ppermute | solution.py:51
  428.4 7.2 %collective-permute-start.24 = (f32[1028]{0:T(1024)S(1)}, f32[1028]{0:T(1024)S(1)}, u32[]{:S(2)}, u32[]{:S(2)}) collective-permute-start(f32[1028]{0:T(1024)S(1)} %add.100), channel_id=1, source_target_pairs={{0,1},{1,0},{2,3},{3,2},{4,5},{5,4},{6,7},{7,6},{8,9},{9,8},{10,11... | collective-permute-start | bytes 12344 | tf_op jit(solution)/shard_map/cond/branch_1_fun/ppermute | solution.py:51
  440.2 6.0 %collective-permute-start.26 = (bf16[3,512,1024]{2,1,0:T(8,128)(2,1)}, bf16[3,512,1024]{2,1,0:T(8,128)(2,1)}, u32[]{:S(2)}, u32[]{:S(2)}) collective-permute-start(bf16[3,512,1024]{2,1,0:T(8,128)(2,1)} %bitcast.10), channel_id=1, source_target_pairs={{0,4},{4,0},{8,12},{12,8},{16,20},{20,16},{24,28},{28,24},{1,5},{5... | collective-permute-start | bytes 9437192 | tf_op jit(solution)/shard_map/cond/branch_1_fun/ppermute | solution.py:51
  (46 other events, 486.3 us)
Sparse Core Ops, SparseCore 0:
  10.8 48.6 all-gather.5
  67.2 25.7 all-gather.7
  94.5 56.5 all-gather.9
  161.5 240.7 all-reduce.2

commit v4 on v3

--- a/solution.py
+++ b/solution.py
@@ -47,6 +47,8 @@
 
 
 def swap(value, axis, mask):
+    if mask == 0:
+        return value
     count = lax.axis_size(axis)
     return lax.ppermute(value, axis, [(source, source ^ mask) for source in range(count)])
 
@@ -69,7 +71,7 @@
     return held[0]
 
 
-def sum_seq(value, order):
+def halve_seq(value, order):
     index = lax.axis_index("seq")
     held = value
     for bit in order[::-1]:
@@ -78,6 +80,12 @@
         keep = jnp.where(upper, held[half:], held[:half])
         send = jnp.where(upper, held[:half], held[half:])
         held = (keep.astype(f32) + swap(send, "seq", bit).astype(f32)).astype(bf16)
+    return held
+
+
+def double_seq(value, order):
+    index = lax.axis_index("seq")
+    held = value
     for bit in order:
         upper = (index & bit) != 0
         came = swap(held, "seq", bit)
@@ -278,9 +286,9 @@
     start = start_ref[0]
     key_iota = lax.broadcasted_iota(jnp.int32, (span, span), 0)
     dkv_ref[...] = jnp.zeros(dkv_ref.shape, bf16)
-    part = do_ref.shape[2]
+    part = do_ref.shape[3]
     for device in range(do_ref.shape[0]):
-        do_t_s[:, part * device : part * (device + 1)] = do_ref[device]
+        do_t_s[:, part * device : part * (device + 1)] = do_ref[device, 0]
     for g in range(group):
         at = slice(DH * g, DH * g + DH)
         q_s[g] = q_ref[at, :].T
@@ -345,7 +353,7 @@
     blocks = kv_all.shape[0]
     key_heads = kv_all.shape[1] // (2 * DH)
     cols = group * DH
-    kv_devices, _, part = do_parts.shape
+    kv_devices, _, _, part = do_parts.shape
     head_spec = pl.BlockSpec((cols, span), lambda h, m: (h, 0))
     kv_spec = pl.BlockSpec((blocks, 2 * DH, span), lambda h, m: (0, h, 0))
     angle_spec = pl.BlockSpec((1, HALF, span), lambda h, m: (row, 0, 0))
@@ -358,7 +366,7 @@
             grid=(key_heads,),
             in_specs=[
                 head_spec,
-                pl.BlockSpec((kv_devices, cols, part), lambda h, m: (0, h, 0)),
+                pl.BlockSpec((kv_devices, 1, cols, part), lambda h, m: (0, row, h, 0)),
                 head_spec,
                 pl.BlockSpec((1, group, span), lambda h, m: (h, 0, 0)),
                 kv_spec,
@@ -395,8 +403,8 @@
     outs = refs[10:]
     row_count, part = heads_ref.shape[1], heads_ref.shape[3]
     out_ref, dh_ref, ggate_ref, gup_ref, send_out, keep_out, gain_grad_ref = outs[:7]
-    d_heads = outs[7 : 7 + row_count]
-    hid_s, hat_s, recip_s, norm_s, norm_t_s, acc_s, dn_s, w_out_s = outs[7 + row_count :]
+    d_heads_ref = outs[7]
+    hid_s, hat_s, recip_s, norm_s, norm_t_s, acc_s, dn_s, w_out_s = outs[8:]
     expert = pl.program_id(0)
     width = x_ref.shape[1]
 
@@ -463,7 +471,9 @@
         for row in range(row_count):
             at = slice(part * row, part * (row + 1))
             piece = d_branch[at, :]
-            d_heads[row][...] = mm(w_out, piece, NT).astype(bf16)
+            d_heads_ref[:, row] = (
+                mm(w_out, piece, NT).astype(bf16).reshape(d_heads_ref.shape[0], -1, part)
+            )
             term = mm(heads_ref[:, row].reshape(-1, part), piece)
             grad_out = term if grad_out is None else grad_out + term
         grad_out = grad_out.astype(bf16)
@@ -529,8 +539,8 @@
                 whole(outer),
                 whole(outer),
                 whole((1, width)),
-            ]
-            + [whole((head_cols, part))] * row_count,
+                whole(heads.shape),
+            ],
             scratch_shapes=[
                 pltpu.VMEM((own, width), f32),
                 pltpu.VMEM((own, width), f32),
@@ -550,8 +560,8 @@
             jax.ShapeDtypeStruct(outer, bf16),
             jax.ShapeDtypeStruct(outer, bf16),
             jax.ShapeDtypeStruct((1, width), f32),
-        ]
-        + [jax.ShapeDtypeStruct((head_cols, part), bf16)] * row_count,
+            jax.ShapeDtypeStruct(heads.shape, bf16),
+        ],
         compiler_params=pltpu.CompilerParams(vmem_limit_bytes=56 * 2**20),
         cost_estimate=pl.CostEstimate(
             flops=18 * own * width * hidden * experts,
@@ -616,33 +626,35 @@
     )(*dq, *dkv, gathered, cosine, sine)
 
 
-def tokens_kernel(core_ref, d_inner_ref, own_ref, other_ref, x_ref, dh_ref, gain_ref, out_ref):
+def tokens_kernel(place_ref, *refs):
+    own_ref, other_ref, x_ref, dh_ref, gain_ref, out_ref = refs[-6:]
     x_float = x_ref[...].astype(f32)
     recip = lax.rsqrt(jnp.mean(x_float * x_float, axis=-1, keepdims=True) + epsilon)
     x_hat = x_float * recip
-    core = core_ref[0]
+    core = place_ref[0]
     d_normed = None
-    for device in range(own_ref.shape[0]):
-        term = mm(d_inner_ref[device, core].T, own_ref[device])
-        term += mm(d_inner_ref[device, 1 - core].T, other_ref[device])
+    for mask, piece in enumerate(refs[:-6]):
+        device = place_ref[1] ^ mask
+        term = mm(piece[core].T, own_ref[device])
+        term += mm(piece[1 - core].T, other_ref[device])
         d_normed = term if d_normed is None else d_normed + term
     d_hat = d_normed * gain_ref[...]
     mean = jnp.mean(d_hat * x_hat, axis=-1, keepdims=True)
     out_ref[...] = (dh_ref[...] + recip * (d_hat - x_hat * mean)).astype(bf16)
 
 
-def token_grads(core, d_inner, w_half, w_other, x_rows, d_hidden, gain):
+def token_grads(place, d_inner, w_half, w_other, x_rows, d_hidden, gain):
     own, width = x_rows.shape
     return pl.pallas_call(
         tokens_kernel,
         in_specs=[pl.BlockSpec(memory_space=pltpu.SMEM)]
-        + [pl.BlockSpec(memory_space=pltpu.VMEM)] * 6,
+        + [pl.BlockSpec(memory_space=pltpu.VMEM)] * (5 + len(d_inner)),
         out_shape=jax.ShapeDtypeStruct((own, width), bf16),
         compiler_params=pltpu.CompilerParams(vmem_limit_bytes=40 * 2**20),
         cost_estimate=pl.CostEstimate(
-            flops=4 * d_inner.size * width, bytes_accessed=4 * w_half.size, transcendentals=0
-        ),
-    )(core, d_inner, w_half, w_other, x_rows, d_hidden, gain)
+            flops=4 * w_half.size * own, bytes_accessed=4 * w_half.size, transcendentals=0
+        ),
+    )(place, *d_inner, w_half, w_other, x_rows, d_hidden, gain)
 
 
 def widen_kernel(core_ref, gate_ref, up_ref, own_ref, other_ref, ggate_ref, gup_ref, gdown_ref, *, half):
@@ -651,11 +663,11 @@
 
     @pl.when(pl.program_id(0) < half)
     def _():
-        gdown_ref[...] = own_ref[...].astype(f32)
+        gdown_ref[0] = own_ref[...].astype(f32)
 
     @pl.when(pl.program_id(0) >= half)
     def _():
-        gdown_ref[...] = other_ref[...].astype(f32)
+        gdown_ref[0] = other_ref[...].astype(f32)
 
 
 def widen(core, grad_gate, grad_up, own_down, other_down):
@@ -675,8 +687,8 @@
             in_specs=[
                 gate_spec,
                 gate_spec,
-                pl.BlockSpec((1, hidden, width), lambda e, m: (jnp.minimum(e, half - 1), 0, 0)),
-                pl.BlockSpec((1, hidden, width), lambda e, m: (jnp.maximum(e - half, 0), 0, 0)),
+                pl.BlockSpec((hidden, width), lambda e, m: (jnp.minimum(e, half - 1), 0)),
+                pl.BlockSpec((hidden, width), lambda e, m: (jnp.maximum(e - half, 0), 0)),
             ],
             out_specs=[gate_spec, gate_spec, down_spec],
         ),
@@ -792,7 +804,7 @@
         w_down,
     )
     block_out, d_hidden, grad_gate, grad_up, send_out, keep_out, second_part = outs[:7]
-    d_heads = outs[7:]
+    d_heads = outs[7]
     grad_gate, grad_up = lax.psum((grad_gate, grad_up), ("seq", "kv"))
 
     chips = seq_devices // 2
@@ -808,14 +820,17 @@
         return jnp.broadcast_to(value[None], (number,) + value.shape)
 
     def rest(d_heads, d_hidden, send_out, keep_out, second_part):
-        do_parts = [exchange(d.reshape(kv_devices, query_cols, block_len)) for d in d_heads]
+        do_parts = exchange(d_heads)
         outer = added(keep_out, swap(send_out, "seq", 1)).reshape(chips, -1, width)
-        do_parts = [behind(do_part, outer) for do_part in do_parts]
+        sums = jnp.concatenate([second_part[0], local_load])
+        for axis in ("seq", "kv"):
+            sums = sum_over(sums, axis)
+        do_parts = behind(do_parts, (outer, sums))
         outer = over_chips(outer)
         dq, dkv = [], []
         for row in rows:
             dq_row, dkv_row = attend_back(
-                row, meta, q_t[row], do_parts[row], o_t[row], lse[row], kv_all[row], starts3,
+                row, meta, q_t[row], do_parts, o_t[row], lse[row], kv_all[row], starts3,
                 cosine, sine, group, orders[row],
             )
             dq.append(dq_row)
@@ -829,39 +844,36 @@
         d_parts, grad_inner_part = inner_grads(
             dq, dkv, gathered, cosine, sine, kv_devices, key_heads
         )
-        d_parts = exchange(d_parts).reshape(kv_devices, 2, inner_cols // 2, own)
         half = inner_cols // 2
+        paths = [seq_order(at, seq_devices) for at in range(2)]
+        shares = [halve_seq(grad_inner_part[half * at :][:half], paths[at]) for at in range(2)]
+        outer = copies(behind(outer, shares), chips)
+        d_parts = behind(d_parts, outer).reshape(kv_devices, 2, inner_cols // 2, own)
+        outer = over_chips(outer).reshape(-1, width)
+        kv_index = lax.axis_index("kv")
+        d_inner = [
+            swap(lax.dynamic_index_in_dim(d_parts, kv_index ^ mask, 0, keepdims=False), "kv", mask)
+            for mask in range(kv_devices)
+        ]
+        place = jnp.stack([core_index, kv_index]).astype(jnp.int32)
+        d_tokens = token_grads(
+            place, d_inner, w_inner_half, w_inner_other, x_rows, d_hidden, norm_first.reshape(1, width)
+        )
+        outer = behind(outer, d_tokens)
+        other_outer = swap(outer, "seq", 1)
+        shares = behind(shares, outer)
         grad_inner = jnp.concatenate(
-            [
-                sum_seq(grad_inner_part[:half], seq_order(0, seq_devices)),
-                sum_seq(grad_inner_part[half:], seq_order(1, seq_devices)),
-            ],
-            axis=0,
+            [double_seq(shares[at], paths[at]) for at in range(2)], axis=0
         ).astype(f32)
-        outer = copies(behind(outer, grad_inner), chips)
-        grad_inner, second_part, d_parts = behind((grad_inner, second_part, d_parts), outer)
-        outer = over_chips(outer)
-        sums = jnp.concatenate([second_part[0], local_load])
-        for axis in ("seq", "kv"):
-            sums = sum_over(sums, axis)
         first_part = jnp.sum(w_t.astype(f32) * grad_inner, axis=0)
         first_sum = sum_over(first_part, "kv") / norm_first
-        d_tokens = token_grads(
-            core, d_parts, w_inner_half, w_inner_other, x_rows, d_hidden, norm_first.reshape(1, width)
-        )
-        own_outer = behind(outer, (d_tokens, first_sum, sums)).reshape(keep_out.shape)
-        other_outer = swap(own_outer, "seq", 1)
-        kv_index = lax.axis_index("kv")
         half_devices = kv_devices // 2
-        start = lax.rem(kv_index, half_devices) * query_cols
+        start = (expert_count // 2) * w_down.shape[1] + lax.rem(kv_index, half_devices) * query_cols
         pieces = [
-            lax.dynamic_slice_in_dim(
-                pair[expert_count // 2 :].reshape(-1, width), start, query_cols, 0
-            )
-            for pair in (own_outer, other_outer)
+            lax.dynamic_slice_in_dim(pair, start, query_cols, 0) for pair in (outer, other_outer)
         ]
         own_out = jnp.where(kv_index // half_devices == core_index, *pieces).astype(f32)
-        return d_tokens, grad_inner, first_sum, own_outer, other_outer, own_out, sums
+        return d_tokens, grad_inner, first_sum, outer, other_outer, own_out, sums
 
     operands = (d_heads, d_hidden, send_out, keep_out, second_part)
     shapes = jax.eval_shape(rest, *operands)

time: 481 us -> 456 us (0.948)
  blocking collectives: 14.6 us -> 0 us
  starting transfers between devices: 121 us -> 115 us
    all_to_all x5 -> x4, waiting for transfers between devices: 75.1 us -> 46.5 us  [exchange(): return lax.all_to_all(value, 'kv', 0, 0)]
    all_to_all x1 -> x0, blocking collectives: 14.6 us -> none  [exchange(): return lax.all_to_all(value, 'kv', 0, 0)]
    all_to_all x2, waiting for transfers between devices: 0.01 us -> 14.4 us  [over_chips(): return lax.all_to_all(value, 'seq', 0, 0, axis_index_groups=groups)]
    ppermute x35 -> x38, waiting for transfers between devices: 75.9 us -> 90.1 us  [swap(): lax.ppermute(value, axis, [(source, source ^ mask) for source in range(co...]
    all_to_all x5 -> x4, starting transfers between devices: 18.4 us -> 16.2 us  [exchange(): return lax.all_to_all(value, 'kv', 0, 0)]
    ppermute x35 -> x38, starting transfers between devices: 82.1 us -> 82.4 us  [swap(): lax.ppermute(value, axis, [(source, source ^ mask) for source in range(co...]
  transfers between devices with their start and end apart: 46 -> 48, of which waited for: 25 -> 33; matrix products, arithmetic and copies ran while one was open for 10% -> 10% of each run, Pallas kernels for 10% -> 11%
where the time goes in v4:
time: 456 us; the launch traced here: 448 us
  waiting for transfers between devices  201 us (44%)
  starting transfers between devices  115 us (25%)
  Pallas kernels  67 us (15%)
  other arithmetic  34 us (7%)
  local copies, waits for them, and re-layouts  15.5 us (3%)
  between operations  15.3 us (3%)
    ppermute x38, waiting for transfers between devices, swap(): lax.ppermute(value, axis, [(source, source ^ mask) for source in range(co...  90.1 us
    ppermute x38, starting transfers between devices, swap(): lax.ppermute(value, axis, [(source, source ^ mask) for source in range(co...  82.4 us
    all_gather x1, waiting for transfers between devices, per_device(): gathered = lax.all_gather(normed, 'kv', axis=1, tiled=True)  47.5 us
    all_to_all x4, waiting for transfers between devices, exchange(): return lax.all_to_all(value, 'kv', 0, 0)  46.5 us
    pallas_call x1, Pallas kernels, run_experts(): pl.pallas_call(functools.partial(experts_kernel, experts=experts), grid_s...  23.8 us
    all_to_all x4, starting transfers between devices, exchange(): return lax.all_to_all(value, 'kv', 0, 0)  16.2 us
    all_to_all x2, starting transfers between devices, over_chips(): return lax.all_to_all(value, 'seq', 0, 0, axis_index_groups=groups)  15.6 us
    all_to_all x2, waiting for transfers between devices, over_chips(): return lax.all_to_all(value, 'seq', 0, 0, axis_index_groups=groups)  14.4 us
  transfers between devices with their start and end apart: 48, of which 33 were waited for; matrix products, arithmetic and copies ran while one was open for 10% of the time, Pallas kernels for 11%

profile of v4, /device:TPU:0, one launch (start us, length us, event | category | flops | bytes accessed | tf_op | source)
XLA Modules:
  0.0 447.7 jit_solution(10869234714938746030)
XLA Ops:
  12.0 47.5 %all-gather.6.cloned.1.call-done.n_ref = bf16[2,512,1024]{2,1,0:T(8,128)(2,1)} async-done(((bf16[2,128,1024]{2,1,0:T(8,128)(2,1)}), bf16[2,512,1024]{2,1,0:T(8,128)(2,1)}) %all-gather.6.cloned.1.call-update) | async-done | bytes 2097168 | tf_op jit(solution)/shard_map/all_gather | solution.py:754
  68.6 4.2 collective-permute-done.33
  77.0 9.4 %collective-permute-done.34 = bf16[2,256,512]{2,1,0:T(8,128)(2,1)S(1)} collective-permute-done((bf16[2,256,512]{2,1,0:T(8,128)(2,1)S(1)}, bf16[2,256,512]{2,1,0:T(8,128)(2,1)S(1)}, u32[]{:S(2)}, u32[]{:S(2)}) %collective-permute-start.34) | collective-permute-done | bytes 524320 | tf_op jit(solution)/shard_map/ppermute | solution.py:53
  96.7 3.5 shard_map.231
  100.2 3.5 shard_map.232
  105.1 3.5 all-to-all-start.5
  109.9 27.0 %all-to-all-done.5.refs_0_ = bf16[4,2,256,128]{3,2,1,0:T(8,128)(2,1)S(1)} async-done(((bf16[4,2,256,128]{3,2,1,0:T(8,128)(2,1)}), bf16[4,2,256,128]{3,2,1,0:T(8,128)(2,1)S(1)}, u32[]{:S(2)}, u32[]{:S(2)}) %all-to-all-start.5) | async-done | bytes 524320 | tf_op jit(solution)/shard_map/all_to_all | solution.py:769
  137.6 23.8 %shard_map.233 = (bf16[256,1024]{1,0:T(8,128)(2,1)}, f32[256,1024]{1,0:T(8,128)}, bf16[4,1024,512]{2,1,0:T(8,128)(2,1)}, bf16[4,1024,512]{2,1,0:T(8,128)(2,1)}, ...) custom-call(s32[1]{0:T(128)} %bitcast.16.core_ref, ...), custom_call_target="tpu_custom_call" | custom-call | flops 9663676416 | bytes 25165824 | tf_op jit(solution)/shard_map/pallas_call | solution.py:517
  168.8 253.7 %conditional.1 = (f32[512,1024]{1,0:T(8,128)}, f32[1024]{0:T(1024)S(1)}, bf16[1536,1024]{1,0:T(8,128)(2,1)}, bf16[1536,1024]{1,0:T(8,128)(2,1)}, f32[256,1024]{1...) conditional(s32[]{:T(128)} %bitcast.37, () %tuple.30, (bf16[4,2,256,128]{3,2,1,0:T(8,128)(2,1)}, ...), branch_computations={%region_2.3_spmd, %region_3.8_spmd} | conditional | flops 23652646912 | bytes 178519072 | solution.py:880
  169.6 4.8 %all-to-all-start = ((bf16[4,2,256,128]{3,2,1,0:T(8,128)(2,1)}), bf16[4,2,256,128]{3,2,1,0:T(8,128)(2,1)S(1)}, u32[]{:S(2)}, u32[]{:S(2)}) async-start(bf16[4,2,256,128]{3,2,1,0:T(8,128)(2,1)} %get-tuple-element.55), calls=%async_computation | async-start | bytes 1048576 | tf_op jit(solution)/shard_map/cond/branch_1_fun/all_to_all | solution.py:769
  175.8 10.0 %collective-permute-start.2 = (f32[1028]{0:T(1024)S(1)}, f32[1028]{0:T(1024)S(1)}, u32[]{:S(2)}, u32[]{:S(2)}) collective-permute-start(f32[1028]{0:T(1024)S(1)} %fusion.2), channel_id=1, source_target_pairs={{0,8},{4,12},{8,0},{12,4},{16,24},{20,28},{24,16},{28,20},{1,9},{5... | collective-permute-start | bytes 12344 | tf_op jit(solution)/shard_map/cond/branch_1_fun/ppermute | solution.py:53
  201.6 6.4 %add_convert_fusion = bf16[3,512,1024]{2,1,0:T(8,128)(2,1)} fusion(bf16[3,512,1024]{2,1,0:T(8,128)(2,1)} %collective-permute-done, bf16[3,512,1024]{2,1,0:T(8,128)(2,1)} %get-tuple-element.56), kind=kLoop, calls=%fused_computation | loop fusion | flops 6291456 | bytes 9437184 | tf_op jit(solution)/shard_map/cond/branch_1_fun/convert_element_type | solution.py:117
  207.9 10.9 %all-to-all-start.1 = ((bf16[4,384,1024]{2,1,0:T(8,128)(2,1)}), bf16[4,384,1024]{2,1,0:T(8,128)(2,1)}, u32[]{:S(2)}, u32[]{:S(2)}) async-start(bf16[4,384,1024]{2,1,0:T(8,128)(2,1)} %bitcast.56), calls=%async_computation.1 | async-start | bytes 6291456 | tf_op jit(solution)/shard_map/cond/branch_1_fun/all_to_all | solution.py:814
  218.9 5.8 %branch_1_fun.4 = (bf16[256,512]{1,0:T(8,128)(2,1)S(1)}, bf16[8,256,512]{2,1,0:T(8,128)(2,1)S(1)}) custom-call(s32[5]{0:T(128)S(1)} %get-tuple-element.53.meta_ref, bf16[256,512]{1,0:T(8,128)(2,1)S(1)} %get-tuple-element.54.q_ref, bf16[4,2,256,128]{3,2,1,0:T(8,128)(2,1)S(1)} %all-to-all-done.do_ref, f32[256,512]{1,0:T(8,128)S(1)} %get-tuple-element.61.o_ref, ...), custom_call_target="tpu_custom_call" | custom-call | flops 10737418240 | bytes 4194304 | tf_op jit(solution)/shard_map/cond/branch_1_fun/pallas_call | solution.py:360
  226.9 4.7 %branch_1_fun.5 = (bf16[256,512]{1,0:T(8,128)(2,1)S(1)}, bf16[8,256,512]{2,1,0:T(8,128)(2,1)S(1)}) custom-call(s32[5]{0:T(128)S(1)} %get-tuple-element.53.meta_ref, bf16[256,512]{1,0:T(8,128)(2,1)S(1)} %copy-done.28, bf16[4,2,256,128]{3,2,1,0:T(8,128)(2,1)S(1)} %all-to-all-done.do_ref, f32[256,512]{1,0:T(8,128)S(1)} %copy-done.31, ...), custom_call_target="tpu_custom_call" | custom-call | flops 10737418240 | bytes 4194304 | tf_op jit(solution)/shard_map/cond/branch_1_fun/pallas_call | solution.py:360
  231.7 5.0 %collective-permute-start.9 = (bf16[4,256,512]{2,1,0:T(8,128)(2,1)S(1)}, bf16[4,256,512]{2,1,0:T(8,128)(2,1)S(1)}, u32[]{:S(2)}, u32[]{:S(2)}) collective-permute-start(bf16[4,256,512]{2,1,0:T(8,128)(2,1)S(1)} %slice.81), channel_id=1, source_target_pairs={{0,4},{4,0},{8,12},{12,8},{16,20},{20,16},{24,28},{28,24},{1,5},{5... | collective-permute-start | bytes 3145736 | tf_op jit(solution)/shard_map/cond/branch_1_fun/ppermute | solution.py:53
  237.0 31.9 %collective-permute-start.7 = (bf16[2,256,512]{2,1,0:T(8,128)(2,1)S(1)}, bf16[2,256,512]{2,1,0:T(8,128)(2,1)}, u32[]{:S(2)}, u32[]{:S(2)}) collective-permute-start(bf16[2,256,512]{2,1,0:T(8,128)(2,1)S(1)} %slice.123), channel_id=1, source_target_pairs={{0,16},{4,20},{8,24},{12,28},{16,0},{20,4},{24,8},{28,12},{1,17},{... | collective-permute-start | bytes 1572872 | tf_op jit(solution)/shard_map/cond/branch_1_fun/ppermute | solution.py:53
  270.1 3.6 reduce_sum.56
  273.7 4.5 all-to-all-start.2
  278.2 5.8 %collective-permute-done.7 = bf16[2,256,512]{2,1,0:T(8,128)(2,1)} collective-permute-done((bf16[2,256,512]{2,1,0:T(8,128)(2,1)S(1)}, bf16[2,256,512]{2,1,0:T(8,128)(2,1)}, u32[]{:S(2)}, u32[]{:S(2)}) %collective-permute-start.7) | collective-permute-done | bytes 524320 | tf_op jit(solution)/shard_map/cond/branch_1_fun/ppermute | solution.py:53
  289.1 3.8 collective-permute-done.8
  295.2 5.8 %all-to-all-done.2 = bf16[4,96,1024]{2,1,0:T(8,128)(2,1)} async-done(((bf16[4,96,1024]{2,1,0:T(8,128)(2,1)}), bf16[4,96,1024]{2,1,0:T(8,128)(2,1)}, u32[]{:S(2)}, u32[]{:S(2)}) %all-to-all-start.2) | async-done | bytes 786464 | tf_op jit(solution)/shard_map/cond/branch_1_fun/all_to_all | solution.py:769
  307.8 3.5 all-to-all-start.3
  325.9 13.7 %all-to-all-done.3 = bf16[4,96,1024]{2,1,0:T(8,128)(2,1)S(1)} async-done(((bf16[4,96,1024]{2,1,0:T(8,128)(2,1)}), bf16[4,96,1024]{2,1,0:T(8,128)(2,1)S(1)}, u32[]{:S(2)}, u32[]{:S(2)}) %all-to-all-start.3) | async-done | bytes 786464 | tf_op jit(solution)/shard_map/cond/branch_1_fun/all_to_all | solution.py:769
  341.7 4.7 %all-to-all-start.4 = ((bf16[4,384,1024]{2,1,0:T(8,128)(2,1)}), bf16[4,384,1024]{2,1,0:T(8,128)(2,1)}, u32[]{:S(2)}, u32[]{:S(2)}) async-start(bf16[4,384,1024]{2,1,0:T(8,128)(2,1)} %broadcast_in_dim.1), calls=%async_computation.4 | async-start | bytes 6291456 | tf_op jit(solution)/shard_map/cond/branch_1_fun/all_to_all | solution.py:814
  351.1 11.8 %collective-permute-done.20.refs_3_ = bf16[2,256,256]{2,1,0:T(8,128)(2,1)S(1)} collective-permute-done((bf16[2,256,256]{2,1,0:T(8,128)(2,1)S(1)}, bf16[2,256,256]{2,1,0:T(8,128)(2,1)S(1)}, u32[]{:S(2)}, u32[]{:S(2)}) %collective-permute-start.20) | collective-permute-done | bytes 262176 | tf_op jit(solution)/shard_map/cond/branch_1_fun/ppermute | solution.py:53
  362.9 15.5 %collective-permute-done.19.refs_2_ = bf16[2,256,256]{2,1,0:T(8,128)(2,1)S(1)} collective-permute-done((bf16[2,256,256]{2,1,0:T(8,128)(2,1)S(1)}, bf16[2,256,256]{2,1,0:T(8,128)(2,1)S(1)}, u32[]{:S(2)}, u32[]{:S(2)}) %collective-permute-start.19) | collective-permute-done | bytes 262176 | tf_op jit(solution)/shard_map/cond/branch_1_fun/ppermute | solution.py:53
  378.5 4.6 %branch_1_fun.7 = bf16[256,1024]{1,0:T(8,128)(2,1)} custom-call(s32[2]{0:T(128)S(1)} %pad_add_fusion.place_ref, bf16[2,256,256]{2,1,0:T(8,128)(2,1)S(1)} %get-tuple-element.178.refs_0_, bf16[2,256,256]{2,1,0:T(8,128)(2,1)S(1)} %collective-permute-done.18.refs_1_, bf16[2,256,256]{2,1,0:T(8,128)(2,1)S(1)} %collective-permute-done.19.refs_2_, ...), custom_call_target="tpu_custom_call" | custom-call | flops 1073741824 | bytes 4194304 | tf_op jit(solution)/shard_map/cond/branch_1_fun/pallas_call | solution.py:648
  383.1 14.4 %all-to-all-done.4 = bf16[4,384,1024]{2,1,0:T(8,128)(2,1)} async-done(((bf16[4,384,1024]{2,1,0:T(8,128)(2,1)}), bf16[4,384,1024]{2,1,0:T(8,128)(2,1)}, u32[]{:S(2)}, u32[]{:S(2)}) %all-to-all-start.4) | async-done | bytes 3145760 | tf_op jit(solution)/shard_map/cond/branch_1_fun/all_to_all | solution.py:814
  412.1 3.6 collective-permute-done.27
  416.2 4.0 collective-permute-done.28
  428.1 12.6 %shard_map.234 = (f32[4,1024,512]{2,1,0:T(8,128)}, f32[4,1024,512]{2,1,0:T(8,128)}, f32[4,512,1024]{2,1,0:T(8,128)}) custom-call(s32[1]{0:T(128)} %bitcast.16.core_ref, bf16[4,1024,512]{2,1,0:T(8,128)(2,1)} %get-tuple-element.169.gate_ref, bf16[4,1024,512]{2,1,0:T(8,128)(2,1)} %get-tuple-element.170.up_ref, bf16[1536,1024]{1,0:T(8,128)(2,1)} %get-tuple-element.164.own_ref, ...), custom_call_target="tpu_custom_call" | custom-call | bytes 37748736 | tf_op jit(solution)/shard_map/pallas_call | solution.py:682
  (227 shorter events, 117.9 us)
Async XLA Ops:
  7.2 52.2 %all-gather.6.cloned.1.call-start = ((), (), s32[]{:S(2)}) async-start(), calls=%async_computation.6 | async-start | bytes 2621440 | tf_op jit(solution)/shard_map/all_gather | solution.py:754
  10.7 82.3 %all-gather.8.cloned.1.call-start = ((), (), s32[]{:S(2)}) async-start(), calls=%async_computation.7 | async-start | bytes 1310720 | tf_op jit(solution)/shard_map/all_gather | solution.py:763
  64.8 8.0 %collective-permute-start.33 = (bf16[1,256,512]{2,1,0:T(8,128)(2,1)S(1)}, bf16[1,256,512]{2,1,0:T(8,128)(2,1)S(1)}, u32[]{:S(2)}, u32[]{:S(2)}) collective-permute-start(bf16[1,256,512]{2,1,0:T(8,128)(2,1)S(1)} %bitcast.64), channel_id=1, source_target_pairs={{0,16},{4,20},{8,24},{12,28},{16,0},{20,4},{24,8},{28,12},{1,17},{... | collective-permute-start | bytes 786440 | tf_op jit(solution)/shard_map/ppermute | solution.py:53
  67.1 94.5 %all-gather.10.cloned.1.call-start = ((), (), s32[]{:S(2)}) async-start(), calls=%async_computation.8 | async-start | bytes 2621440 | tf_op jit(solution)/shard_map/all_gather | solution.py:765
  67.1 8.6 %collective-permute-start.30 = (bf16[1,256,512]{2,1,0:T(8,128)(2,1)}, bf16[1,256,512]{2,1,0:T(8,128)(2,1)S(1)}, u32[]{:S(2)}, u32[]{:S(2)}) collective-permute-start(bf16[1,256,512]{2,1,0:T(8,128)(2,1)} %bitcast.60), channel_id=1, source_target_pairs={{0,8},{4,12},{8,0},{12,4},{16,24},{20,28},{24,16},{28,20},{1,9},{5... | collective-permute-start | bytes 786440 | tf_op jit(solution)/shard_map/ppermute | solution.py:53
  72.9 13.5 %collective-permute-start.34 = (bf16[2,256,512]{2,1,0:T(8,128)(2,1)S(1)}, bf16[2,256,512]{2,1,0:T(8,128)(2,1)S(1)}, u32[]{:S(2)}, u32[]{:S(2)}) collective-permute-start(bf16[2,256,512]{2,1,0:T(8,128)(2,1)S(1)} %pad_maximum_fusion.7), channel_id=1, source_target_pairs={{0,8},{4,12},{8,0},{12,4},{16,24},{20,28},{24,16},{28,20},{1,9},{5... | collective-permute-start | bytes 1572872 | tf_op jit(solution)/shard_map/ppermute | solution.py:53
  76.7 11.9 %collective-permute-start.31 = (bf16[2,256,512]{2,1,0:T(8,128)(2,1)S(1)}, bf16[2,256,512]{2,1,0:T(8,128)(2,1)S(1)}, u32[]{:S(2)}, u32[]{:S(2)}) collective-permute-start(bf16[2,256,512]{2,1,0:T(8,128)(2,1)S(1)} %pad_maximum_fusion.6), channel_id=1, source_target_pairs={{0,16},{4,20},{8,24},{12,28},{16,0},{20,4},{24,8},{28,12},{1,17},{... | collective-permute-start | bytes 1572872 | tf_op jit(solution)/shard_map/ppermute | solution.py:53
  87.4 5.5 %collective-permute-start.35 = (bf16[4,256,512]{2,1,0:T(8,128)(2,1)}, bf16[4,256,512]{2,1,0:T(8,128)(2,1)}, u32[]{:S(2)}, u32[]{:S(2)}) collective-permute-start(bf16[4,256,512]{2,1,0:T(8,128)(2,1)} %pad_maximum_fusion.5), channel_id=1, source_target_pairs={{0,4},{4,0},{8,12},{12,8},{16,20},{20,16},{24,28},{28,24},{1,5},{5... | collective-permute-start | bytes 3145736 | tf_op jit(solution)/shard_map/ppermute | solution.py:53
  93.0 16.9 %collective-permute-start.36 = (bf16[4,128,1024]{2,1,0:T(8,128)(2,1)}, bf16[4,128,1024]{2,1,0:T(8,128)(2,1)}, u32[]{:S(2)}, u32[]{:S(2)}) collective-permute-start(bf16[4,128,1024]{2,1,0:T(8,128)(2,1)} %bitcast.82), channel_id=1, source_target_pairs={{0,4},{4,0},{8,12},{12,8},{16,20},{20,16},{24,28},{28,24},{1,5},{5... | collective-permute-start | bytes 3145736 | tf_op jit(solution)/shard_map/ppermute | solution.py:53
  105.1 31.7 %all-to-all-start.5 = ((bf16[4,2,256,128]{3,2,1,0:T(8,128)(2,1)}), bf16[4,2,256,128]{3,2,1,0:T(8,128)(2,1)S(1)}, u32[]{:S(2)}, u32[]{:S(2)}) async-start(bf16[4,2,256,128]{3,2,1,0:T(8,128)(2,1)} %pad_maximum_fusion.8), calls=%async_computation.5 | async-start | bytes 1048576 | tf_op jit(solution)/shard_map/all_to_all | solution.py:769
  108.6 319.5 %all-reduce.3.cloned.1.call-start = ((), (), s32[]{:S(2)}) async-start(), calls=%async_computation.9 | async-start | bytes 16777216 | tf_op jit(solution)/shard_map/psum | solution.py:808
  161.6 7.3 %collective-permute-start.37 = (bf16[4,256,1024]{2,1,0:T(8,128)(2,1)}, bf16[4,256,1024]{2,1,0:T(8,128)(2,1)}, u32[]{:S(2)}, u32[]{:S(2)}) collective-permute-start(bf16[4,256,1024]{2,1,0:T(8,128)(2,1)} %bitcast.68), channel_id=1, source_target_pairs={{0,4},{4,0},{8,12},{12,8},{16,20},{20,16},{24,28},{28,24},{1,5},{5... | collective-permute-start | bytes 6291464 | tf_op jit(solution)/shard_map/ppermute | solution.py:53
  168.9 32.7 %collective-permute-start = (bf16[3,512,1024]{2,1,0:T(8,128)(2,1)}, bf16[3,512,1024]{2,1,0:T(8,128)(2,1)}, u32[]{:S(2)}, u32[]{:S(2)}) collective-permute-start(bf16[3,512,1024]{2,1,0:T(8,128)(2,1)} %get-tuple-element.57), channel_id=1, source_target_pairs={{0,4},{4,0},{8,12},{12,8},{16,20},{20,16},{24,28},{28,24},{1,5},{5... | collective-permute-start | bytes 9437192 | tf_op jit(solution)/shard_map/cond/branch_1_fun/ppermute | solution.py:53
  169.6 38.3 %all-to-all-start = ((bf16[4,2,256,128]{3,2,1,0:T(8,128)(2,1)}), bf16[4,2,256,128]{3,2,1,0:T(8,128)(2,1)S(1)}, u32[]{:S(2)}, u32[]{:S(2)}) async-start(bf16[4,2,256,128]{3,2,1,0:T(8,128)(2,1)} %get-tuple-element.55), calls=%async_computation | async-start | bytes 1048576 | tf_op jit(solution)/shard_map/cond/branch_1_fun/all_to_all | solution.py:769
  175.8 11.9 %collective-permute-start.2 = (f32[1028]{0:T(1024)S(1)}, f32[1028]{0:T(1024)S(1)}, u32[]{:S(2)}, u32[]{:S(2)}) collective-permute-start(f32[1028]{0:T(1024)S(1)} %fusion.2), channel_id=1, source_target_pairs={{0,8},{4,12},{8,0},{12,4},{16,24},{20,28},{24,16},{28,20},{1,9},{5... | collective-permute-start | bytes 12344 | tf_op jit(solution)/shard_map/cond/branch_1_fun/ppermute | solution.py:53
  207.9 62.1 %all-to-all-start.1 = ((bf16[4,384,1024]{2,1,0:T(8,128)(2,1)}), bf16[4,384,1024]{2,1,0:T(8,128)(2,1)}, u32[]{:S(2)}, u32[]{:S(2)}) async-start(bf16[4,384,1024]{2,1,0:T(8,128)(2,1)} %bitcast.56), calls=%async_computation.1 | async-start | bytes 6291456 | tf_op jit(solution)/shard_map/cond/branch_1_fun/all_to_all | solution.py:814
  224.8 11.9 %collective-permute-start.6 = (bf16[4,256,512]{2,1,0:T(8,128)(2,1)S(1)}, bf16[4,256,512]{2,1,0:T(8,128)(2,1)S(1)}, u32[]{:S(2)}, u32[]{:S(2)}) collective-permute-start(bf16[4,256,512]{2,1,0:T(8,128)(2,1)S(1)} %slice.23), channel_id=1, source_target_pairs={{0,4},{4,0},{8,12},{12,8},{16,20},{20,16},{24,28},{28,24},{1,5},{5... | collective-permute-start | bytes 3145736 | tf_op jit(solution)/shard_map/cond/branch_1_fun/ppermute | solution.py:53
  231.7 37.2 %collective-permute-start.9 = (bf16[4,256,512]{2,1,0:T(8,128)(2,1)S(1)}, bf16[4,256,512]{2,1,0:T(8,128)(2,1)S(1)}, u32[]{:S(2)}, u32[]{:S(2)}) collective-permute-start(bf16[4,256,512]{2,1,0:T(8,128)(2,1)S(1)} %slice.81), channel_id=1, source_target_pairs={{0,4},{4,0},{8,12},{12,8},{16,20},{20,16},{24,28},{28,24},{1,5},{5... | collective-permute-start | bytes 3145736 | tf_op jit(solution)/shard_map/cond/branch_1_fun/ppermute | solution.py:53
  237.0 46.9 %collective-permute-start.7 = (bf16[2,256,512]{2,1,0:T(8,128)(2,1)S(1)}, bf16[2,256,512]{2,1,0:T(8,128)(2,1)}, u32[]{:S(2)}, u32[]{:S(2)}) collective-permute-start(bf16[2,256,512]{2,1,0:T(8,128)(2,1)S(1)} %slice.123), channel_id=1, source_target_pairs={{0,16},{4,20},{8,24},{12,28},{16,0},{20,4},{24,8},{28,12},{1,17},{... | collective-permute-start | bytes 1572872 | tf_op jit(solution)/shard_map/cond/branch_1_fun/ppermute | solution.py:53
  270.0 15.3 %collective-permute-start.10 = (bf16[2,256,512]{2,1,0:T(8,128)(2,1)}, bf16[2,256,512]{2,1,0:T(8,128)(2,1)}, u32[]{:S(2)}, u32[]{:S(2)}) collective-permute-start(bf16[2,256,512]{2,1,0:T(8,128)(2,1)} %slice.127), channel_id=1, source_target_pairs={{0,8},{4,12},{8,0},{12,4},{16,24},{20,28},{24,16},{28,20},{1,9},{5... | collective-permute-start | bytes 1572872 | tf_op jit(solution)/shard_map/cond/branch_1_fun/ppermute | solution.py:53
  273.7 27.4 %all-to-all-start.2 = ((bf16[4,96,1024]{2,1,0:T(8,128)(2,1)}), bf16[4,96,1024]{2,1,0:T(8,128)(2,1)}, u32[]{:S(2)}, u32[]{:S(2)}) async-start(bf16[4,96,1024]{2,1,0:T(8,128)(2,1)} %bitcast.4), calls=%async_computation.2 | async-start | bytes 1572864 | tf_op jit(solution)/shard_map/cond/branch_1_fun/all_to_all | solution.py:769
  285.1 7.8 %collective-permute-start.8 = (bf16[1,256,512]{2,1,0:T(8,128)(2,1)S(1)}, bf16[1,256,512]{2,1,0:T(8,128)(2,1)S(1)}, u32[]{:S(2)}, u32[]{:S(2)}) collective-permute-start(bf16[1,256,512]{2,1,0:T(8,128)(2,1)S(1)} %slice.125), channel_id=1, source_target_pairs={{0,8},{4,12},{8,0},{12,4},{16,24},{20,28},{24,16},{28,20},{1,9},{5... | collective-permute-start | bytes 786440 | tf_op jit(solution)/shard_map/cond/branch_1_fun/ppermute | solution.py:53
  286.5 8.6 %collective-permute-start.11 = (bf16[1,256,512]{2,1,0:T(8,128)(2,1)S(1)}, bf16[1,256,512]{2,1,0:T(8,128)(2,1)S(1)}, u32[]{:S(2)}, u32[]{:S(2)}) collective-permute-start(bf16[1,256,512]{2,1,0:T(8,128)(2,1)S(1)} %slice.129), channel_id=1, source_target_pairs={{0,16},{4,20},{8,24},{12,28},{16,0},{20,4},{24,8},{28,12},{1,17},{... | collective-permute-start | bytes 786440 | tf_op jit(solution)/shard_map/cond/branch_1_fun/ppermute | solution.py:53
  306.2 5.8 %collective-permute-start.12 = (bf16[128,1024]{1,0:T(8,128)(2,1)S(1)}, bf16[128,1024]{1,0:T(8,128)(2,1)}, u32[]{:S(2)}, u32[]{:S(2)}) collective-permute-start(bf16[128,1024]{1,0:T(8,128)(2,1)S(1)} %get-tuple-element.182), channel_id=1, source_target_pairs={{0,4},{4,0},{8,12},{12,8},{16,20},{20,16},{24,28},{28,24},{1,5},{5... | collective-permute-start | bytes 786440 | tf_op jit(solution)/shard_map/cond/branch_1_fun/ppermute | solution.py:53
  307.8 31.9 %all-to-all-start.3 = ((bf16[4,96,1024]{2,1,0:T(8,128)(2,1)}), bf16[4,96,1024]{2,1,0:T(8,128)(2,1)S(1)}, u32[]{:S(2)}, u32[]{:S(2)}) async-start(bf16[4,96,1024]{2,1,0:T(8,128)(2,1)} %broadcast_in_dim.0), calls=%async_computation.3 | async-start | bytes 1572864 | tf_op jit(solution)/shard_map/cond/branch_1_fun/all_to_all | solution.py:769
  313.3 5.7 %collective-permute-start.13 = (bf16[64,1024]{1,0:T(8,128)(2,1)S(1)}, bf16[64,1024]{1,0:T(8,128)(2,1)S(1)}, u32[]{:S(2)}, u32[]{:S(2)}) collective-permute-start(bf16[64,1024]{1,0:T(8,128)(2,1)S(1)} %broadcast_select_fusion.2), channel_id=1, source_target_pairs={{0,16},{4,20},{8,24},{12,28},{16,0},{20,4},{24,8},{28,12},{1,17},{... | collective-permute-start | bytes 393224 | tf_op jit(solution)/shard_map/cond/branch_1_fun/ppermute | solution.py:53
  341.7 55.8 %all-to-all-start.4 = ((bf16[4,384,1024]{2,1,0:T(8,128)(2,1)}), bf16[4,384,1024]{2,1,0:T(8,128)(2,1)}, u32[]{:S(2)}, u32[]{:S(2)}) async-start(bf16[4,384,1024]{2,1,0:T(8,128)(2,1)} %broadcast_in_dim.1), calls=%async_computation.4 | async-start | bytes 6291456 | tf_op jit(solution)/shard_map/cond/branch_1_fun/all_to_all | solution.py:814
  346.6 16.4 %collective-permute-start.20 = (bf16[2,256,256]{2,1,0:T(8,128)(2,1)S(1)}, bf16[2,256,256]{2,1,0:T(8,128)(2,1)S(1)}, u32[]{:S(2)}, u32[]{:S(2)}) collective-permute-start(bf16[2,256,256]{2,1,0:T(8,128)(2,1)S(1)} %get-tuple-element.175), channel_id=1, source_target_pairs={{0,3},{1,2},{2,1},{3,0},{4,7},{5,6},{6,5},{7,4},{8,11},{9,10},{10,... | collective-permute-start | bytes 786440 | tf_op jit(solution)/shard_map/cond/branch_1_fun/ppermute | solution.py:53
  348.1 30.4 %collective-permute-start.19 = (bf16[2,256,256]{2,1,0:T(8,128)(2,1)S(1)}, bf16[2,256,256]{2,1,0:T(8,128)(2,1)S(1)}, u32[]{:S(2)}, u32[]{:S(2)}) collective-permute-start(bf16[2,256,256]{2,1,0:T(8,128)(2,1)S(1)} %get-tuple-element.176), channel_id=1, source_target_pairs={{0,2},{1,3},{2,0},{3,1},{4,6},{5,7},{6,4},{7,5},{8,10},{9,11},{10,... | collective-permute-start | bytes 786440 | tf_op jit(solution)/shard_map/cond/branch_1_fun/ppermute | solution.py:53
  348.1 30.4 %collective-permute-start.18 = (bf16[2,256,256]{2,1,0:T(8,128)(2,1)S(1)}, bf16[2,256,256]{2,1,0:T(8,128)(2,1)S(1)}, u32[]{:S(2)}, u32[]{:S(2)}) collective-permute-start(bf16[2,256,256]{2,1,0:T(8,128)(2,1)S(1)} %get-tuple-element.177), channel_id=1, source_target_pairs={{0,1},{1,0},{2,3},{3,2},{4,5},{5,4},{6,7},{7,6},{8,9},{9,8},{10,11... | collective-permute-start | bytes 786440 | tf_op jit(solution)/shard_map/cond/branch_1_fun/ppermute | solution.py:53
  397.5 23.3 %collective-permute-start.29 = (bf16[1536,1024]{1,0:T(8,128)(2,1)}, bf16[1536,1024]{1,0:T(8,128)(2,1)}, u32[]{:S(2)}, u32[]{:S(2)}) collective-permute-start(bf16[1536,1024]{1,0:T(8,128)(2,1)} %bitcast.6), channel_id=1, source_target_pairs={{0,4},{4,0},{8,12},{12,8},{16,20},{20,16},{24,28},{28,24},{1,5},{5... | collective-permute-start | bytes 9437192 | tf_op jit(solution)/shard_map/cond/branch_1_fun/ppermute | solution.py:53
  402.1 5.3 %collective-permute-start.22 = (bf16[64,1024]{1,0:T(8,128)(2,1)S(1)}, bf16[64,1024]{1,0:T(8,128)(2,1)S(1)}, u32[]{:S(2)}, u32[]{:S(2)}) collective-permute-start(bf16[64,1024]{1,0:T(8,128)(2,1)S(1)} %maximum_select_fusion.4), channel_id=1, source_target_pairs={{0,16},{4,20},{8,24},{12,28},{16,0},{20,4},{24,8},{28,12},{1,17},{... | collective-permute-start | bytes 393224 | tf_op jit(solution)/shard_map/cond/branch_1_fun/ppermute | solution.py:53
  (48 other events, 470.5 us)
Sparse Core Ops, SparseCore 0:
  10.8 48.6 all-gather.5
  67.2 25.7 all-gather.7
  94.5 56.5 all-gather.9
  161.7 245.5 all-reduce.2

commit v5 on v4

--- a/solution.py
+++ b/solution.py
@@ -657,10 +657,28 @@
     )(place, *d_inner, w_half, w_other, x_rows, d_hidden, gain)
 
 
-def widen_kernel(core_ref, gate_ref, up_ref, own_ref, other_ref, ggate_ref, gup_ref, gdown_ref, *, half):
+def widen_whole_kernel(gate_ref, up_ref, ggate_ref, gup_ref):
     ggate_ref[...] = gate_ref[...].astype(f32)
     gup_ref[...] = up_ref[...].astype(f32)
 
+
+def widen_whole(grad_gate, grad_up):
+    experts, width, hidden = grad_gate.shape
+    spec = pl.BlockSpec((1, width, hidden), lambda e: (e, 0, 0))
+    return pl.pallas_call(
+        widen_whole_kernel,
+        grid=(experts,),
+        in_specs=[spec, spec],
+        out_specs=[spec, spec],
+        out_shape=[jax.ShapeDtypeStruct(grad_gate.shape, f32)] * 2,
+        compiler_params=pltpu.CompilerParams(vmem_limit_bytes=60 * 2**20),
+        cost_estimate=pl.CostEstimate(
+            flops=0, bytes_accessed=12 * grad_gate.size, transcendentals=0
+        ),
+    )(grad_gate, grad_up)
+
+
+def widen_halves_kernel(core_ref, own_ref, other_ref, gdown_ref, *, half):
     @pl.when(pl.program_id(0) < half)
     def _():
         gdown_ref[0] = own_ref[...].astype(f32)
@@ -670,38 +688,28 @@
         gdown_ref[0] = other_ref[...].astype(f32)
 
 
-def widen(core, grad_gate, grad_up, own_down, other_down):
-    experts, width, hidden = grad_gate.shape
+def widen_halves(core, own_rows, other_rows, experts, hidden):
+    width = own_rows.shape[1]
     half = experts // 2
-
-    def which(e, m):
-        return lax.rem(e + m[0] * half, experts)
-
-    gate_spec = pl.BlockSpec((1, width, hidden), lambda e, m: (which(e, m), 0, 0))
-    down_spec = pl.BlockSpec((1, hidden, width), lambda e, m: (which(e, m), 0, 0))
     return pl.pallas_call(
-        functools.partial(widen_kernel, half=half),
+        functools.partial(widen_halves_kernel, half=half),
         grid_spec=pltpu.PrefetchScalarGridSpec(
             num_scalar_prefetch=1,
             grid=(experts,),
             in_specs=[
-                gate_spec,
-                gate_spec,
                 pl.BlockSpec((hidden, width), lambda e, m: (jnp.minimum(e, half - 1), 0)),
                 pl.BlockSpec((hidden, width), lambda e, m: (jnp.maximum(e - half, 0), 0)),
             ],
-            out_specs=[gate_spec, gate_spec, down_spec],
-        ),
-        out_shape=[
-            jax.ShapeDtypeStruct(grad_gate.shape, f32),
-            jax.ShapeDtypeStruct(grad_gate.shape, f32),
-            jax.ShapeDtypeStruct((experts, hidden, width), f32),
-        ],
+            out_specs=pl.BlockSpec(
+                (1, hidden, width), lambda e, m: (lax.rem(e + m[0] * half, experts), 0, 0)
+            ),
+        ),
+        out_shape=jax.ShapeDtypeStruct((experts, hidden, width), f32),
         compiler_params=pltpu.CompilerParams(vmem_limit_bytes=60 * 2**20),
         cost_estimate=pl.CostEstimate(
-            flops=0, bytes_accessed=18 * grad_gate.size, transcendentals=0
-        ),
-    )(core, grad_gate, grad_up, own_down, other_down)
+            flops=0, bytes_accessed=6 * experts * hidden * width, transcendentals=0
+        ),
+    )(core, own_rows, other_rows)
 
 
 def per_device(
@@ -860,30 +868,32 @@
             place, d_inner, w_inner_half, w_inner_other, x_rows, d_hidden, norm_first.reshape(1, width)
         )
         outer = behind(outer, d_tokens)
-        other_outer = swap(outer, "seq", 1)
-        shares = behind(shares, outer)
-        grad_inner = jnp.concatenate(
-            [double_seq(shares[at], paths[at]) for at in range(2)], axis=0
-        ).astype(f32)
-        first_part = jnp.sum(w_t.astype(f32) * grad_inner, axis=0)
-        first_sum = sum_over(first_part, "kv") / norm_first
-        half_devices = kv_devices // 2
-        start = (expert_count // 2) * w_down.shape[1] + lax.rem(kv_index, half_devices) * query_cols
-        pieces = [
-            lax.dynamic_slice_in_dim(pair, start, query_cols, 0) for pair in (outer, other_outer)
-        ]
-        own_out = jnp.where(kv_index // half_devices == core_index, *pieces).astype(f32)
-        return d_tokens, grad_inner, first_sum, outer, other_outer, own_out, sums
+        return d_tokens, outer, behind(shares, outer), sums
 
     operands = (d_heads, d_hidden, send_out, keep_out, second_part)
     shapes = jax.eval_shape(rest, *operands)
-    d_tokens, grad_inner, first_sum, own_outer, other_outer, own_out, sums = lax.cond(
+    d_tokens, outer, shares, sums = lax.cond(
         positions[0, 0] >= 0,
         rest,
         lambda *ignored: jax.tree.map(lambda leaf: jnp.zeros(leaf.shape, leaf.dtype), shapes),
         *operands,
     )
-    grad_gate, grad_up, grad_down = widen(core, grad_gate, grad_up, own_outer, other_outer)
+    kv_index = lax.axis_index("kv")
+    paths = [seq_order(at, seq_devices) for at in range(2)]
+    other_outer = swap(outer, "seq", 1)
+    grad_inner = jnp.concatenate(
+        [double_seq(shares[at], paths[at]) for at in range(2)], axis=0
+    ).astype(f32)
+    first_part = jnp.sum(w_t.astype(f32) * grad_inner, axis=0)
+    first_sum = sum_over(first_part, "kv") / norm_first
+    half_devices = kv_devices // 2
+    start = (expert_count // 2) * w_down.shape[1] + lax.rem(kv_index, half_devices) * query_cols
+    pieces = [
+        lax.dynamic_slice_in_dim(pair, start, query_cols, 0) for pair in (outer, other_outer)
+    ]
+    own_out = jnp.where(kv_index // half_devices == core_index, *pieces).astype(f32)
+    grad_gate, grad_up = widen_whole(grad_gate, grad_up)
+    grad_down = widen_halves(core, outer, other_outer, expert_count, w_down.shape[1])
     return (
         block_out.reshape(tokens.shape),
         d_tokens.reshape(tokens.shape),

time: 456 us -> 454 us (level)
  starting transfers between devices: 115 us -> 109 us
  other arithmetic: 34 us -> 38.6 us
    all_gather x1, waiting for transfers between devices: 0.02 us -> 38.1 us  [per_device(): w_inner_half = lax.all_gather(cut(w_t, core_index, inner_cols // 2), 'kv')]
    all_to_all x4, waiting for transfers between devices: 46.5 us -> 20.5 us  [exchange(): return lax.all_to_all(value, 'kv', 0, 0)]
    all_to_all x2, waiting for transfers between devices: 14.4 us -> 8.44 us  [over_chips(): return lax.all_to_all(value, 'seq', 0, 0, axis_index_groups=groups)]
    all_to_all x2, starting transfers between devices: 15.6 us -> 9.73 us  [over_chips(): return lax.all_to_all(value, 'seq', 0, 0, axis_index_groups=groups)]
    pallas_call x1 -> x2, Pallas kernels: 12.6 us -> 15.6 us  [the longest x1 9.28 us: widen_whole(): pl.pallas_call(widen_whole_kernel, grid=(experts,), in_specs=[spec, spec]...]
  transfers between devices with their start and end apart: 48 -> 48, of which waited for: 33 -> 28; matrix products, arithmetic and copies ran while one was open for 10% -> 11% of each run, Pallas kernels for 11% -> 14%
where the time goes in v5:
time: 454 us; the launch traced here: 447 us
  waiting for transfers between devices  198 us (44%)
  starting transfers between devices  109 us (24%)
  Pallas kernels  70.3 us (15%)
  other arithmetic  38.6 us (9%)
  local copies, waits for them, and re-layouts  15.7 us (3%)
  between operations  15.2 us (3%)
    ppermute x38, waiting for transfers between devices, swap(): lax.ppermute(value, axis, [(source, source ^ mask) for source in range(co...  85.6 us
    ppermute x38, starting transfers between devices, swap(): lax.ppermute(value, axis, [(source, source ^ mask) for source in range(co...  83.4 us
    all_gather x1, waiting for transfers between devices, per_device(): gathered = lax.all_gather(normed, 'kv', axis=1, tiled=True)  45.6 us
    all_gather x1, waiting for transfers between devices, per_device(): w_inner_half = lax.all_gather(cut(w_t, core_index, inner_cols // 2), 'kv')  38.1 us
    pallas_call x1, Pallas kernels, run_experts(): pl.pallas_call(functools.partial(experts_kernel, experts=experts), grid_s...  23.8 us
    all_to_all x4, waiting for transfers between devices, exchange(): return lax.all_to_all(value, 'kv', 0, 0)  20.5 us
    all_to_all x4, starting transfers between devices, exchange(): return lax.all_to_all(value, 'kv', 0, 0)  14.9 us
    pallas_call x2, Pallas kernels, attend_back(): pl.pallas_call(functools.partial(backward_kernel, row=row, group=group, o...  10.2 us
  transfers between devices with their start and end apart: 48, of which 28 were waited for; matrix products, arithmetic and copies ran while one was open for 11% of the time, Pallas kernels for 14%

profile of v5, /device:TPU:0, one launch (start us, length us, event | category | flops | bytes accessed | tf_op | source)
XLA Modules:
  0.0 447.5 jit_solution(8497271686806395149)
XLA Ops:
  13.8 45.6 %all-gather.6.cloned.1.call-done.n_ref = bf16[2,512,1024]{2,1,0:T(8,128)(2,1)} async-done(((bf16[2,128,1024]{2,1,0:T(8,128)(2,1)}), bf16[2,512,1024]{2,1,0:T(8,128)(2,1)}) %all-gather.6.cloned.1.call-update) | async-done | bytes 2097168 | tf_op jit(solution)/shard_map/all_gather | solution.py:762
  68.6 5.3 %collective-permute-done.21 = bf16[1,256,512]{2,1,0:T(8,128)(2,1)S(1)} collective-permute-done((bf16[1,256,512]{2,1,0:T(8,128)(2,1)}, bf16[1,256,512]{2,1,0:T(8,128)(2,1)S(1)}, u32[]{:S(2)}, u32[]{:S(2)}) %collective-permute-start.21) | collective-permute-done | bytes 262176 | tf_op jit(solution)/shard_map/ppermute | solution.py:53
  80.3 8.4 %collective-permute-done.22 = bf16[2,256,512]{2,1,0:T(8,128)(2,1)S(1)} collective-permute-done((bf16[2,256,512]{2,1,0:T(8,128)(2,1)}, bf16[2,256,512]{2,1,0:T(8,128)(2,1)S(1)}, u32[]{:S(2)}, u32[]{:S(2)}) %collective-permute-start.22) | collective-permute-done | bytes 524320 | tf_op jit(solution)/shard_map/ppermute | solution.py:53
  104.8 3.5 all-to-all-start.5
  108.9 38.1 %all-gather.10.cloned.1.call-done = bf16[1024,1024]{1,0:T(8,128)(2,1)} async-done(((bf16[256,1024]{1,0:T(8,128)(2,1)}), bf16[1024,1024]{1,0:T(8,128)(2,1)}) %all-gather.10.cloned.1.call-update) | async-done | bytes 2097168 | tf_op jit(solution)/shard_map/all_gather | solution.py:773
  148.8 23.8 %shard_map.233 = (bf16[256,1024]{1,0:T(8,128)(2,1)}, f32[256,1024]{1,0:T(8,128)}, bf16[4,1024,512]{2,1,0:T(8,128)(2,1)}, bf16[4,1024,512]{2,1,0:T(8,128)(2,1)}, ...) custom-call(s32[1]{0:T(128)} %bitcast.16.core_ref, ...), custom_call_target="tpu_custom_call" | custom-call | flops 9663676416 | bytes 25165824 | tf_op jit(solution)/shard_map/pallas_call | solution.py:517
  173.8 223.2 %conditional.1 = (bf16[1536,1024]{1,0:T(8,128)(2,1)}, bf16[32,1024]{1,0:T(8,128)(2,1)}, bf16[32,1024]{1,0:T(8,128)(2,1)}, f32[1028]{0:T(1024)}, bf16[2,128,1024]{2,1,0:T(8,128)(2,1)}) conditional(s32[]{:T(128)} %bitcast.37, () %tuple.30, (bf16[3,512,1024]{2,1,0:T(8,128)(2,1)}, bf16[3,512,1024]{2,1,0:T(8,128)(2,1)}, ...), branch_computations={%region_2.3_spmd, %region_3.7_spmd} | conditional | flops 23640193024 | bytes 161642848 | solution.py:875
  175.4 3.5 all-to-all-start.1
  189.7 7.5 %collective-permute-done.4 = f32[1028]{0:T(1024)S(1)} collective-permute-done((f32[1028]{0:T(1024)S(1)}, f32[1028]{0:T(1024)S(1)}, u32[]{:S(2)}, u32[]{:S(2)}) %collective-permute-start.4) | collective-permute-done | bytes 4144 | tf_op jit(solution)/shard_map/cond/branch_1_fun/ppermute | solution.py:53
  197.3 4.7 %collective-permute-start.5 = (f32[1028]{0:T(1024)S(1)}, f32[1028]{0:T(1024)S(1)}, u32[]{:S(2)}, u32[]{:S(2)}) collective-permute-start(f32[1028]{0:T(1024)S(1)} %add.98), channel_id=1, source_target_pairs={{0,2},{1,3},{2,0},{3,1},{4,6},{5,7},{6,4},{7,5},{8,10},{9,11},{10,... | collective-permute-start | bytes 12344 | tf_op jit(solution)/shard_map/cond/branch_1_fun/ppermute | solution.py:53
  204.6 6.3 %add_convert_fusion = bf16[3,512,1024]{2,1,0:T(8,128)(2,1)} fusion(bf16[3,512,1024]{2,1,0:T(8,128)(2,1)} %collective-permute-done, bf16[3,512,1024]{2,1,0:T(8,128)(2,1)} %get-tuple-element.51), kind=kLoop, calls=%fused_computation | loop fusion | flops 6291456 | bytes 9437184 | tf_op jit(solution)/shard_map/cond/branch_1_fun/convert_element_type | solution.py:117
  211.0 5.0 %all-to-all-start = ((bf16[4,384,1024]{2,1,0:T(8,128)(2,1)}), bf16[4,384,1024]{2,1,0:T(8,128)(2,1)}, u32[]{:S(2)}, u32[]{:S(2)}) async-start(bf16[4,384,1024]{2,1,0:T(8,128)(2,1)} %bitcast.56), calls=%async_computation | async-start | bytes 6291456 | tf_op jit(solution)/shard_map/cond/branch_1_fun/all_to_all | solution.py:822
  216.0 5.5 %branch_1_fun.4 = (bf16[256,512]{1,0:T(8,128)(2,1)S(1)}, bf16[8,256,512]{2,1,0:T(8,128)(2,1)S(1)}) custom-call(s32[5]{0:T(128)S(1)} %get-tuple-element.53.meta_ref, bf16[256,512]{1,0:T(8,128)(2,1)S(1)} %copy-done.31, bf16[4,2,256,128]{3,2,1,0:T(8,128)(2,1)S(1)} %all-to-all-done.1.do_ref, f32[256,512]{1,0:T(8,128)} %get-tuple-element.59.o_ref, ...), custom_call_target="tpu_custom_call" | custom-call | flops 10737418240 | bytes 4194304 | tf_op jit(solution)/shard_map/cond/branch_1_fun/pallas_call | solution.py:360
  224.0 4.7 %branch_1_fun.5 = (bf16[256,512]{1,0:T(8,128)(2,1)S(1)}, bf16[8,256,512]{2,1,0:T(8,128)(2,1)S(1)}) custom-call(s32[5]{0:T(128)S(1)} %get-tuple-element.53.meta_ref, bf16[256,512]{1,0:T(8,128)(2,1)S(1)} %copy-done.33, bf16[4,2,256,128]{3,2,1,0:T(8,128)(2,1)S(1)} %all-to-all-done.1.do_ref, f32[256,512]{1,0:T(8,128)S(1)} %copy-done.34, ...), custom_call_target="tpu_custom_call" | custom-call | flops 10737418240 | bytes 4194304 | tf_op jit(solution)/shard_map/cond/branch_1_fun/pallas_call | solution.py:360
  228.8 5.1 %collective-permute-start.9 = (bf16[4,256,512]{2,1,0:T(8,128)(2,1)S(1)}, bf16[4,256,512]{2,1,0:T(8,128)(2,1)S(1)}, u32[]{:S(2)}, u32[]{:S(2)}) collective-permute-start(bf16[4,256,512]{2,1,0:T(8,128)(2,1)S(1)} %slice.81), channel_id=1, source_target_pairs={{0,4},{4,0},{8,12},{12,8},{16,20},{20,16},{24,28},{28,24},{1,5},{5... | collective-permute-start | bytes 3145736 | tf_op jit(solution)/shard_map/cond/branch_1_fun/ppermute | solution.py:53
  234.3 5.2 %collective-permute-start.7 = (bf16[2,256,512]{2,1,0:T(8,128)(2,1)S(1)}, bf16[2,256,512]{2,1,0:T(8,128)(2,1)}, u32[]{:S(2)}, u32[]{:S(2)}) collective-permute-start(bf16[2,256,512]{2,1,0:T(8,128)(2,1)S(1)} %slice.123), channel_id=1, source_target_pairs={{0,8},{4,12},{8,0},{12,4},{16,24},{20,28},{24,16},{28,20},{1,9},{5... | collective-permute-start | bytes 1572872 | tf_op jit(solution)/shard_map/cond/branch_1_fun/ppermute | solution.py:53
  240.6 30.1 %collective-permute-start.10 = (bf16[2,256,512]{2,1,0:T(8,128)(2,1)}, bf16[2,256,512]{2,1,0:T(8,128)(2,1)}, u32[]{:S(2)}, u32[]{:S(2)}) collective-permute-start(bf16[2,256,512]{2,1,0:T(8,128)(2,1)} %slice.127), channel_id=1, source_target_pairs={{0,16},{4,20},{8,24},{12,28},{16,0},{20,4},{24,8},{28,12},{1,17},{... | collective-permute-start | bytes 1572872 | tf_op jit(solution)/shard_map/cond/branch_1_fun/ppermute | solution.py:53
  270.7 3.6 reduce_sum.56
  274.3 4.4 all-to-all-start.2
  279.9 4.5 %collective-permute-start.8 = (bf16[1,256,512]{2,1,0:T(8,128)(2,1)S(1)}, bf16[1,256,512]{2,1,0:T(8,128)(2,1)S(1)}, u32[]{:S(2)}, u32[]{:S(2)}) collective-permute-start(bf16[1,256,512]{2,1,0:T(8,128)(2,1)S(1)} %slice.125), channel_id=1, source_target_pairs={{0,16},{4,20},{8,24},{12,28},{16,0},{20,4},{24,8},{28,12},{1,17},{... | collective-permute-start | bytes 786440 | tf_op jit(solution)/shard_map/cond/branch_1_fun/ppermute | solution.py:53
  293.9 8.8 %all-to-all-done.2 = bf16[4,96,1024]{2,1,0:T(8,128)(2,1)} async-done(((bf16[4,96,1024]{2,1,0:T(8,128)(2,1)}), bf16[4,96,1024]{2,1,0:T(8,128)(2,1)}, u32[]{:S(2)}, u32[]{:S(2)}) %all-to-all-start.2) | async-done | bytes 786464 | tf_op jit(solution)/shard_map/cond/branch_1_fun/all_to_all | solution.py:777
  309.3 3.5 all-to-all-start.3
  317.1 5.6 %collective-permute-done.13 = bf16[64,1024]{1,0:T(8,128)(2,1)S(1)} collective-permute-done((bf16[64,1024]{1,0:T(8,128)(2,1)S(1)}, bf16[64,1024]{1,0:T(8,128)(2,1)S(1)}, u32[]{:S(2)}, u32[]{:S(2)}) %collective-permute-start.13) | collective-permute-done | bytes 131104 | tf_op jit(solution)/shard_map/cond/branch_1_fun/ppermute | solution.py:53
  329.3 11.7 %all-to-all-done.3 = bf16[4,96,1024]{2,1,0:T(8,128)(2,1)S(1)} async-done(((bf16[4,96,1024]{2,1,0:T(8,128)(2,1)}), bf16[4,96,1024]{2,1,0:T(8,128)(2,1)S(1)}, u32[]{:S(2)}, u32[]{:S(2)}) %all-to-all-start.3) | async-done | bytes 786464 | tf_op jit(solution)/shard_map/cond/branch_1_fun/all_to_all | solution.py:777
  343.1 4.7 %all-to-all-start.4 = ((bf16[4,384,1024]{2,1,0:T(8,128)(2,1)}), bf16[4,384,1024]{2,1,0:T(8,128)(2,1)}, u32[]{:S(2)}, u32[]{:S(2)}) async-start(bf16[4,384,1024]{2,1,0:T(8,128)(2,1)} %broadcast_in_dim.1), calls=%async_computation.4 | async-start | bytes 6291456 | tf_op jit(solution)/shard_map/cond/branch_1_fun/all_to_all | solution.py:822
  352.5 15.4 %collective-permute-done.18.refs_1_ = bf16[2,256,256]{2,1,0:T(8,128)(2,1)S(1)} collective-permute-done((bf16[2,256,256]{2,1,0:T(8,128)(2,1)S(1)}, bf16[2,256,256]{2,1,0:T(8,128)(2,1)S(1)}, u32[]{:S(2)}, u32[]{:S(2)}) %collective-permute-start.18) | collective-permute-done | bytes 262176 | tf_op jit(solution)/shard_map/cond/branch_1_fun/ppermute | solution.py:53
  367.9 3.7 collective-permute-done.19.refs_2_
  371.6 12.3 %collective-permute-done.20.refs_3_ = bf16[2,256,256]{2,1,0:T(8,128)(2,1)S(1)} collective-permute-done((bf16[2,256,256]{2,1,0:T(8,128)(2,1)S(1)}, bf16[2,256,256]{2,1,0:T(8,128)(2,1)S(1)}, u32[]{:S(2)}, u32[]{:S(2)}) %collective-permute-start.20) | collective-permute-done | bytes 262176 | tf_op jit(solution)/shard_map/cond/branch_1_fun/ppermute | solution.py:53
  383.9 4.5 %branch_1_fun.7 = bf16[256,1024]{1,0:T(8,128)(2,1)} custom-call(s32[2]{0:T(128)S(1)} %pad_add_fusion.place_ref, bf16[2,256,256]{2,1,0:T(8,128)(2,1)S(1)} %get-tuple-element.203.refs_0_, bf16[2,256,256]{2,1,0:T(8,128)(2,1)S(1)} %collective-permute-done.18.refs_1_, bf16[2,256,256]{2,1,0:T(8,128)(2,1)S(1)} %collective-permute-done.19.refs_2_, ...), custom_call_target="tpu_custom_call" | custom-call | flops 1073741824 | bytes 4194304 | tf_op jit(solution)/shard_map/cond/branch_1_fun/pallas_call | solution.py:648
  388.4 8.4 %all-to-all-done.4 = bf16[4,384,1024]{2,1,0:T(8,128)(2,1)} async-done(((bf16[4,384,1024]{2,1,0:T(8,128)(2,1)}), bf16[4,384,1024]{2,1,0:T(8,128)(2,1)}, u32[]{:S(2)}, u32[]{:S(2)}) %all-to-all-start.4) | async-done | bytes 3145760 | tf_op jit(solution)/shard_map/cond/branch_1_fun/all_to_all | solution.py:822
  422.7 6.4 %shard_map.235 = f32[4,512,1024]{2,1,0:T(8,128)} custom-call(s32[1]{0:T(128)} %bitcast.16.core_ref, bf16[1536,1024]{1,0:T(8,128)(2,1)} %get-tuple-element.154.own_ref, bf16[1536,1024]{1,0:T(8,128)(2,1)} %collective-permute-done.37.other_ref), custom_call_target="tpu_custom_call" | custom-call | bytes 12582912 | tf_op jit(solution)/shard_map/pallas_call | solution.py:694
  431.4 9.3 %shard_map.234 = (f32[4,1024,512]{2,1,0:T(8,128)}, f32[4,1024,512]{2,1,0:T(8,128)}) custom-call(bf16[4,1024,512]{2,1,0:T(8,128)(2,1)} %get-tuple-element.196.gate_ref, bf16[4,1024,512]{2,1,0:T(8,128)(2,1)} %get-tuple-element.197.up_ref), custom_call_target="tpu_custom_call" | custom-call | bytes 25165824 | tf_op jit(solution)/shard_map/pallas_call | solution.py:668
  (237 shorter events, 122.6 us)
Async XLA Ops:
  7.2 52.2 %all-gather.6.cloned.1.call-start = ((), (), s32[]{:S(2)}) async-start(), calls=%async_computation.6 | async-start | bytes 2621440 | tf_op jit(solution)/shard_map/all_gather | solution.py:762
  10.7 81.5 %all-gather.8.cloned.1.call-start = ((), (), s32[]{:S(2)}) async-start(), calls=%async_computation.7 | async-start | bytes 1310720 | tf_op jit(solution)/shard_map/all_gather | solution.py:771
  11.5 135.5 %all-gather.10.cloned.1.call-start = ((), (), s32[]{:S(2)}) async-start(), calls=%async_computation.8 | async-start | bytes 2621440 | tf_op jit(solution)/shard_map/all_gather | solution.py:773
  65.6 8.2 %collective-permute-start.21 = (bf16[1,256,512]{2,1,0:T(8,128)(2,1)}, bf16[1,256,512]{2,1,0:T(8,128)(2,1)S(1)}, u32[]{:S(2)}, u32[]{:S(2)}) collective-permute-start(bf16[1,256,512]{2,1,0:T(8,128)(2,1)} %bitcast.66), channel_id=1, source_target_pairs={{0,8},{4,12},{8,0},{12,4},{16,24},{20,28},{24,16},{28,20},{1,9},{5... | collective-permute-start | bytes 786440 | tf_op jit(solution)/shard_map/ppermute | solution.py:53
  67.1 10.0 %collective-permute-start.24 = (bf16[1,256,512]{2,1,0:T(8,128)(2,1)S(1)}, bf16[1,256,512]{2,1,0:T(8,128)(2,1)S(1)}, u32[]{:S(2)}, u32[]{:S(2)}) collective-permute-start(bf16[1,256,512]{2,1,0:T(8,128)(2,1)S(1)} %bitcast.62), channel_id=1, source_target_pairs={{0,16},{4,20},{8,24},{12,28},{16,0},{20,4},{24,8},{28,12},{1,17},{... | collective-permute-start | bytes 786440 | tf_op jit(solution)/shard_map/ppermute | solution.py:53
  75.7 13.0 %collective-permute-start.22 = (bf16[2,256,512]{2,1,0:T(8,128)(2,1)}, bf16[2,256,512]{2,1,0:T(8,128)(2,1)S(1)}, u32[]{:S(2)}, u32[]{:S(2)}) collective-permute-start(bf16[2,256,512]{2,1,0:T(8,128)(2,1)} %pad_maximum_fusion.6), channel_id=1, source_target_pairs={{0,16},{4,20},{8,24},{12,28},{16,0},{20,4},{24,8},{28,12},{1,17},{... | collective-permute-start | bytes 1572872 | tf_op jit(solution)/shard_map/ppermute | solution.py:53
  78.0 12.8 %collective-permute-start.25 = (bf16[2,256,512]{2,1,0:T(8,128)(2,1)}, bf16[2,256,512]{2,1,0:T(8,128)(2,1)S(1)}, u32[]{:S(2)}, u32[]{:S(2)}) collective-permute-start(bf16[2,256,512]{2,1,0:T(8,128)(2,1)} %pad_maximum_fusion.7), channel_id=1, source_target_pairs={{0,8},{4,12},{8,0},{12,4},{16,24},{20,28},{24,16},{28,20},{1,9},{5... | collective-permute-start | bytes 1572872 | tf_op jit(solution)/shard_map/ppermute | solution.py:53
  92.1 55.9 %collective-permute-start.27 = (bf16[4,128,1024]{2,1,0:T(8,128)(2,1)}, bf16[4,128,1024]{2,1,0:T(8,128)(2,1)}, u32[]{:S(2)}, u32[]{:S(2)}) collective-permute-start(bf16[4,128,1024]{2,1,0:T(8,128)(2,1)} %bitcast.84), channel_id=1, source_target_pairs={{0,4},{4,0},{8,12},{12,8},{16,20},{20,16},{24,28},{28,24},{1,5},{5... | collective-permute-start | bytes 3145736 | tf_op jit(solution)/shard_map/ppermute | solution.py:53
  104.8 43.2 %all-to-all-start.5 = ((bf16[4,2,256,128]{3,2,1,0:T(8,128)(2,1)}), bf16[4,2,256,128]{3,2,1,0:T(8,128)(2,1)S(1)}, u32[]{:S(2)}, u32[]{:S(2)}) async-start(bf16[4,2,256,128]{3,2,1,0:T(8,128)(2,1)} %pad_maximum_fusion.8), calls=%async_computation.5 | async-start | bytes 1048576 | tf_op jit(solution)/shard_map/all_to_all | solution.py:777
  108.3 323.1 %all-reduce.3.cloned.1.call-start = ((), (), s32[]{:S(2)}) async-start(), calls=%async_computation.9 | async-start | bytes 16777216 | tf_op jit(solution)/shard_map/psum | solution.py:816
  147.0 26.9 %collective-permute-start.28 = (bf16[4,256,1024]{2,1,0:T(8,128)(2,1)}, bf16[4,256,1024]{2,1,0:T(8,128)(2,1)S(1)}, u32[]{:S(2)}, u32[]{:S(2)}) collective-permute-start(bf16[4,256,1024]{2,1,0:T(8,128)(2,1)} %bitcast.74), channel_id=1, source_target_pairs={{0,4},{4,0},{8,12},{12,8},{16,20},{20,16},{24,28},{28,24},{1,5},{5... | collective-permute-start | bytes 6291464 | tf_op jit(solution)/shard_map/ppermute | solution.py:53
  173.9 30.7 %collective-permute-start = (bf16[3,512,1024]{2,1,0:T(8,128)(2,1)}, bf16[3,512,1024]{2,1,0:T(8,128)(2,1)}, u32[]{:S(2)}, u32[]{:S(2)}) collective-permute-start(bf16[3,512,1024]{2,1,0:T(8,128)(2,1)} %get-tuple-element.52), channel_id=1, source_target_pairs={{0,4},{4,0},{8,12},{12,8},{16,20},{20,16},{24,28},{28,24},{1,5},{5... | collective-permute-start | bytes 9437192 | tf_op jit(solution)/shard_map/cond/branch_1_fun/ppermute | solution.py:53
  175.4 35.6 %all-to-all-start.1 = ((bf16[4,2,256,128]{3,2,1,0:T(8,128)(2,1)}), bf16[4,2,256,128]{3,2,1,0:T(8,128)(2,1)S(1)}, u32[]{:S(2)}, u32[]{:S(2)}) async-start(bf16[4,2,256,128]{3,2,1,0:T(8,128)(2,1)} %get-tuple-element.55), calls=%async_computation.1 | async-start | bytes 1048576 | tf_op jit(solution)/shard_map/cond/branch_1_fun/all_to_all | solution.py:777
  187.9 9.4 %collective-permute-start.4 = (f32[1028]{0:T(1024)S(1)}, f32[1028]{0:T(1024)S(1)}, u32[]{:S(2)}, u32[]{:S(2)}) collective-permute-start(f32[1028]{0:T(1024)S(1)} %add.97), channel_id=1, source_target_pairs={{0,1},{1,0},{2,3},{3,2},{4,5},{5,4},{6,7},{7,6},{8,9},{9,8},{10,11... | collective-permute-start | bytes 12344 | tf_op jit(solution)/shard_map/cond/branch_1_fun/ppermute | solution.py:53
  197.3 6.8 %collective-permute-start.5 = (f32[1028]{0:T(1024)S(1)}, f32[1028]{0:T(1024)S(1)}, u32[]{:S(2)}, u32[]{:S(2)}) collective-permute-start(f32[1028]{0:T(1024)S(1)} %add.98), channel_id=1, source_target_pairs={{0,2},{1,3},{2,0},{3,1},{4,6},{5,7},{6,4},{7,5},{8,10},{9,11},{10,... | collective-permute-start | bytes 12344 | tf_op jit(solution)/shard_map/cond/branch_1_fun/ppermute | solution.py:53
  211.0 59.7 %all-to-all-start = ((bf16[4,384,1024]{2,1,0:T(8,128)(2,1)}), bf16[4,384,1024]{2,1,0:T(8,128)(2,1)}, u32[]{:S(2)}, u32[]{:S(2)}) async-start(bf16[4,384,1024]{2,1,0:T(8,128)(2,1)} %bitcast.56), calls=%async_computation | async-start | bytes 6291456 | tf_op jit(solution)/shard_map/cond/branch_1_fun/all_to_all | solution.py:822
  221.6 12.3 %collective-permute-start.6 = (bf16[4,256,512]{2,1,0:T(8,128)(2,1)S(1)}, bf16[4,256,512]{2,1,0:T(8,128)(2,1)S(1)}, u32[]{:S(2)}, u32[]{:S(2)}) collective-permute-start(bf16[4,256,512]{2,1,0:T(8,128)(2,1)S(1)} %slice.23), channel_id=1, source_target_pairs={{0,4},{4,0},{8,12},{12,8},{16,20},{20,16},{24,28},{28,24},{1,5},{5... | collective-permute-start | bytes 3145736 | tf_op jit(solution)/shard_map/cond/branch_1_fun/ppermute | solution.py:53
  228.8 10.6 %collective-permute-start.9 = (bf16[4,256,512]{2,1,0:T(8,128)(2,1)S(1)}, bf16[4,256,512]{2,1,0:T(8,128)(2,1)S(1)}, u32[]{:S(2)}, u32[]{:S(2)}) collective-permute-start(bf16[4,256,512]{2,1,0:T(8,128)(2,1)S(1)} %slice.81), channel_id=1, source_target_pairs={{0,4},{4,0},{8,12},{12,8},{16,20},{20,16},{24,28},{28,24},{1,5},{5... | collective-permute-start | bytes 3145736 | tf_op jit(solution)/shard_map/cond/branch_1_fun/ppermute | solution.py:53
  234.3 44.5 %collective-permute-start.7 = (bf16[2,256,512]{2,1,0:T(8,128)(2,1)S(1)}, bf16[2,256,512]{2,1,0:T(8,128)(2,1)}, u32[]{:S(2)}, u32[]{:S(2)}) collective-permute-start(bf16[2,256,512]{2,1,0:T(8,128)(2,1)S(1)} %slice.123), channel_id=1, source_target_pairs={{0,8},{4,12},{8,0},{12,4},{16,24},{20,28},{24,16},{28,20},{1,9},{5... | collective-permute-start | bytes 1572872 | tf_op jit(solution)/shard_map/cond/branch_1_fun/ppermute | solution.py:53
  240.6 44.0 %collective-permute-start.10 = (bf16[2,256,512]{2,1,0:T(8,128)(2,1)}, bf16[2,256,512]{2,1,0:T(8,128)(2,1)}, u32[]{:S(2)}, u32[]{:S(2)}) collective-permute-start(bf16[2,256,512]{2,1,0:T(8,128)(2,1)} %slice.127), channel_id=1, source_target_pairs={{0,16},{4,20},{8,24},{12,28},{16,0},{20,4},{24,8},{28,12},{1,17},{... | collective-permute-start | bytes 1572872 | tf_op jit(solution)/shard_map/cond/branch_1_fun/ppermute | solution.py:53
  274.3 28.4 %all-to-all-start.2 = ((bf16[4,96,1024]{2,1,0:T(8,128)(2,1)}), bf16[4,96,1024]{2,1,0:T(8,128)(2,1)}, u32[]{:S(2)}, u32[]{:S(2)}) async-start(bf16[4,96,1024]{2,1,0:T(8,128)(2,1)} %bitcast.2), calls=%async_computation.2 | async-start | bytes 1572864 | tf_op jit(solution)/shard_map/cond/branch_1_fun/all_to_all | solution.py:777
  279.9 10.5 %collective-permute-start.8 = (bf16[1,256,512]{2,1,0:T(8,128)(2,1)S(1)}, bf16[1,256,512]{2,1,0:T(8,128)(2,1)S(1)}, u32[]{:S(2)}, u32[]{:S(2)}) collective-permute-start(bf16[1,256,512]{2,1,0:T(8,128)(2,1)S(1)} %slice.125), channel_id=1, source_target_pairs={{0,16},{4,20},{8,24},{12,28},{16,0},{20,4},{24,8},{28,12},{1,17},{... | collective-permute-start | bytes 786440 | tf_op jit(solution)/shard_map/cond/branch_1_fun/ppermute | solution.py:53
  285.8 8.0 %collective-permute-start.11 = (bf16[1,256,512]{2,1,0:T(8,128)(2,1)S(1)}, bf16[1,256,512]{2,1,0:T(8,128)(2,1)S(1)}, u32[]{:S(2)}, u32[]{:S(2)}) collective-permute-start(bf16[1,256,512]{2,1,0:T(8,128)(2,1)S(1)} %slice.129), channel_id=1, source_target_pairs={{0,8},{4,12},{8,0},{12,4},{16,24},{20,28},{24,16},{28,20},{1,9},{5... | collective-permute-start | bytes 786440 | tf_op jit(solution)/shard_map/cond/branch_1_fun/ppermute | solution.py:53
  309.3 31.8 %all-to-all-start.3 = ((bf16[4,96,1024]{2,1,0:T(8,128)(2,1)}), bf16[4,96,1024]{2,1,0:T(8,128)(2,1)S(1)}, u32[]{:S(2)}, u32[]{:S(2)}) async-start(bf16[4,96,1024]{2,1,0:T(8,128)(2,1)} %broadcast_in_dim.0), calls=%async_computation.3 | async-start | bytes 1572864 | tf_op jit(solution)/shard_map/cond/branch_1_fun/all_to_all | solution.py:777
  314.9 7.8 %collective-permute-start.13 = (bf16[64,1024]{1,0:T(8,128)(2,1)S(1)}, bf16[64,1024]{1,0:T(8,128)(2,1)S(1)}, u32[]{:S(2)}, u32[]{:S(2)}) collective-permute-start(bf16[64,1024]{1,0:T(8,128)(2,1)S(1)} %broadcast_select_fusion.3), channel_id=1, source_target_pairs={{0,16},{4,20},{8,24},{12,28},{16,0},{20,4},{24,8},{28,12},{1,17},{... | collective-permute-start | bytes 393224 | tf_op jit(solution)/shard_map/cond/branch_1_fun/ppermute | solution.py:53
  315.0 9.3 %collective-permute-start.16 = (bf16[64,1024]{1,0:T(8,128)(2,1)S(1)}, bf16[64,1024]{1,0:T(8,128)(2,1)S(1)}, u32[]{:S(2)}, u32[]{:S(2)}) collective-permute-start(bf16[64,1024]{1,0:T(8,128)(2,1)S(1)} %broadcast_select_fusion.2), channel_id=1, source_target_pairs={{0,8},{4,12},{8,0},{12,4},{16,24},{20,28},{24,16},{28,20},{1,9},{5... | collective-permute-start | bytes 393224 | tf_op jit(solution)/shard_map/cond/branch_1_fun/ppermute | solution.py:53
  343.1 53.7 %all-to-all-start.4 = ((bf16[4,384,1024]{2,1,0:T(8,128)(2,1)}), bf16[4,384,1024]{2,1,0:T(8,128)(2,1)}, u32[]{:S(2)}, u32[]{:S(2)}) async-start(bf16[4,384,1024]{2,1,0:T(8,128)(2,1)} %broadcast_in_dim.1), calls=%async_computation.4 | async-start | bytes 6291456 | tf_op jit(solution)/shard_map/cond/branch_1_fun/all_to_all | solution.py:822
  348.0 19.9 %collective-permute-start.18 = (bf16[2,256,256]{2,1,0:T(8,128)(2,1)S(1)}, bf16[2,256,256]{2,1,0:T(8,128)(2,1)S(1)}, u32[]{:S(2)}, u32[]{:S(2)}) collective-permute-start(bf16[2,256,256]{2,1,0:T(8,128)(2,1)S(1)} %get-tuple-element.202), channel_id=1, source_target_pairs={{0,1},{1,0},{2,3},{3,2},{4,5},{5,4},{6,7},{7,6},{8,9},{9,8},{10,11... | collective-permute-start | bytes 786440 | tf_op jit(solution)/shard_map/cond/branch_1_fun/ppermute | solution.py:53
  348.1 23.5 %collective-permute-start.19 = (bf16[2,256,256]{2,1,0:T(8,128)(2,1)S(1)}, bf16[2,256,256]{2,1,0:T(8,128)(2,1)S(1)}, u32[]{:S(2)}, u32[]{:S(2)}) collective-permute-start(bf16[2,256,256]{2,1,0:T(8,128)(2,1)S(1)} %get-tuple-element.201), channel_id=1, source_target_pairs={{0,2},{1,3},{2,0},{3,1},{4,6},{5,7},{6,4},{7,5},{8,10},{9,11},{10,... | collective-permute-start | bytes 786440 | tf_op jit(solution)/shard_map/cond/branch_1_fun/ppermute | solution.py:53
  349.6 34.3 %collective-permute-start.20 = (bf16[2,256,256]{2,1,0:T(8,128)(2,1)S(1)}, bf16[2,256,256]{2,1,0:T(8,128)(2,1)S(1)}, u32[]{:S(2)}, u32[]{:S(2)}) collective-permute-start(bf16[2,256,256]{2,1,0:T(8,128)(2,1)S(1)} %get-tuple-element.200), channel_id=1, source_target_pairs={{0,3},{1,2},{2,1},{3,0},{4,7},{5,6},{6,5},{7,4},{8,11},{9,10},{10,... | collective-permute-start | bytes 786440 | tf_op jit(solution)/shard_map/cond/branch_1_fun/ppermute | solution.py:53
  397.1 25.6 %collective-permute-start.37 = (bf16[1536,1024]{1,0:T(8,128)(2,1)}, bf16[1536,1024]{1,0:T(8,128)(2,1)}, u32[]{:S(2)}, u32[]{:S(2)}) collective-permute-start(bf16[1536,1024]{1,0:T(8,128)(2,1)} %get-tuple-element.154.own_ref), channel_id=1, source_target_pairs={{0,4},{4,0},{8,12},{12,8},{16,20},{20,16},{24,28},{28,24},{1,5},{5... | collective-permute-start | bytes 9437192 | tf_op jit(solution)/shard_map/ppermute | solution.py:53
  416.3 5.8 %collective-permute-start.36 = (f32[1024]{0:T(1024)S(1)}, f32[1024]{0:T(1024)S(1)}, u32[]{:S(2)}, u32[]{:S(2)}) collective-permute-start(f32[1024]{0:T(1024)S(1)} %add.133), channel_id=1, source_target_pairs={{0,2},{1,3},{2,0},{3,1},{4,6},{5,7},{6,4},{7,5},{8,10},{9,11},{10,... | collective-permute-start | bytes 12296 | tf_op jit(solution)/shard_map/ppermute | solution.py:53
  (51 other events, 631.6 us)
Sparse Core Ops, SparseCore 0:
  10.8 48.6 all-gather.5
  61.6 26.6 all-gather.7
  90.4 56.4 all-gather.9
  172.8 235.3 all-reduce.2

commit v6 on v5

--- a/solution.py
+++ b/solution.py
@@ -884,7 +884,8 @@
     grad_inner = jnp.concatenate(
         [double_seq(shares[at], paths[at]) for at in range(2)], axis=0
     ).astype(f32)
-    first_part = jnp.sum(w_t.astype(f32) * grad_inner, axis=0)
+    grad_gate, grad_up = widen_whole(grad_gate, grad_up)
+    first_part = jnp.sum(w_t.astype(f32) * behind(grad_inner, grad_gate), axis=0)
     first_sum = sum_over(first_part, "kv") / norm_first
     half_devices = kv_devices // 2
     start = (expert_count // 2) * w_down.shape[1] + lax.rem(kv_index, half_devices) * query_cols
@@ -892,7 +893,6 @@
         lax.dynamic_slice_in_dim(pair, start, query_cols, 0) for pair in (outer, other_outer)
     ]
     own_out = jnp.where(kv_index // half_devices == core_index, *pieces).astype(f32)
-    grad_gate, grad_up = widen_whole(grad_gate, grad_up)
     grad_down = widen_halves(core, outer, other_outer, expert_count, w_down.shape[1])
     return (
         block_out.reshape(tokens.shape),

time: 454 us -> 453 us (level)
  waiting for transfers between devices: 198 us -> 193 us
    ppermute x38, starting transfers between devices: 83.4 us -> 88.2 us  [swap(): lax.ppermute(value, axis, [(source, source ^ mask) for source in range(co...]
  transfers between devices with their start and end apart: 48 -> 48, of which waited for: 28 -> 26; matrix products, arithmetic and copies ran while one was open for 11% -> 11% of each run, Pallas kernels for 14% -> 16%
where the time goes in v6:
time: 453 us; the launch traced here: 449 us
  waiting for transfers between devices  193 us (43%)
  starting transfers between devices  113 us (25%)
  Pallas kernels  70.4 us (16%)
  other arithmetic  38.5 us (8%)
  local copies, waits for them, and re-layouts  17.9 us (4%)
  between operations  15.2 us (3%)
    ppermute x38, starting transfers between devices, swap(): lax.ppermute(value, axis, [(source, source ^ mask) for source in range(co...  88.2 us
    ppermute x38, waiting for transfers between devices, swap(): lax.ppermute(value, axis, [(source, source ^ mask) for source in range(co...  82.4 us
    all_gather x1, waiting for transfers between devices, per_device(): gathered = lax.all_gather(normed, 'kv', axis=1, tiled=True)  45.6 us
    all_gather x1, waiting for transfers between devices, per_device(): w_inner_half = lax.all_gather(cut(w_t, core_index, inner_cols // 2), 'kv')  37 us
    pallas_call x1, Pallas kernels, run_experts(): pl.pallas_call(functools.partial(experts_kernel, experts=experts), grid_s...  23.8 us
    all_to_all x4, waiting for transfers between devices, exchange(): return lax.all_to_all(value, 'kv', 0, 0)  20.8 us
    all_to_all x4, starting transfers between devices, exchange(): return lax.all_to_all(value, 'kv', 0, 0)  14.8 us
    pallas_call x2, Pallas kernels, attend_back(): pl.pallas_call(functools.partial(backward_kernel, row=row, group=group, o...  10.2 us
  transfers between devices with their start and end apart: 48, of which 26 were waited for; matrix products, arithmetic and copies ran while one was open for 11% of the time, Pallas kernels for 16%

profile of v6, /device:TPU:0, one launch (start us, length us, event | category | flops | bytes accessed | tf_op | source)
XLA Modules:
  0.0 448.8 jit_solution(15998237960160580307)
XLA Ops:
  13.8 45.6 %all-gather.6.cloned.1.call-done.n_ref = bf16[2,512,1024]{2,1,0:T(8,128)(2,1)} async-done(((bf16[2,128,1024]{2,1,0:T(8,128)(2,1)}), bf16[2,512,1024]{2,1,0:T(8,128)(2,1)}) %all-gather.6.cloned.1.call-update) | async-done | bytes 2097168 | tf_op jit(solution)/shard_map/all_gather | solution.py:762
  68.6 5.3 %collective-permute-done.21 = bf16[1,256,512]{2,1,0:T(8,128)(2,1)S(1)} collective-permute-done((bf16[1,256,512]{2,1,0:T(8,128)(2,1)}, bf16[1,256,512]{2,1,0:T(8,128)(2,1)S(1)}, u32[]{:S(2)}, u32[]{:S(2)}) %collective-permute-start.21) | collective-permute-done | bytes 262176 | tf_op jit(solution)/shard_map/ppermute | solution.py:53
  80.3 8.4 %collective-permute-done.22 = bf16[2,256,512]{2,1,0:T(8,128)(2,1)S(1)} collective-permute-done((bf16[2,256,512]{2,1,0:T(8,128)(2,1)}, bf16[2,256,512]{2,1,0:T(8,128)(2,1)S(1)}, u32[]{:S(2)}, u32[]{:S(2)}) %collective-permute-start.22) | collective-permute-done | bytes 524320 | tf_op jit(solution)/shard_map/ppermute | solution.py:53
  96.4 3.5 shard_map.232
  104.8 3.5 all-to-all-start.5
  109.9 37.0 %all-gather.10.cloned.1.call-done = bf16[1024,1024]{1,0:T(8,128)(2,1)} async-done(((bf16[256,1024]{1,0:T(8,128)(2,1)}), bf16[1024,1024]{1,0:T(8,128)(2,1)}) %all-gather.10.cloned.1.call-update) | async-done | bytes 2097168 | tf_op jit(solution)/shard_map/all_gather | solution.py:773
  147.8 23.8 %shard_map.233 = (bf16[256,1024]{1,0:T(8,128)(2,1)}, f32[256,1024]{1,0:T(8,128)}, bf16[4,1024,512]{2,1,0:T(8,128)(2,1)}, bf16[4,1024,512]{2,1,0:T(8,128)(2,1)}, ...) custom-call(s32[1]{0:T(128)} %bitcast.16.core_ref, ...), custom_call_target="tpu_custom_call" | custom-call | flops 9663676416 | bytes 25165824 | tf_op jit(solution)/shard_map/pallas_call | solution.py:517
  172.8 225.2 %conditional.1 = (bf16[1536,1024]{1,0:T(8,128)(2,1)}, bf16[32,1024]{1,0:T(8,128)(2,1)}, bf16[32,1024]{1,0:T(8,128)(2,1)}, f32[1028]{0:T(1024)}, bf16[2,128,1024]{2,1,0:T(8,128)(2,1)}) conditional(s32[]{:T(128)} %bitcast.37, () %tuple.31, (bf16[3,512,1024]{2,1,0:T(8,128)(2,1)}, bf16[3,512,1024]{2,1,0:T(8,128)(2,1)}, ...), branch_computations={%region_2.3_spmd, %region_3.7_spmd} | conditional | flops 23640193024 | bytes 161642848 | solution.py:875
  174.3 3.5 all-to-all-start.1
  188.6 7.6 %collective-permute-done.4 = f32[1028]{0:T(1024)S(1)} collective-permute-done((f32[1028]{0:T(1024)S(1)}, f32[1028]{0:T(1024)S(1)}, u32[]{:S(2)}, u32[]{:S(2)}) %collective-permute-start.4) | collective-permute-done | bytes 4144 | tf_op jit(solution)/shard_map/cond/branch_1_fun/ppermute | solution.py:53
  196.2 4.7 %collective-permute-start.5 = (f32[1028]{0:T(1024)S(1)}, f32[1028]{0:T(1024)S(1)}, u32[]{:S(2)}, u32[]{:S(2)}) collective-permute-start(f32[1028]{0:T(1024)S(1)} %add.98), channel_id=1, source_target_pairs={{0,2},{1,3},{2,0},{3,1},{4,6},{5,7},{6,4},{7,5},{8,10},{9,11},{10,... | collective-permute-start | bytes 12344 | tf_op jit(solution)/shard_map/cond/branch_1_fun/ppermute | solution.py:53
  203.6 6.3 %add_convert_fusion = bf16[3,512,1024]{2,1,0:T(8,128)(2,1)} fusion(bf16[3,512,1024]{2,1,0:T(8,128)(2,1)} %collective-permute-done, bf16[3,512,1024]{2,1,0:T(8,128)(2,1)} %get-tuple-element.51), kind=kLoop, calls=%fused_computation | loop fusion | flops 6291456 | bytes 9437184 | tf_op jit(solution)/shard_map/cond/branch_1_fun/convert_element_type | solution.py:117
  209.9 5.0 %all-to-all-start = ((bf16[4,384,1024]{2,1,0:T(8,128)(2,1)}), bf16[4,384,1024]{2,1,0:T(8,128)(2,1)}, u32[]{:S(2)}, u32[]{:S(2)}) async-start(bf16[4,384,1024]{2,1,0:T(8,128)(2,1)} %bitcast.56), calls=%async_computation | async-start | bytes 6291456 | tf_op jit(solution)/shard_map/cond/branch_1_fun/all_to_all | solution.py:822
  214.9 5.5 %branch_1_fun.4 = (bf16[256,512]{1,0:T(8,128)(2,1)S(1)}, bf16[8,256,512]{2,1,0:T(8,128)(2,1)S(1)}) custom-call(s32[5]{0:T(128)S(1)} %get-tuple-element.53.meta_ref, bf16[256,512]{1,0:T(8,128)(2,1)S(1)} %copy-done.31, bf16[4,2,256,128]{3,2,1,0:T(8,128)(2,1)S(1)} %all-to-all-done.1.do_ref, f32[256,512]{1,0:T(8,128)} %get-tuple-element.59.o_ref, ...), custom_call_target="tpu_custom_call" | custom-call | flops 10737418240 | bytes 4194304 | tf_op jit(solution)/shard_map/cond/branch_1_fun/pallas_call | solution.py:360
  223.1 4.7 %branch_1_fun.5 = (bf16[256,512]{1,0:T(8,128)(2,1)S(1)}, bf16[8,256,512]{2,1,0:T(8,128)(2,1)S(1)}) custom-call(s32[5]{0:T(128)S(1)} %get-tuple-element.53.meta_ref, bf16[256,512]{1,0:T(8,128)(2,1)S(1)} %copy-done.33, bf16[4,2,256,128]{3,2,1,0:T(8,128)(2,1)S(1)} %all-to-all-done.1.do_ref, f32[256,512]{1,0:T(8,128)S(1)} %copy-done.34, ...), custom_call_target="tpu_custom_call" | custom-call | flops 10737418240 | bytes 4194304 | tf_op jit(solution)/shard_map/cond/branch_1_fun/pallas_call | solution.py:360
  227.9 5.1 %collective-permute-start.9 = (bf16[4,256,512]{2,1,0:T(8,128)(2,1)S(1)}, bf16[4,256,512]{2,1,0:T(8,128)(2,1)S(1)}, u32[]{:S(2)}, u32[]{:S(2)}) collective-permute-start(bf16[4,256,512]{2,1,0:T(8,128)(2,1)S(1)} %slice.81), channel_id=1, source_target_pairs={{0,4},{4,0},{8,12},{12,8},{16,20},{20,16},{24,28},{28,24},{1,5},{5... | collective-permute-start | bytes 3145736 | tf_op jit(solution)/shard_map/cond/branch_1_fun/ppermute | solution.py:53
  233.3 12.3 %collective-permute-start.7 = (bf16[2,256,512]{2,1,0:T(8,128)(2,1)S(1)}, bf16[2,256,512]{2,1,0:T(8,128)(2,1)}, u32[]{:S(2)}, u32[]{:S(2)}) collective-permute-start(bf16[2,256,512]{2,1,0:T(8,128)(2,1)S(1)} %slice.123), channel_id=1, source_target_pairs={{0,8},{4,12},{8,0},{12,4},{16,24},{20,28},{24,16},{28,20},{1,9},{5... | collective-permute-start | bytes 1572872 | tf_op jit(solution)/shard_map/cond/branch_1_fun/ppermute | solution.py:53
  246.7 27.7 %collective-permute-start.10 = (bf16[2,256,512]{2,1,0:T(8,128)(2,1)}, bf16[2,256,512]{2,1,0:T(8,128)(2,1)}, u32[]{:S(2)}, u32[]{:S(2)}) collective-permute-start(bf16[2,256,512]{2,1,0:T(8,128)(2,1)} %slice.127), channel_id=1, source_target_pairs={{0,16},{4,20},{8,24},{12,28},{16,0},{20,4},{24,8},{28,12},{1,17},{... | collective-permute-start | bytes 1572872 | tf_op jit(solution)/shard_map/cond/branch_1_fun/ppermute | solution.py:53
  274.4 3.7 reduce_sum.56
  278.1 4.4 all-to-all-start.2
  290.7 4.9 %collective-permute-done.8 = bf16[1,256,512]{2,1,0:T(8,128)(2,1)S(1)} collective-permute-done((bf16[1,256,512]{2,1,0:T(8,128)(2,1)S(1)}, bf16[1,256,512]{2,1,0:T(8,128)(2,1)S(1)}, u32[]{:S(2)}, u32[]{:S(2)}) %collective-permute-start.8) | collective-permute-done | bytes 262176 | tf_op jit(solution)/shard_map/cond/branch_1_fun/ppermute | solution.py:53
  297.0 10.0 %all-to-all-done.2 = bf16[4,96,1024]{2,1,0:T(8,128)(2,1)} async-done(((bf16[4,96,1024]{2,1,0:T(8,128)(2,1)}), bf16[4,96,1024]{2,1,0:T(8,128)(2,1)}, u32[]{:S(2)}, u32[]{:S(2)}) %all-to-all-start.2) | async-done | bytes 786464 | tf_op jit(solution)/shard_map/cond/branch_1_fun/all_to_all | solution.py:777
  313.6 3.5 all-to-all-start.3
  332.3 10.8 %all-to-all-done.3 = bf16[4,96,1024]{2,1,0:T(8,128)(2,1)S(1)} async-done(((bf16[4,96,1024]{2,1,0:T(8,128)(2,1)}), bf16[4,96,1024]{2,1,0:T(8,128)(2,1)S(1)}, u32[]{:S(2)}, u32[]{:S(2)}) %all-to-all-start.3) | async-done | bytes 786464 | tf_op jit(solution)/shard_map/cond/branch_1_fun/all_to_all | solution.py:777
  345.2 4.7 %all-to-all-start.4 = ((bf16[4,384,1024]{2,1,0:T(8,128)(2,1)}), bf16[4,384,1024]{2,1,0:T(8,128)(2,1)}, u32[]{:S(2)}, u32[]{:S(2)}) async-start(bf16[4,384,1024]{2,1,0:T(8,128)(2,1)} %broadcast_in_dim.1), calls=%async_computation.4 | async-start | bytes 6291456 | tf_op jit(solution)/shard_map/cond/branch_1_fun/all_to_all | solution.py:822
  354.5 15.5 %collective-permute-done.18.refs_1_ = bf16[2,256,256]{2,1,0:T(8,128)(2,1)S(1)} collective-permute-done((bf16[2,256,256]{2,1,0:T(8,128)(2,1)S(1)}, bf16[2,256,256]{2,1,0:T(8,128)(2,1)S(1)}, u32[]{:S(2)}, u32[]{:S(2)}) %collective-permute-start.18) | collective-permute-done | bytes 262176 | tf_op jit(solution)/shard_map/cond/branch_1_fun/ppermute | solution.py:53
  370.1 3.5 collective-permute-done.19.refs_2_
  373.6 12.8 %collective-permute-done.20.refs_3_ = bf16[2,256,256]{2,1,0:T(8,128)(2,1)S(1)} collective-permute-done((bf16[2,256,256]{2,1,0:T(8,128)(2,1)S(1)}, bf16[2,256,256]{2,1,0:T(8,128)(2,1)S(1)}, u32[]{:S(2)}, u32[]{:S(2)}) %collective-permute-start.20) | collective-permute-done | bytes 262176 | tf_op jit(solution)/shard_map/cond/branch_1_fun/ppermute | solution.py:53
  386.4 4.6 %branch_1_fun.7 = bf16[256,1024]{1,0:T(8,128)(2,1)} custom-call(s32[2]{0:T(128)S(1)} %pad_add_fusion.place_ref, bf16[2,256,256]{2,1,0:T(8,128)(2,1)S(1)} %get-tuple-element.205.refs_0_, bf16[2,256,256]{2,1,0:T(8,128)(2,1)S(1)} %collective-permute-done.18.refs_1_, bf16[2,256,256]{2,1,0:T(8,128)(2,1)S(1)} %collective-permute-done.19.refs_2_, ...), custom_call_target="tpu_custom_call" | custom-call | flops 1073741824 | bytes 4194304 | tf_op jit(solution)/shard_map/cond/branch_1_fun/pallas_call | solution.py:648
  391.0 6.8 %all-to-all-done.4 = bf16[4,384,1024]{2,1,0:T(8,128)(2,1)} async-done(((bf16[4,384,1024]{2,1,0:T(8,128)(2,1)}), bf16[4,384,1024]{2,1,0:T(8,128)(2,1)}, u32[]{:S(2)}, u32[]{:S(2)}) %all-to-all-start.4) | async-done | bytes 3145760 | tf_op jit(solution)/shard_map/cond/branch_1_fun/all_to_all | solution.py:822
  414.4 9.3 %shard_map.234 = (f32[4,1024,512]{2,1,0:T(8,128)}, f32[4,1024,512]{2,1,0:T(8,128)}) custom-call(bf16[4,1024,512]{2,1,0:T(8,128)(2,1)} %get-tuple-element.198.gate_ref, bf16[4,1024,512]{2,1,0:T(8,128)(2,1)} %get-tuple-element.199.up_ref), custom_call_target="tpu_custom_call" | custom-call | bytes 25165824 | tf_op jit(solution)/shard_map/pallas_call | solution.py:668
  435.0 6.4 %shard_map.235 = f32[4,512,1024]{2,1,0:T(8,128)} custom-call(s32[1]{0:T(128)} %bitcast.16.core_ref, bf16[1536,1024]{1,0:T(8,128)(2,1)} %get-tuple-element.159.own_ref, bf16[1536,1024]{1,0:T(8,128)(2,1)} %collective-permute-done.37.other_ref), custom_call_target="tpu_custom_call" | custom-call | bytes 12582912 | tf_op jit(solution)/shard_map/pallas_call | solution.py:694
  (237 shorter events, 122.8 us)
Async XLA Ops:
  7.2 52.2 %all-gather.6.cloned.1.call-start = ((), (), s32[]{:S(2)}) async-start(), calls=%async_computation.6 | async-start | bytes 2621440 | tf_op jit(solution)/shard_map/all_gather | solution.py:762
  10.7 81.5 %all-gather.8.cloned.1.call-start = ((), (), s32[]{:S(2)}) async-start(), calls=%async_computation.7 | async-start | bytes 1310720 | tf_op jit(solution)/shard_map/all_gather | solution.py:771
  11.5 135.5 %all-gather.10.cloned.1.call-start = ((), (), s32[]{:S(2)}) async-start(), calls=%async_computation.8 | async-start | bytes 2621440 | tf_op jit(solution)/shard_map/all_gather | solution.py:773
  65.6 8.2 %collective-permute-start.21 = (bf16[1,256,512]{2,1,0:T(8,128)(2,1)}, bf16[1,256,512]{2,1,0:T(8,128)(2,1)S(1)}, u32[]{:S(2)}, u32[]{:S(2)}) collective-permute-start(bf16[1,256,512]{2,1,0:T(8,128)(2,1)} %bitcast.70), channel_id=1, source_target_pairs={{0,8},{4,12},{8,0},{12,4},{16,24},{20,28},{24,16},{28,20},{1,9},{5... | collective-permute-start | bytes 786440 | tf_op jit(solution)/shard_map/ppermute | solution.py:53
  67.1 10.0 %collective-permute-start.24 = (bf16[1,256,512]{2,1,0:T(8,128)(2,1)S(1)}, bf16[1,256,512]{2,1,0:T(8,128)(2,1)S(1)}, u32[]{:S(2)}, u32[]{:S(2)}) collective-permute-start(bf16[1,256,512]{2,1,0:T(8,128)(2,1)S(1)} %bitcast.66), channel_id=1, source_target_pairs={{0,16},{4,20},{8,24},{12,28},{16,0},{20,4},{24,8},{28,12},{1,17},{... | collective-permute-start | bytes 786440 | tf_op jit(solution)/shard_map/ppermute | solution.py:53
  75.7 13.0 %collective-permute-start.22 = (bf16[2,256,512]{2,1,0:T(8,128)(2,1)}, bf16[2,256,512]{2,1,0:T(8,128)(2,1)S(1)}, u32[]{:S(2)}, u32[]{:S(2)}) collective-permute-start(bf16[2,256,512]{2,1,0:T(8,128)(2,1)} %pad_maximum_fusion.6), channel_id=1, source_target_pairs={{0,16},{4,20},{8,24},{12,28},{16,0},{20,4},{24,8},{28,12},{1,17},{... | collective-permute-start | bytes 1572872 | tf_op jit(solution)/shard_map/ppermute | solution.py:53
  78.0 12.8 %collective-permute-start.25 = (bf16[2,256,512]{2,1,0:T(8,128)(2,1)}, bf16[2,256,512]{2,1,0:T(8,128)(2,1)S(1)}, u32[]{:S(2)}, u32[]{:S(2)}) collective-permute-start(bf16[2,256,512]{2,1,0:T(8,128)(2,1)} %pad_maximum_fusion.7), channel_id=1, source_target_pairs={{0,8},{4,12},{8,0},{12,4},{16,24},{20,28},{24,16},{28,20},{1,9},{5... | collective-permute-start | bytes 1572872 | tf_op jit(solution)/shard_map/ppermute | solution.py:53
  92.1 54.8 %collective-permute-start.27 = (bf16[4,128,1024]{2,1,0:T(8,128)(2,1)}, bf16[4,128,1024]{2,1,0:T(8,128)(2,1)}, u32[]{:S(2)}, u32[]{:S(2)}) collective-permute-start(bf16[4,128,1024]{2,1,0:T(8,128)(2,1)} %bitcast.84), channel_id=1, source_target_pairs={{0,4},{4,0},{8,12},{12,8},{16,20},{20,16},{24,28},{28,24},{1,5},{5... | collective-permute-start | bytes 3145736 | tf_op jit(solution)/shard_map/ppermute | solution.py:53
  104.8 42.1 %all-to-all-start.5 = ((bf16[4,2,256,128]{3,2,1,0:T(8,128)(2,1)}), bf16[4,2,256,128]{3,2,1,0:T(8,128)(2,1)S(1)}, u32[]{:S(2)}, u32[]{:S(2)}) async-start(bf16[4,2,256,128]{3,2,1,0:T(8,128)(2,1)} %pad_maximum_fusion.8), calls=%async_computation.5 | async-start | bytes 1048576 | tf_op jit(solution)/shard_map/all_to_all | solution.py:777
  108.3 306.1 %all-reduce.3.cloned.1.call-start = ((), (), s32[]{:S(2)}) async-start(), calls=%async_computation.9 | async-start | bytes 16777216 | tf_op jit(solution)/shard_map/psum | solution.py:816
  147.0 25.8 %collective-permute-start.28 = (bf16[4,256,1024]{2,1,0:T(8,128)(2,1)}, bf16[4,256,1024]{2,1,0:T(8,128)(2,1)S(1)}, u32[]{:S(2)}, u32[]{:S(2)}) collective-permute-start(bf16[4,256,1024]{2,1,0:T(8,128)(2,1)} %bitcast.74), channel_id=1, source_target_pairs={{0,4},{4,0},{8,12},{12,8},{16,20},{20,16},{24,28},{28,24},{1,5},{5... | collective-permute-start | bytes 6291464 | tf_op jit(solution)/shard_map/ppermute | solution.py:53
  172.8 30.7 %collective-permute-start = (bf16[3,512,1024]{2,1,0:T(8,128)(2,1)}, bf16[3,512,1024]{2,1,0:T(8,128)(2,1)}, u32[]{:S(2)}, u32[]{:S(2)}) collective-permute-start(bf16[3,512,1024]{2,1,0:T(8,128)(2,1)} %get-tuple-element.52), channel_id=1, source_target_pairs={{0,4},{4,0},{8,12},{12,8},{16,20},{20,16},{24,28},{28,24},{1,5},{5... | collective-permute-start | bytes 9437192 | tf_op jit(solution)/shard_map/cond/branch_1_fun/ppermute | solution.py:53
  174.3 35.5 %all-to-all-start.1 = ((bf16[4,2,256,128]{3,2,1,0:T(8,128)(2,1)}), bf16[4,2,256,128]{3,2,1,0:T(8,128)(2,1)S(1)}, u32[]{:S(2)}, u32[]{:S(2)}) async-start(bf16[4,2,256,128]{3,2,1,0:T(8,128)(2,1)} %get-tuple-element.55), calls=%async_computation.1 | async-start | bytes 1048576 | tf_op jit(solution)/shard_map/cond/branch_1_fun/all_to_all | solution.py:777
  186.8 9.4 %collective-permute-start.4 = (f32[1028]{0:T(1024)S(1)}, f32[1028]{0:T(1024)S(1)}, u32[]{:S(2)}, u32[]{:S(2)}) collective-permute-start(f32[1028]{0:T(1024)S(1)} %add.97), channel_id=1, source_target_pairs={{0,1},{1,0},{2,3},{3,2},{4,5},{5,4},{6,7},{7,6},{8,9},{9,8},{10,11... | collective-permute-start | bytes 12344 | tf_op jit(solution)/shard_map/cond/branch_1_fun/ppermute | solution.py:53
  196.2 6.8 %collective-permute-start.5 = (f32[1028]{0:T(1024)S(1)}, f32[1028]{0:T(1024)S(1)}, u32[]{:S(2)}, u32[]{:S(2)}) collective-permute-start(f32[1028]{0:T(1024)S(1)} %add.98), channel_id=1, source_target_pairs={{0,2},{1,3},{2,0},{3,1},{4,6},{5,7},{6,4},{7,5},{8,10},{9,11},{10,... | collective-permute-start | bytes 12344 | tf_op jit(solution)/shard_map/cond/branch_1_fun/ppermute | solution.py:53
  209.9 64.5 %all-to-all-start = ((bf16[4,384,1024]{2,1,0:T(8,128)(2,1)}), bf16[4,384,1024]{2,1,0:T(8,128)(2,1)}, u32[]{:S(2)}, u32[]{:S(2)}) async-start(bf16[4,384,1024]{2,1,0:T(8,128)(2,1)} %bitcast.56), calls=%async_computation | async-start | bytes 6291456 | tf_op jit(solution)/shard_map/cond/branch_1_fun/all_to_all | solution.py:822
  220.5 12.5 %collective-permute-start.6 = (bf16[4,256,512]{2,1,0:T(8,128)(2,1)S(1)}, bf16[4,256,512]{2,1,0:T(8,128)(2,1)S(1)}, u32[]{:S(2)}, u32[]{:S(2)}) collective-permute-start(bf16[4,256,512]{2,1,0:T(8,128)(2,1)S(1)} %slice.23), channel_id=1, source_target_pairs={{0,4},{4,0},{8,12},{12,8},{16,20},{20,16},{24,28},{28,24},{1,5},{5... | collective-permute-start | bytes 3145736 | tf_op jit(solution)/shard_map/cond/branch_1_fun/ppermute | solution.py:53
  227.9 17.7 %collective-permute-start.9 = (bf16[4,256,512]{2,1,0:T(8,128)(2,1)S(1)}, bf16[4,256,512]{2,1,0:T(8,128)(2,1)S(1)}, u32[]{:S(2)}, u32[]{:S(2)}) collective-permute-start(bf16[4,256,512]{2,1,0:T(8,128)(2,1)S(1)} %slice.81), channel_id=1, source_target_pairs={{0,4},{4,0},{8,12},{12,8},{16,20},{20,16},{24,28},{28,24},{1,5},{5... | collective-permute-start | bytes 3145736 | tf_op jit(solution)/shard_map/cond/branch_1_fun/ppermute | solution.py:53
  233.3 49.2 %collective-permute-start.7 = (bf16[2,256,512]{2,1,0:T(8,128)(2,1)S(1)}, bf16[2,256,512]{2,1,0:T(8,128)(2,1)}, u32[]{:S(2)}, u32[]{:S(2)}) collective-permute-start(bf16[2,256,512]{2,1,0:T(8,128)(2,1)S(1)} %slice.123), channel_id=1, source_target_pairs={{0,8},{4,12},{8,0},{12,4},{16,24},{20,28},{24,16},{28,20},{1,9},{5... | collective-permute-start | bytes 1572872 | tf_op jit(solution)/shard_map/cond/branch_1_fun/ppermute | solution.py:53
  246.7 40.0 %collective-permute-start.10 = (bf16[2,256,512]{2,1,0:T(8,128)(2,1)}, bf16[2,256,512]{2,1,0:T(8,128)(2,1)}, u32[]{:S(2)}, u32[]{:S(2)}) collective-permute-start(bf16[2,256,512]{2,1,0:T(8,128)(2,1)} %slice.127), channel_id=1, source_target_pairs={{0,16},{4,20},{8,24},{12,28},{16,0},{20,4},{24,8},{28,12},{1,17},{... | collective-permute-start | bytes 1572872 | tf_op jit(solution)/shard_map/cond/branch_1_fun/ppermute | solution.py:53
  278.1 29.0 %all-to-all-start.2 = ((bf16[4,96,1024]{2,1,0:T(8,128)(2,1)}), bf16[4,96,1024]{2,1,0:T(8,128)(2,1)}, u32[]{:S(2)}, u32[]{:S(2)}) async-start(bf16[4,96,1024]{2,1,0:T(8,128)(2,1)} %bitcast.2), calls=%async_computation.2 | async-start | bytes 1572864 | tf_op jit(solution)/shard_map/cond/branch_1_fun/all_to_all | solution.py:777
  283.7 11.8 %collective-permute-start.8 = (bf16[1,256,512]{2,1,0:T(8,128)(2,1)S(1)}, bf16[1,256,512]{2,1,0:T(8,128)(2,1)S(1)}, u32[]{:S(2)}, u32[]{:S(2)}) collective-permute-start(bf16[1,256,512]{2,1,0:T(8,128)(2,1)S(1)} %slice.125), channel_id=1, source_target_pairs={{0,16},{4,20},{8,24},{12,28},{16,0},{20,4},{24,8},{28,12},{1,17},{... | collective-permute-start | bytes 786440 | tf_op jit(solution)/shard_map/cond/branch_1_fun/ppermute | solution.py:53
  288.0 9.0 %collective-permute-start.11 = (bf16[1,256,512]{2,1,0:T(8,128)(2,1)S(1)}, bf16[1,256,512]{2,1,0:T(8,128)(2,1)S(1)}, u32[]{:S(2)}, u32[]{:S(2)}) collective-permute-start(bf16[1,256,512]{2,1,0:T(8,128)(2,1)S(1)} %slice.129), channel_id=1, source_target_pairs={{0,8},{4,12},{8,0},{12,4},{16,24},{20,28},{24,16},{28,20},{1,9},{5... | collective-permute-start | bytes 786440 | tf_op jit(solution)/shard_map/cond/branch_1_fun/ppermute | solution.py:53
  313.6 29.5 %all-to-all-start.3 = ((bf16[4,96,1024]{2,1,0:T(8,128)(2,1)}), bf16[4,96,1024]{2,1,0:T(8,128)(2,1)S(1)}, u32[]{:S(2)}, u32[]{:S(2)}) async-start(bf16[4,96,1024]{2,1,0:T(8,128)(2,1)} %broadcast_in_dim.0), calls=%async_computation.3 | async-start | bytes 1572864 | tf_op jit(solution)/shard_map/cond/branch_1_fun/all_to_all | solution.py:777
  319.6 7.7 %collective-permute-start.16 = (bf16[64,1024]{1,0:T(8,128)(2,1)S(1)}, bf16[64,1024]{1,0:T(8,128)(2,1)S(1)}, u32[]{:S(2)}, u32[]{:S(2)}) collective-permute-start(bf16[64,1024]{1,0:T(8,128)(2,1)S(1)} %broadcast_select_fusion.2), channel_id=1, source_target_pairs={{0,8},{4,12},{8,0},{12,4},{16,24},{20,28},{24,16},{28,20},{1,9},{5... | collective-permute-start | bytes 393224 | tf_op jit(solution)/shard_map/cond/branch_1_fun/ppermute | solution.py:53
  345.2 52.6 %all-to-all-start.4 = ((bf16[4,384,1024]{2,1,0:T(8,128)(2,1)}), bf16[4,384,1024]{2,1,0:T(8,128)(2,1)}, u32[]{:S(2)}, u32[]{:S(2)}) async-start(bf16[4,384,1024]{2,1,0:T(8,128)(2,1)} %broadcast_in_dim.1), calls=%async_computation.4 | async-start | bytes 6291456 | tf_op jit(solution)/shard_map/cond/branch_1_fun/all_to_all | solution.py:822
  350.0 20.1 %collective-permute-start.18 = (bf16[2,256,256]{2,1,0:T(8,128)(2,1)S(1)}, bf16[2,256,256]{2,1,0:T(8,128)(2,1)S(1)}, u32[]{:S(2)}, u32[]{:S(2)}) collective-permute-start(bf16[2,256,256]{2,1,0:T(8,128)(2,1)S(1)} %get-tuple-element.204), channel_id=1, source_target_pairs={{0,1},{1,0},{2,3},{3,2},{4,5},{5,4},{6,7},{7,6},{8,9},{9,8},{10,11... | collective-permute-start | bytes 786440 | tf_op jit(solution)/shard_map/cond/branch_1_fun/ppermute | solution.py:53
  350.1 23.5 %collective-permute-start.19 = (bf16[2,256,256]{2,1,0:T(8,128)(2,1)S(1)}, bf16[2,256,256]{2,1,0:T(8,128)(2,1)S(1)}, u32[]{:S(2)}, u32[]{:S(2)}) collective-permute-start(bf16[2,256,256]{2,1,0:T(8,128)(2,1)S(1)} %get-tuple-element.203), channel_id=1, source_target_pairs={{0,2},{1,3},{2,0},{3,1},{4,6},{5,7},{6,4},{7,5},{8,10},{9,11},{10,... | collective-permute-start | bytes 786440 | tf_op jit(solution)/shard_map/cond/branch_1_fun/ppermute | solution.py:53
  352.0 34.4 %collective-permute-start.20 = (bf16[2,256,256]{2,1,0:T(8,128)(2,1)S(1)}, bf16[2,256,256]{2,1,0:T(8,128)(2,1)S(1)}, u32[]{:S(2)}, u32[]{:S(2)}) collective-permute-start(bf16[2,256,256]{2,1,0:T(8,128)(2,1)S(1)} %get-tuple-element.202), channel_id=1, source_target_pairs={{0,3},{1,2},{2,1},{3,0},{4,7},{5,6},{6,5},{7,4},{8,11},{9,10},{10,... | collective-permute-start | bytes 786440 | tf_op jit(solution)/shard_map/cond/branch_1_fun/ppermute | solution.py:53
  398.0 34.6 %collective-permute-start.37 = (bf16[1536,1024]{1,0:T(8,128)(2,1)}, bf16[1536,1024]{1,0:T(8,128)(2,1)}, u32[]{:S(2)}, u32[]{:S(2)}) collective-permute-start(bf16[1536,1024]{1,0:T(8,128)(2,1)} %get-tuple-element.159.own_ref), channel_id=1, source_target_pairs={{0,4},{4,0},{8,12},{12,8},{16,20},{20,16},{24,28},{28,24},{1,5},{5... | collective-permute-start | bytes 9437192 | tf_op jit(solution)/shard_map/ppermute | solution.py:53
  424.0 6.2 %collective-permute-start.35 = (f32[1024]{0:T(1024)S(1)}, f32[1024]{0:T(1024)S(1)}, u32[]{:S(2)}, u32[]{:S(2)}) collective-permute-start(f32[1024]{0:T(1024)S(1)} %multiply_reduce_fusion), channel_id=1, source_target_pairs={{0,1},{1,0},{2,3},{3,2},{4,5},{5,4},{6,7},{7,6},{8,9},{9,8},{10,11... | collective-permute-start | bytes 12296 | tf_op jit(solution)/shard_map/ppermute | solution.py:53
  430.2 11.2 %collective-permute-start.36 = (f32[1024]{0:T(1024)S(1)}, f32[1024]{0:T(1024)S(1)}, u32[]{:S(2)}, u32[]{:S(2)}) collective-permute-start(f32[1024]{0:T(1024)S(1)} %add.133), channel_id=1, source_target_pairs={{0,2},{1,3},{2,0},{3,1},{4,6},{5,7},{6,4},{7,5},{8,10},{9,11},{10,... | collective-permute-start | bytes 12296 | tf_op jit(solution)/shard_map/ppermute | solution.py:53
  (51 other events, 538.7 us)
Sparse Core Ops, SparseCore 0:
  10.8 48.6 all-gather.5
  61.6 26.6 all-gather.7
  90.4 56.4 all-gather.9
  171.7 237.6 all-reduce.2
